TPU v7x, 32 devices: a whole 2x2x4 slice. The times are simulated.
32 devices in a mesh: slab: 4 (over x, core), brick: 8 (over z, y).
Axes of the slice: x: 2, y: 2, z: 4, core: 2. Of those that a mesh axis runs over, the one named last changes fastest.
Arguments:
- volume: bfloat16 [16, 8, 128, 256], P(None, 'slab', 'brick'), may hold values from -6 to 6
- kernel_one: bfloat16 [32, 16, 3, 3, 3], replicated, may hold values from -0.3125 to 0.3125
- kernel_two: bfloat16 [96, 32, 2, 2, 2], replicated, may hold values from -0.375 to 0.375
- upstream: bfloat16 [96, 4, 8192], P('brick', 'slab'), may hold values from -0.023925781 to 0.023925781
Outputs:
- output: bfloat16 [96, 4, 8192], P('brick', 'slab')
- grad_one: float32 [32, 16, 3, 3, 3], replicated
- grad_two: float32 [96, 32, 2, 2, 2], replicated
All inputs are finite; a program needn't handle non-finite values.
Results may differ from a plain program's by a relative error of at most 0.0051.
Values may be sent and summed in bfloat16 or wider, within the bound.
No kernel may reach another device: no remote copies, remote signals or barrier semaphores. Data moves between devices by JAX's collectives and lax.ppermute only.
A program may use at most 64 MiB of HBM per device.

v0:
```python
import functools

import jax
import jax.numpy as jnp
from jax import lax
from jax.experimental import pallas as pl
from jax.experimental.pallas import tpu as pltpu
from jax.sharding import PartitionSpec as P

bf16 = jnp.bfloat16
f32 = jnp.float32
ALL = ("slab", "brick")
LIMIT = 40 * 1024 * 1024
GRAD_BLOCKS = 9 + 16


def call(body, outs, *args, scratch=()):
    return pl.pallas_call(
        body,
        out_shape=outs,
        in_specs=[pl.BlockSpec(memory_space=pltpu.VMEM)] * len(args),
        out_specs=jax.tree.map(lambda _: pl.BlockSpec(memory_space=pltpu.VMEM), outs),
        scratch_shapes=list(scratch),
        compiler_params=pltpu.CompilerParams(vmem_limit_bytes=LIMIT),
    )(*args)


def one_hot(shape, source_of_row):
    rows = lax.broadcasted_iota(jnp.int32, shape, 0)
    cols = lax.broadcasted_iota(jnp.int32, shape, 1)
    return jnp.where(cols == source_of_row(rows), 1.0, 0.0).astype(bf16)


def dot(a, b):
    return jnp.dot(a, b, preferred_element_type=f32)


def dot_nt(a, b):
    return lax.dot_general(a, b, (((1,), (1,)), ((), ())), preferred_element_type=f32)


def planes(v_ref, low_ref, high_ref):
    channels, _, rows, cols = v_ref.shape
    parts = [low_ref[...], v_ref[:, 0], v_ref[:, 1], high_ref[...]]
    parts = [p.reshape(channels * rows, cols) for p in parts]
    return jnp.concatenate(parts, axis=1)


def pack_edges(v_ref, low_ref, high_ref, first_ref, last_ref):
    channels, _, rows, _ = v_ref.shape
    stacked = planes(v_ref, low_ref, high_ref)
    pick = one_hot(
        (2 * channels, channels * rows),
        lambda r: (r % channels) * rows + (r // channels) * (rows - 1),
    )
    both = dot(pick, stacked).astype(bf16)
    first_ref[...] = both[:channels]
    last_ref[...] = both[channels:]


def pack_cotangent(u_ref, out_ref):
    filters = u_ref.shape[0]
    bricks, padded, cells = out_ref.shape
    for b in range(bricks):
        out_ref[b, :filters, :] = u_ref[:, b * cells : (b + 1) * cells]
        if padded > filters:
            out_ref[b, filters:, :] = jnp.zeros((padded - filters, cells), bf16)


def main_kernel(
    own_filters,
    v_ref,
    low_ref,
    high_ref,
    before_ref,
    after_ref,
    g_ref,
    w1_ref,
    w2p_ref,
    w2t_ref,
    out_ref,
    grad_ref,
    d_ref,
    x_ref,
):
    channels, _, rows, cols = v_ref.shape
    half = cols // 2
    bricks, padded, cells = g_ref.shape
    filters = w2t_ref.shape[1]
    swap = one_hot(
        (channels * rows, channels * rows), lambda r: (r % channels) * rows + r // channels
    )
    turned = dot(swap, planes(v_ref, low_ref, high_ref)).astype(bf16)
    at = lax.broadcasted_iota(jnp.int32, (cols, 4 * half), 0)
    lane = lax.broadcasted_iota(jnp.int32, (cols, 4 * half), 1)
    spread = jnp.where(at == 2 * (lane % half) + lane // half - 1, 1.0, 0.0).astype(bf16)
    for a in range(4):
        lanes = slice(a * cols, (a + 1) * cols)
        inner = dot(turned[:, lanes], spread).astype(bf16)
        edge = jnp.concatenate([before_ref[:, lanes], after_ref[:, lanes]], axis=0)
        edge = dot(edge, spread).astype(bf16)
        for e in range(4):
            piece = slice(e * half, (e + 1) * half)
            d_ref[1 : rows + 1, a, e] = inner[:, piece].reshape(rows, channels, half)
            d_ref[0, a, e] = edge[:channels, piece]
            d_ref[rows + 1, a, e] = edge[channels:, piece]
    for j in range(rows // 2):
        window = d_ref[2 * j : 2 * j + 4].reshape(64 * channels, half)
        x_ref[:, j * half : (j + 1) * half] = window
    compact = one_hot(
        (filters, bricks * padded), lambda r: (r // own_filters) * padded + r % own_filters
    )
    gradient = dot(compact, g_ref[...].reshape(bricks * padded, cells)).astype(bf16)

    pre = dot(w1_ref[...], x_ref[...])
    sigma = jax.nn.sigmoid(pre)
    hidden = (pre * sigma).astype(bf16)
    result = dot(w2p_ref[...], hidden).astype(bf16)
    for b in range(bricks):
        out_ref[b] = result[b * padded : b * padded + own_filters]
    back = dot(w2t_ref[...], gradient)
    delta = (back * sigma * (1.0 + pre * (1.0 - sigma))).astype(bf16)
    mid = hidden.shape[0] // 8
    natural = one_hot(
        (8 * mid, 8 * mid),
        lambda s: (s % 2) * (4 * mid) + ((s // 2) % 4) * mid + s // 8,
    )
    ordered = dot(natural, hidden).astype(bf16)
    grad_two = dot_nt(ordered, gradient)
    moments = dot_nt(x_ref[...], delta).reshape(4, 4, 4, channels, 8 * mid)
    by_r = moments[:, :, 0:3, :, : 4 * mid] + moments[:, :, 1:4, :, 4 * mid :]
    group = lax.broadcasted_iota(jnp.int32, (9 * channels, 4 * mid), 1) // mid
    total = jnp.zeros((9 * channels, 4 * mid), f32)
    for shift in range(-3, 3):
        moved = jnp.zeros((9 * channels, 4 * mid), f32)
        for a in range(3):
            source = a - shift
            if 0 <= source < 4:
                p, q = source // 2, source % 2
                piece = by_r[q : q + 3, a + p].reshape(9 * channels, 4 * mid)
                moved = jnp.where(group == source, piece, moved)
        amount = (shift * mid) % (4 * mid)
        total = total + (pltpu.roll(moved, amount, 1) if amount else moved)
    kind = grad_ref.dtype
    grad_ref[...] = jnp.zeros_like(grad_ref)
    grad_ref[0:9] = total.astype(kind).reshape(9, channels, 4 * mid)
    grad_ref[9:25, :, :filters] = grad_two.astype(kind).reshape(16, -1, filters)


def shifts(count):
    up = [(i, i + 1) for i in range(count - 1)]
    return up, [(j, i) for i, j in up]


def place_kernel(kernel_one):
    base = jnp.transpose(kernel_one, (0, 3, 2, 4, 1))
    out = base.shape[0]
    pieces = []
    for r in (0, 1):
        for p in (0, 1):
            for q in (0, 1):
                pads = ((0, 0), (q, 1 - q), (p, 1 - p), (r, 1 - r), (0, 0))
                pieces.append(jnp.pad(base, pads).reshape(out, -1))
    return jnp.concatenate(pieces, axis=0)


def per_device(volume, kernel_one, kernel_two, upstream):
    channels, _, rows, cols = volume.shape
    bricks, slabs = lax.axis_size("brick"), lax.axis_size("slab")
    devices = bricks * slabs
    filters, mid = kernel_two.shape[:2]
    own_filters = filters // bricks
    padded = -(-own_filters // 16) * 16
    cells = (rows // 2) * (cols // 2)

    up, down = shifts(slabs)
    low = lax.ppermute(volume[:, 1], "slab", up)
    high = lax.ppermute(volume[:, 0], "slab", down)

    cotangent = call(
        pack_cotangent,
        jax.ShapeDtypeStruct((bricks, padded, cells), bf16),
        upstream.reshape(own_filters, -1),
    )
    cotangent = lax.all_to_all(cotangent, "brick", 0, 0, tiled=True)

    edge = jax.ShapeDtypeStruct((channels, 4 * cols), bf16)
    first, last = call(pack_edges, (edge, edge), volume, low, high)
    up, down = shifts(bricks)
    before = lax.ppermute(last, "brick", up)
    after = lax.ppermute(first, "brick", down)

    weights_one = place_kernel(kernel_one)
    weights_two = jnp.transpose(kernel_two, (0, 4, 2, 3, 1)).reshape(filters, 8 * mid)
    grouped = weights_two.reshape(bricks, own_filters, 8 * mid)
    grouped = jnp.pad(grouped, ((0, 0), (0, padded - own_filters), (0, 0)))
    grouped = grouped.reshape(bricks * padded, 8 * mid)

    share = -(-GRAD_BLOCKS // devices)
    out, grads = call(
        functools.partial(main_kernel, own_filters),
        (
            jax.ShapeDtypeStruct((bricks, own_filters, cells), bf16),
            jax.ShapeDtypeStruct((devices * share, 16, 128), bf16),
        ),
        volume,
        low,
        high,
        before,
        after,
        cotangent,
        weights_one,
        grouped,
        weights_two.T,
        scratch=(
            pltpu.VMEM((rows + 2, 4, 4, channels, cols // 2), bf16),
            pltpu.VMEM((64 * channels, cells), bf16),
        ),
    )
    parts = lax.all_to_all(grads, ALL, 0, 0, tiled=True)
    parts = parts.reshape(devices, share, 16, 128).astype(f32).sum(0).astype(bf16)
    whole = jnp.broadcast_to(parts[None], (devices,) + parts.shape)
    whole = lax.all_to_all(whole, ALL, 0, 0, tiled=True).reshape(-1, 16, 128).astype(f32)

    out = lax.all_to_all(out, "brick", 0, 0, tiled=True)
    output = jnp.transpose(out, (1, 0, 2)).reshape(own_filters, 1, -1)

    one = whole[0:9, :, : 3 * mid].reshape(3, 3, channels, 3, mid)
    grad_one = jnp.transpose(one, (4, 2, 3, 0, 1))
    two = whole[9:25].reshape(8 * mid, 128)[:, :filters]
    grad_two = jnp.transpose(two.reshape(mid, 2, 2, 2, filters), (4, 0, 1, 2, 3))
    return output, grad_one, grad_two


def solution(mesh):
    in_specs = (P(None, "slab", "brick", None), P(), P(), P("brick", "slab", None))
    out_specs = (P("brick", "slab", None), P(), P())
    return jax.shard_map(
        per_device, mesh=mesh, in_specs=in_specs, out_specs=out_specs, check_vma=False
    )
```

profile of v0, /device:TPU:0, one launch (start us, length us, event | category | flops | bytes accessed | tf_op | source)
XLA Modules:
  0.0 69.3 jit_solution(4824472708292579695)
XLA Ops:
  0.7 1.0 %slice_bitcast_fusion = (bf16[16,16,256]{2,1,0:T(8,128)(2,1)S(1)}, bf16[16,16,256]{2,1,0:T(8,128)(2,1)S(1)}) fusion(bf16[16,2,16,256]{3,2,1,0:T(8,128)(2,1)} %v_ref.3), kind=kLoop, calls=%fused_computation | loop fusion | bytes 524288 | tf_op jit(solution)/shard_map/squeeze | solution.py:178
  1.7 2.4 %collective-permute-start = (bf16[16,16,256]{2,1,0:T(8,128)(2,1)S(1)}, bf16[16,16,256]{2,1,0:T(8,128)(2,1)S(1)}, u32[]{:S(2)}, u32[]{:S(2)}) collective-permute-start(bf16[16,16,256]{2,1,0:T(8,128)(2,1)S(1)} %get-tuple-element.18), channel_id=1, source_target_pairs={{0,8},{8,16},{16,24},{1,9},{9,17},{17,25},{2,10},{10,18},{18,26},{... | collective-permute-start | bytes 393224 | tf_op jit(solution)/shard_map/ppermute | solution.py:177
  4.1 1.3 %collective-permute-start.1 = (bf16[16,16,256]{2,1,0:T(8,128)(2,1)S(1)}, bf16[16,16,256]{2,1,0:T(8,128)(2,1)S(1)}, u32[]{:S(2)}, u32[]{:S(2)}) collective-permute-start(bf16[16,16,256]{2,1,0:T(8,128)(2,1)S(1)} %get-tuple-element.17), channel_id=1, source_target_pairs={{8,0},{16,8},{24,16},{9,1},{17,9},{25,17},{10,2},{18,10},{26,18},{... | collective-permute-start | bytes 393224 | tf_op jit(solution)/shard_map/ppermute | solution.py:178
  5.4 0.7 %shard_map.68 = bf16[8,16,1024]{2,1,0:T(8,128)(2,1)} custom-call(bf16[12,8192]{1,0:T(8,128)(2,1)S(1)} %bitcast.37), custom_call_target="tpu_custom_call" | custom-call | tf_op jit(solution)/shard_map/pallas_call | solution.py:18
  6.1 6.7 %all-to-all-start = ((bf16[8,16,1024]{2,1,0:T(8,128)(2,1)}), bf16[8,16,1024]{2,1,0:T(8,128)(2,1)S(1)}, u32[]{:S(2)}, u32[]{:S(2)}) async-start(bf16[8,16,1024]{2,1,0:T(8,128)(2,1)} %shard_map.68), calls=%async_computation | async-start | bytes 524288 | tf_op jit(solution)/shard_map/all_to_all | solution.py:185
  12.8 0.5 fusion
  14.4 0.8 %copy-done.1 = bf16[16,2,16,256]{3,2,1,0:T(8,128)(2,1)S(1)} copy-done((bf16[16,2,16,256]{3,2,1,0:T(8,128)(2,1)S(1)}, bf16[16,2,16,256]{3,2,1,0:T(8,128)(2,1)}, u32[]{:S(2)}) %copy-start.1) | copy-done | bytes 262168
  15.2 0.2 shard_map.67
  15.3 3.9 %collective-permute-start.2 = (bf16[16,1024]{1,0:T(8,128)(2,1)S(1)}, bf16[16,1024]{1,0:T(8,128)(2,1)S(1)}, u32[]{:S(2)}, u32[]{:S(2)}) collective-permute-start(bf16[16,1024]{1,0:T(8,128)(2,1)S(1)} %get-tuple-element.7), channel_id=1, source_target_pairs={{0,1},{1,2},{2,3},{3,4},{4,5},{5,6},{6,7},{8,9},{9,10},{10,11},{11... | collective-permute-start | bytes 98312 | tf_op jit(solution)/shard_map/ppermute | solution.py:190
  19.3 1.4 %collective-permute-start.3 = (bf16[16,1024]{1,0:T(8,128)(2,1)S(1)}, bf16[16,1024]{1,0:T(8,128)(2,1)S(1)}, u32[]{:S(2)}, u32[]{:S(2)}) collective-permute-start(bf16[16,1024]{1,0:T(8,128)(2,1)S(1)} %get-tuple-element.8), channel_id=1, source_target_pairs={{1,0},{2,1},{3,2},{4,3},{5,4},{6,5},{7,6},{9,8},{10,9},{11,10},{12... | collective-permute-start | bytes 98312 | tf_op jit(solution)/shard_map/ppermute | solution.py:191
  20.7 0.2 copy.58
  20.9 0.2 reshape_reshape.3
  21.1 4.1 %collective-permute-done.3.after_ref = bf16[16,1024]{1,0:T(8,128)(2,1)S(1)} collective-permute-done((bf16[16,1024]{1,0:T(8,128)(2,1)S(1)}, bf16[16,1024]{1,0:T(8,128)(2,1)S(1)}, u32[]{:S(2)}, u32[]{:S(2)}) %collective-permute-start.3) | collective-permute-done | bytes 32800 | tf_op jit(solution)/shard_map/ppermute | solution.py:191
  25.2 3.0 %shard_map.69 = (bf16[8,12,1024]{2,1,0:T(8,128)(2,1)}, bf16[32,16,128]{2,1,0:T(8,128)(2,1)S(1)}) custom-call(bf16[16,2,16,256]{3,2,1,0:T(8,128)(2,1)S(1)} %copy-done.1, bf16[16,16,256]{2,1,0:T(8,128)(2,1)S(1)} %collective-permute-done.low_ref, bf16[16,16,256]{2,1,0:T(8,128)(2,1)S(1)} %collective-permute-done.1.high_ref, ...), custom_call_target="tpu_custom_call" | custom-call | tf_op jit(solution)/shard_map/pallas_call | solution.py:18
  28.2 15.5 %all_to_all.20 = bf16[32,16,128]{2,1,0:T(8,128)(2,1)S(1)} all-to-all(bf16[32,16,128]{2,1,0:T(8,128)(2,1)S(1)} %get-tuple-element.10), channel_id=1, replica_groups=mesh['slab'=4,'brick'=8] {'slab','brick'}, dimensions={0} | all-to-all | bytes 262144 | tf_op jit(solution)/shard_map/all_to_all | solution.py:220
  43.8 3.4 %all-to-all-start.1 = ((bf16[8,12,1024]{2,1,0:T(8,128)(2,1)}), bf16[8,12,1024]{2,1,0:T(8,128)(2,1)S(1)}, u32[]{:S(2)}, u32[]{:S(2)}) async-start(bf16[8,12,1024]{2,1,0:T(8,128)(2,1)} %get-tuple-element.9), calls=%async_computation.1 | async-start | bytes 524288 | tf_op jit(solution)/shard_map/all_to_all | solution.py:225
  47.2 9.4 %all-to-all-done.1 = bf16[8,12,1024]{2,1,0:T(8,128)(2,1)S(1)} async-done(((bf16[8,12,1024]{2,1,0:T(8,128)(2,1)}), bf16[8,12,1024]{2,1,0:T(8,128)(2,1)S(1)}, u32[]{:S(2)}, u32[]{:S(2)}) %all-to-all-start.1) | async-done | bytes 196640 | tf_op jit(solution)/shard_map/all_to_all | solution.py:225
  56.6 0.7 broadcast_in_dim.2
  57.3 2.7 %all-to-all-start.3 = ((bf16[32,1,16,128]{3,2,1,0:T(8,128)(2,1)}), bf16[32,1,16,128]{3,2,1,0:T(8,128)(2,1)S(1)}, u32[]{:S(2)}, u32[]{:S(2)}) async-start(bf16[32,1,16,128]{3,2,1,0:T(8,128)(2,1)} %broadcast_in_dim.2), calls=%async_computation.3 | async-start | bytes 262144 | tf_op jit(solution)/shard_map/all_to_all | solution.py:223
  60.1 0.9 %reshape.72 = bf16[12,1,8192]{2,0,1:T(8,128)(2,1)} reshape(bf16[12,8,1024]{2,1,0:T(8,128)(2,1)S(1)} %copy.60) | data formatting | bytes 393216 | tf_op jit(solution)/shard_map/reshape | solution.py:226
  61.0 6.8 %all-to-all-done.3 = bf16[32,1,16,128]{3,2,1,0:T(8,128)(2,1)S(1)} async-done(((bf16[32,1,16,128]{3,2,1,0:T(8,128)(2,1)}), bf16[32,1,16,128]{3,2,1,0:T(8,128)(2,1)S(1)}, u32[]{:S(2)}, u32[]{:S(2)}) %all-to-all-start.3) | async-done | bytes 131104 | tf_op jit(solution)/shard_map/all_to_all | solution.py:223
  67.8 0.2 reshape.73
  68.0 0.7 %copy.61 = f32[32,16,3,3,3]{0,1,4,3,2:T(8,128)} copy(f32[32,16,3,3,3]{0,2,1,4,3:T(4,128)S(1)} %bitcast.38) | data formatting | bytes 110592
  68.7 0.7 slice.22
  (33 shorter events, 1.3 us)
Async XLA Ops:
  0.6 12.1 %copy-start = (bf16[32,16,3,3,3]{0,1,4,3,2:T(8,128)(2,1)S(1)}, bf16[32,16,3,3,3]{0,1,4,3,2:T(8,128)(2,1)}, u32[]{:S(2)}) copy-start(bf16[32,16,3,3,3]{0,1,4,3,2:T(8,128)(2,1)} %param.5) | copy-start | bytes 82948
  0.6 4.7 %copy-start.2 = (bf16[12,1,8192]{2,0,1:T(8,128)(2,1)S(1)}, bf16[12,1,8192]{2,0,1:T(8,128)(2,1)}, u32[]{:S(2)}) copy-start(bf16[12,1,8192]{2,0,1:T(8,128)(2,1)} %param.7) | copy-start | bytes 589828
  1.7 12.6 %collective-permute-start = (bf16[16,16,256]{2,1,0:T(8,128)(2,1)S(1)}, bf16[16,16,256]{2,1,0:T(8,128)(2,1)S(1)}, u32[]{:S(2)}, u32[]{:S(2)}) collective-permute-start(bf16[16,16,256]{2,1,0:T(8,128)(2,1)S(1)} %get-tuple-element.18), channel_id=1, source_target_pairs={{0,8},{8,16},{16,24},{1,9},{9,17},{17,25},{2,10},{10,18},{18,26},{... | collective-permute-start | bytes 393224 | tf_op jit(solution)/shard_map/ppermute | solution.py:177
  4.1 10.3 %collective-permute-start.1 = (bf16[16,16,256]{2,1,0:T(8,128)(2,1)S(1)}, bf16[16,16,256]{2,1,0:T(8,128)(2,1)S(1)}, u32[]{:S(2)}, u32[]{:S(2)}) collective-permute-start(bf16[16,16,256]{2,1,0:T(8,128)(2,1)S(1)} %get-tuple-element.17), channel_id=1, source_target_pairs={{8,0},{16,8},{24,16},{9,1},{17,9},{25,17},{10,2},{18,10},{26,18},{... | collective-permute-start | bytes 393224 | tf_op jit(solution)/shard_map/ppermute | solution.py:178
  6.1 19.1 %all-to-all-start = ((bf16[8,16,1024]{2,1,0:T(8,128)(2,1)}), bf16[8,16,1024]{2,1,0:T(8,128)(2,1)S(1)}, u32[]{:S(2)}, u32[]{:S(2)}) async-start(bf16[8,16,1024]{2,1,0:T(8,128)(2,1)} %shard_map.68), calls=%async_computation | async-start | bytes 524288 | tf_op jit(solution)/shard_map/all_to_all | solution.py:185
  14.2 1.0 %copy-start.1 = (bf16[16,2,16,256]{3,2,1,0:T(8,128)(2,1)S(1)}, bf16[16,2,16,256]{3,2,1,0:T(8,128)(2,1)}, u32[]{:S(2)}) copy-start(bf16[16,2,16,256]{3,2,1,0:T(8,128)(2,1)} %v_ref.3) | copy-start | bytes 786436
  15.3 5.8 %collective-permute-start.2 = (bf16[16,1024]{1,0:T(8,128)(2,1)S(1)}, bf16[16,1024]{1,0:T(8,128)(2,1)S(1)}, u32[]{:S(2)}, u32[]{:S(2)}) collective-permute-start(bf16[16,1024]{1,0:T(8,128)(2,1)S(1)} %get-tuple-element.7), channel_id=1, source_target_pairs={{0,1},{1,2},{2,3},{3,4},{4,5},{5,6},{6,7},{8,9},{9,10},{10,11},{11... | collective-permute-start | bytes 98312 | tf_op jit(solution)/shard_map/ppermute | solution.py:190
  19.3 1.5 %copy-start.3 = (bf16[96,32,2,2,2]{0,4,3,2,1:T(2,128)(2,1)S(1)}, bf16[96,32,2,2,2]{0,4,3,2,1:T(2,128)(2,1)}, u32[]{:S(2)}) copy-start(bf16[96,32,2,2,2]{0,4,3,2,1:T(2,128)(2,1)} %param.6) | copy-start | bytes 147460
  19.3 5.9 %collective-permute-start.3 = (bf16[16,1024]{1,0:T(8,128)(2,1)S(1)}, bf16[16,1024]{1,0:T(8,128)(2,1)S(1)}, u32[]{:S(2)}, u32[]{:S(2)}) collective-permute-start(bf16[16,1024]{1,0:T(8,128)(2,1)S(1)} %get-tuple-element.8), channel_id=1, source_target_pairs={{1,0},{2,1},{3,2},{4,3},{5,4},{6,5},{7,6},{9,8},{10,9},{11,10},{12... | collective-permute-start | bytes 98312 | tf_op jit(solution)/shard_map/ppermute | solution.py:191
  43.8 12.8 %all-to-all-start.1 = ((bf16[8,12,1024]{2,1,0:T(8,128)(2,1)}), bf16[8,12,1024]{2,1,0:T(8,128)(2,1)S(1)}, u32[]{:S(2)}, u32[]{:S(2)}) async-start(bf16[8,12,1024]{2,1,0:T(8,128)(2,1)} %get-tuple-element.9), calls=%async_computation.1 | async-start | bytes 524288 | tf_op jit(solution)/shard_map/all_to_all | solution.py:225
  57.3 10.5 %all-to-all-start.3 = ((bf16[32,1,16,128]{3,2,1,0:T(8,128)(2,1)}), bf16[32,1,16,128]{3,2,1,0:T(8,128)(2,1)S(1)}, u32[]{:S(2)}, u32[]{:S(2)}) async-start(bf16[32,1,16,128]{3,2,1,0:T(8,128)(2,1)} %broadcast_in_dim.2), calls=%async_computation.3 | async-start | bytes 262144 | tf_op jit(solution)/shard_map/all_to_all | solution.py:223
where the time goes:
time: 69.9 us; the launch traced here: 69.3 us
  starting transfers between devices  21.8 us (31%)
  waiting for transfers between devices  20.3 us (29%)
  blocking collectives  15.5 us (22%)
  local copies, waits for them, and re-layouts  6.85 us (10%)
  Pallas kernels  3.93 us (6%)
  between operations  0.9 us (1%)
    all_to_all x1, blocking collectives, per_device(): parts = lax.all_to_all(grads, ALL, 0, 0, tiled=True)  15.5 us
    all_to_all x1, waiting for transfers between devices, per_device(): out = lax.all_to_all(out, 'brick', 0, 0, tiled=True)  9.36 us
    all_to_all x1, waiting for transfers between devices, per_device(): lax.all_to_all(whole, ALL, 0, 0, tiled=True).reshape(-1, 16, 128)  6.76 us
    all_to_all x1, starting transfers between devices, per_device(): cotangent = lax.all_to_all(cotangent, 'brick', 0, 0, tiled=True)  6.66 us
    ppermute x1, waiting for transfers between devices, per_device(): after = lax.ppermute(first, 'brick', down)  4.11 us
    pallas_call x3, Pallas kernels, call(): pl.pallas_call(body, out_shape=outs, in_specs=[pl.BlockSpec(memory_space=...  3.93 us
    ppermute x1, starting transfers between devices, per_device(): before = lax.ppermute(last, 'brick', up)  3.92 us
    all_to_all x1, starting transfers between devices, per_device(): out = lax.all_to_all(out, 'brick', 0, 0, tiled=True)  3.41 us
  transfers between devices with their start and end apart: 7, of which 3 were waited for; matrix products, arithmetic and copies ran while one was open for 4% of the time, Pallas kernels for 1%

commit v1 on v0

--- a/solution.py
+++ b/solution.py
@@ -39,23 +39,35 @@
     return lax.dot_general(a, b, (((1,), (1,)), ((), ())), preferred_element_type=f32)
 
 
-def planes(v_ref, low_ref, high_ref):
-    channels, _, rows, cols = v_ref.shape
-    parts = [low_ref[...], v_ref[:, 0], v_ref[:, 1], high_ref[...]]
-    parts = [p.reshape(channels * rows, cols) for p in parts]
+def side_by_side(v_ref):
+    channels, depth, rows, cols = v_ref.shape
+    parts = [v_ref[:, a].reshape(channels * rows, cols) for a in range(depth)]
     return jnp.concatenate(parts, axis=1)
 
 
-def pack_edges(v_ref, low_ref, high_ref, first_ref, last_ref):
+def pack_kernel(v_ref, u_ref, first_ref, last_ref, cot_ref):
     channels, _, rows, _ = v_ref.shape
-    stacked = planes(v_ref, low_ref, high_ref)
     pick = one_hot(
         (2 * channels, channels * rows),
         lambda r: (r % channels) * rows + (r // channels) * (rows - 1),
     )
-    both = dot(pick, stacked).astype(bf16)
+    both = dot(pick, side_by_side(v_ref)).astype(bf16)
     first_ref[...] = both[:channels]
     last_ref[...] = both[channels:]
+    pack_cotangent(u_ref, cot_ref)
+
+
+def turn_kernel(v_ref, before_ref, after_ref, zero_ref, one_ref):
+    channels, _, rows, cols = v_ref.shape
+    swap = one_hot(
+        (channels * rows, channels * rows), lambda r: (r % channels) * rows + r // channels
+    )
+    turned = dot(swap, side_by_side(v_ref)).astype(bf16)
+    for a, out_ref in enumerate((zero_ref, one_ref)):
+        lanes = slice(a * cols, (a + 1) * cols)
+        out_ref[:channels] = before_ref[:, lanes]
+        out_ref[channels : (rows + 1) * channels] = turned[:, lanes]
+        out_ref[(rows + 1) * channels :] = after_ref[:, lanes]
 
 
 def pack_cotangent(u_ref, out_ref):
@@ -69,41 +81,32 @@
 
 def main_kernel(
     own_filters,
-    v_ref,
+    chunks,
     low_ref,
+    zero_ref,
+    one_ref,
     high_ref,
-    before_ref,
-    after_ref,
     g_ref,
     w1_ref,
     w2p_ref,
     w2t_ref,
-    out_ref,
-    grad_ref,
+    send_ref,
     d_ref,
     x_ref,
 ):
-    channels, _, rows, cols = v_ref.shape
-    half = cols // 2
+    rows, channels, half = d_ref.shape[0] - 2, d_ref.shape[3], d_ref.shape[4]
+    cols = 2 * half
     bricks, padded, cells = g_ref.shape
+    slabs = send_ref.shape[0] // bricks
     filters = w2t_ref.shape[1]
-    swap = one_hot(
-        (channels * rows, channels * rows), lambda r: (r % channels) * rows + r // channels
-    )
-    turned = dot(swap, planes(v_ref, low_ref, high_ref)).astype(bf16)
     at = lax.broadcasted_iota(jnp.int32, (cols, 4 * half), 0)
     lane = lax.broadcasted_iota(jnp.int32, (cols, 4 * half), 1)
     spread = jnp.where(at == 2 * (lane % half) + lane // half - 1, 1.0, 0.0).astype(bf16)
-    for a in range(4):
-        lanes = slice(a * cols, (a + 1) * cols)
-        inner = dot(turned[:, lanes], spread).astype(bf16)
-        edge = jnp.concatenate([before_ref[:, lanes], after_ref[:, lanes]], axis=0)
-        edge = dot(edge, spread).astype(bf16)
+    for a, plane_ref in enumerate((low_ref, zero_ref, one_ref, high_ref)):
+        inner = dot(plane_ref[...], spread).astype(bf16)
         for e in range(4):
             piece = slice(e * half, (e + 1) * half)
-            d_ref[1 : rows + 1, a, e] = inner[:, piece].reshape(rows, channels, half)
-            d_ref[0, a, e] = edge[:channels, piece]
-            d_ref[rows + 1, a, e] = edge[channels:, piece]
+            d_ref[:, a, e] = inner[:, piece].reshape(rows + 2, channels, half)
     for j in range(rows // 2):
         window = d_ref[2 * j : 2 * j + 4].reshape(64 * channels, half)
         x_ref[:, j * half : (j + 1) * half] = window
@@ -116,8 +119,15 @@
     sigma = jax.nn.sigmoid(pre)
     hidden = (pre * sigma).astype(bf16)
     result = dot(w2p_ref[...], hidden).astype(bf16)
-    for b in range(bricks):
-        out_ref[b] = result[b * padded : b * padded + own_filters]
+    width = cells // chunks
+    for t in range(slabs):
+        for b in range(bricks):
+            place = t * bricks + b
+            if t < chunks:
+                piece = result[b * padded : (b + 1) * padded, t * width : (t + 1) * width]
+            else:
+                piece = jnp.zeros((padded, width), bf16)
+            send_ref[place, :, 128:] = piece
     back = dot(w2t_ref[...], gradient)
     delta = (back * sigma * (1.0 + pre * (1.0 - sigma))).astype(bf16)
     mid = hidden.shape[0] // 8
@@ -141,10 +151,40 @@
                 moved = jnp.where(group == source, piece, moved)
         amount = (shift * mid) % (4 * mid)
         total = total + (pltpu.roll(moved, amount, 1) if amount else moved)
-    kind = grad_ref.dtype
-    grad_ref[...] = jnp.zeros_like(grad_ref)
-    grad_ref[0:9] = total.astype(kind).reshape(9, channels, 4 * mid)
-    grad_ref[9:25, :, :filters] = grad_two.astype(kind).reshape(16, -1, filters)
+    send_ref[0:9, :, :128] = total.astype(bf16).reshape(9, channels, 4 * mid)
+    send_ref[9:25, :, :filters] = grad_two.astype(bf16).reshape(16, -1, filters)
+    send_ref[9:25, :, filters:128] = jnp.zeros((16, 16, 128 - filters), bf16)
+    send_ref[25:, :, :128] = jnp.zeros((slabs * bricks - 25, 16, 128), bf16)
+
+
+def sum_kernel(got_ref, share_ref, *piece_refs):
+    devices = got_ref.shape[0]
+    bricks = piece_refs[0].shape[0]
+    total = got_ref[0, :, :128].astype(f32)
+    for d in range(1, devices):
+        total = total + got_ref[d, :, :128].astype(f32)
+    total = total.astype(bf16)
+    for d in range(devices):
+        share_ref[d] = total
+    me = lax.axis_index("slab")
+    for k, piece_ref in enumerate(piece_refs):
+        start = jnp.bitwise_xor(me, k) * bricks
+        piece_ref[...] = got_ref[pl.ds(start, bricks), :, 128:]
+
+
+def output_kernel(chunks, *refs):
+    out_ref = refs[-1]
+    own_filters = out_ref.shape[0]
+    bricks, _, width = refs[0].shape
+    me = lax.axis_index("slab")
+    for k, piece_ref in enumerate(refs[:-1]):
+        source = jnp.bitwise_xor(me, k)
+
+        @pl.when(source < chunks)
+        def _():
+            for b in range(bricks):
+                start = pl.multiple_of((b * chunks + source) * width, 128)
+                out_ref[:, pl.ds(start, width)] = piece_ref[b, :own_filters, :]
 
 
 def shifts(count):
@@ -173,41 +213,43 @@
     padded = -(-own_filters // 16) * 16
     cells = (rows // 2) * (cols // 2)
 
-    up, down = shifts(slabs)
-    low = lax.ppermute(volume[:, 1], "slab", up)
-    high = lax.ppermute(volume[:, 0], "slab", down)
-
-    cotangent = call(
-        pack_cotangent,
-        jax.ShapeDtypeStruct((bricks, padded, cells), bf16),
+    chunks = min(slabs, cells // 128)
+
+    edge = jax.ShapeDtypeStruct((channels, 2 * cols), bf16)
+    first, last, cotangent = call(
+        pack_kernel,
+        (edge, edge, jax.ShapeDtypeStruct((bricks, padded, cells), bf16)),
+        volume,
         upstream.reshape(own_filters, -1),
     )
-    cotangent = lax.all_to_all(cotangent, "brick", 0, 0, tiled=True)
-
-    edge = jax.ShapeDtypeStruct((channels, 4 * cols), bf16)
-    first, last = call(pack_edges, (edge, edge), volume, low, high)
     up, down = shifts(bricks)
     before = lax.ppermute(last, "brick", up)
     after = lax.ppermute(first, "brick", down)
-
+    cotangent = lax.all_to_all(cotangent, "brick", 0, 0, tiled=True)
+
+    plane = jax.ShapeDtypeStruct(((rows + 2) * channels, cols), bf16)
+    zero, one = call(turn_kernel, (plane, plane), volume, before, after)
+    up, down = shifts(slabs)
+    low = lax.ppermute(one, "slab", up)
+    high = lax.ppermute(zero, "slab", down)
+
+    zero, one, kernel_one, kernel_two = lax.optimization_barrier(
+        (zero, one, kernel_one, kernel_two)
+    )
     weights_one = place_kernel(kernel_one)
     weights_two = jnp.transpose(kernel_two, (0, 4, 2, 3, 1)).reshape(filters, 8 * mid)
     grouped = weights_two.reshape(bricks, own_filters, 8 * mid)
     grouped = jnp.pad(grouped, ((0, 0), (0, padded - own_filters), (0, 0)))
     grouped = grouped.reshape(bricks * padded, 8 * mid)
 
-    share = -(-GRAD_BLOCKS // devices)
-    out, grads = call(
-        functools.partial(main_kernel, own_filters),
-        (
-            jax.ShapeDtypeStruct((bricks, own_filters, cells), bf16),
-            jax.ShapeDtypeStruct((devices * share, 16, 128), bf16),
-        ),
-        volume,
+    width = cells // chunks
+    send = call(
+        functools.partial(main_kernel, own_filters, chunks),
+        jax.ShapeDtypeStruct((devices, 16, 128 + width), bf16),
         low,
+        zero,
+        one,
         high,
-        before,
-        after,
         cotangent,
         weights_one,
         grouped,
@@ -217,14 +259,25 @@
             pltpu.VMEM((64 * channels, cells), bf16),
         ),
     )
-    parts = lax.all_to_all(grads, ALL, 0, 0, tiled=True)
-    parts = parts.reshape(devices, share, 16, 128).astype(f32).sum(0).astype(bf16)
-    whole = jnp.broadcast_to(parts[None], (devices,) + parts.shape)
-    whole = lax.all_to_all(whole, ALL, 0, 0, tiled=True).reshape(-1, 16, 128).astype(f32)
-
-    out = lax.all_to_all(out, "brick", 0, 0, tiled=True)
-    output = jnp.transpose(out, (1, 0, 2)).reshape(own_filters, 1, -1)
-
+    got = lax.all_to_all(send, ALL, 0, 0, tiled=True)
+    piece = jax.ShapeDtypeStruct((bricks, padded, width), bf16)
+    share, *pieces = call(
+        sum_kernel,
+        (jax.ShapeDtypeStruct((devices, 16, 128), bf16),) + (piece,) * slabs,
+        got,
+    )
+    whole = lax.all_to_all(share, ALL, 0, 0, tiled=True)
+    for k in range(1, slabs):
+        swaps = [(i, i ^ k) for i in range(slabs)]
+        pieces[k] = lax.ppermute(pieces[k], "slab", swaps)
+    output = call(
+        functools.partial(output_kernel, chunks),
+        jax.ShapeDtypeStruct((own_filters, bricks * cells), bf16),
+        *pieces,
+    )
+    output = output.reshape(own_filters, 1, -1)
+
+    whole = whole.astype(f32)
     one = whole[0:9, :, : 3 * mid].reshape(3, 3, channels, 3, mid)
     grad_one = jnp.transpose(one, (4, 2, 3, 0, 1))
     two = whole[9:25].reshape(8 * mid, 128)[:, :filters]

time: 69.9 us -> 60.7 us (0.87)
  waiting for transfers between devices: 20.3 us -> 7.91 us
  blocking collectives: 15.5 us -> 19.8 us
  starting transfers between devices: 21.8 us -> 20.4 us
  Pallas kernels: 3.93 us -> 5.16 us
  local copies, waits for them, and re-layouts: 6.85 us -> 6.13 us
    all_to_all x2 -> x1, waiting for transfers between devices: 16.1 us -> 0.18 us  [per_device(): whole = lax.all_to_all(share, ALL, 0, 0, tiled=True)]
    ppermute x2 -> x5, waiting for transfers between devices: 0.01 us -> 5.77 us  [the longest x3 4.86 us: per_device(): pieces[k] = lax.ppermute(pieces[k], 'slab', swaps)]
    all_to_all x1, blocking collectives: 15.5 us -> 19.8 us  [per_device(): got = lax.all_to_all(send, ALL, 0, 0, tiled=True)]
    ppermute x1, waiting for transfers between devices: 4.11 us -> 0.01 us  [per_device(): after = lax.ppermute(first, 'brick', down)]
    all_to_all x2 -> x1, starting transfers between devices: 6.13 us -> 2.58 us  [per_device(): whole = lax.all_to_all(share, ALL, 0, 0, tiled=True)]
    unnamed x16 -> x18, local copies, waits for them, and re-layouts: 1.56 us -> 3.51 us
    all_to_all x1, waiting for transfers between devices: 0.01 us -> 1.96 us  [per_device(): cotangent = lax.all_to_all(cotangent, 'brick', 0, 0, tiled=True)]
    pallas_call x3 -> x5, Pallas kernels: 3.93 us -> 5.16 us  [call(): pl.pallas_call(body, out_shape=outs, in_specs=[pl.BlockSpec(memory_space=...]
  transfers between devices with their start and end apart: 7 -> 9, of which waited for: 3 -> 5; matrix products, arithmetic and copies ran while one was open for 4% -> 3% of each run, Pallas kernels for 1% -> 2%
where the time goes in v1:
time: 60.7 us; the launch traced here: 60.2 us
  starting transfers between devices  20.4 us (34%)
  blocking collectives  19.8 us (33%)
  waiting for transfers between devices  7.91 us (13%)
  local copies, waits for them, and re-layouts  6.13 us (10%)
  Pallas kernels  5.16 us (9%)
  between operations  0.86 us (1%)
    all_to_all x1, blocking collectives, per_device(): got = lax.all_to_all(send, ALL, 0, 0, tiled=True)  19.8 us
    all_to_all x1, starting transfers between devices, per_device(): cotangent = lax.all_to_all(cotangent, 'brick', 0, 0, tiled=True)  7.1 us
    pallas_call x5, Pallas kernels, call(): pl.pallas_call(body, out_shape=outs, in_specs=[pl.BlockSpec(memory_space=...  5.16 us
    ppermute x3, waiting for transfers between devices, per_device(): pieces[k] = lax.ppermute(pieces[k], 'slab', swaps)  4.86 us
    ppermute x1, starting transfers between devices, per_device(): before = lax.ppermute(last, 'brick', up)  4.86 us
    unnamed x18, local copies, waits for them, and re-layouts  3.51 us
    all_to_all x1, starting transfers between devices, per_device(): whole = lax.all_to_all(share, ALL, 0, 0, tiled=True)  2.58 us
    ppermute x3, starting transfers between devices, per_device(): pieces[k] = lax.ppermute(pieces[k], 'slab', swaps)  1.96 us
  transfers between devices with their start and end apart: 9, of which 5 were waited for; matrix products, arithmetic and copies ran while one was open for 3% of the time, Pallas kernels for 2%

profile of v1, /device:TPU:0, one launch (start us, length us, event | category | flops | bytes accessed | tf_op | source)
XLA Modules:
  0.0 60.2 jit_solution(18047908596505138701)
XLA Ops:
  0.7 1.0 %copy-done.1 = bf16[16,2,16,256]{3,2,1,0:T(8,128)(2,1)S(1)} copy-done((bf16[16,2,16,256]{3,2,1,0:T(8,128)(2,1)S(1)}, bf16[16,2,16,256]{3,2,1,0:T(8,128)(2,1)}, u32[]{:S(2)}) %copy-start.1) | copy-done | bytes 262168
  1.6 0.9 %copy-done.3 = bf16[12,1,8192]{2,0,1:T(8,128)(2,1)S(1)} copy-done((bf16[12,1,8192]{2,0,1:T(8,128)(2,1)S(1)}, bf16[12,1,8192]{2,0,1:T(8,128)(2,1)}, u32[]{:S(2)}) %copy-start.3) | copy-done | bytes 196632
  2.6 0.8 %shard_map.67 = (bf16[16,512]{1,0:T(8,128)(2,1)S(1)}, bf16[16,512]{1,0:T(8,128)(2,1)S(1)}, bf16[8,16,1024]{2,1,0:T(8,128)(2,1)}) custom-call(bf16[16,2,16,256]{3,2,1,0:T(8,128)(2,1)S(1)} %copy-done.1, bf16[12,8192]{1,0:T(8,128)(2,1)S(1)} %bitcast.25), custom_call_target="tpu_custom_call" | custom-call | tf_op jit(solution)/shard_map/pallas_call | solution.py:18
  3.4 4.9 %collective-permute-start = (bf16[16,512]{1,0:T(8,128)(2,1)S(1)}, bf16[16,512]{1,0:T(8,128)(2,1)S(1)}, u32[]{:S(2)}, u32[]{:S(2)}) collective-permute-start(bf16[16,512]{1,0:T(8,128)(2,1)S(1)} %get-tuple-element.17), channel_id=1, source_target_pairs={{0,1},{1,2},{2,3},{3,4},{4,5},{5,6},{6,7},{8,9},{9,10},{10,11},{11... | collective-permute-start | bytes 49160 | tf_op jit(solution)/shard_map/ppermute | solution.py:226
  8.2 1.3 %collective-permute-start.1 = (bf16[16,512]{1,0:T(8,128)(2,1)S(1)}, bf16[16,512]{1,0:T(8,128)(2,1)S(1)}, u32[]{:S(2)}, u32[]{:S(2)}) collective-permute-start(bf16[16,512]{1,0:T(8,128)(2,1)S(1)} %get-tuple-element.18), channel_id=1, source_target_pairs={{1,0},{2,1},{3,2},{4,3},{5,4},{6,5},{7,6},{9,8},{10,9},{11,10},{12... | collective-permute-start | bytes 49160 | tf_op jit(solution)/shard_map/ppermute | solution.py:227
  9.5 7.1 %all-to-all-start = ((bf16[8,16,1024]{2,1,0:T(8,128)(2,1)}), bf16[8,16,1024]{2,1,0:T(8,128)(2,1)S(1)}, u32[]{:S(2)}, u32[]{:S(2)}) async-start(bf16[8,16,1024]{2,1,0:T(8,128)(2,1)} %get-tuple-element.23), calls=%async_computation | async-start | bytes 524288 | tf_op jit(solution)/shard_map/all_to_all | solution.py:228
  16.7 0.2 shard_map.68
  16.9 1.3 %collective-permute-start.2 = (bf16[288,256]{1,0:T(8,128)(2,1)S(1)}, bf16[288,256]{1,0:T(8,128)(2,1)S(1)}, u32[]{:S(2)}, u32[]{:S(2)}) collective-permute-start(bf16[288,256]{1,0:T(8,128)(2,1)S(1)} %get-tuple-element.22.one_ref), channel_id=1, source_target_pairs={{0,8},{8,16},{16,24},{1,9},{9,17},{17,25},{2,10},{10,18},{18,26},{... | collective-permute-start | bytes 442376 | tf_op jit(solution)/shard_map/ppermute | solution.py:233
  18.2 1.3 %collective-permute-start.3 = (bf16[288,256]{1,0:T(8,128)(2,1)S(1)}, bf16[288,256]{1,0:T(8,128)(2,1)S(1)}, u32[]{:S(2)}, u32[]{:S(2)}) collective-permute-start(bf16[288,256]{1,0:T(8,128)(2,1)S(1)} %get-tuple-element.21.zero_ref), channel_id=1, source_target_pairs={{8,0},{16,8},{24,16},{9,1},{17,9},{25,17},{10,2},{18,10},{26,18},{... | collective-permute-start | bytes 442376 | tf_op jit(solution)/shard_map/ppermute | solution.py:234
  19.5 0.5 fusion
  21.0 0.8 %copy-done.4 = bf16[96,32,2,2,2]{0,4,3,2,1:T(2,128)(2,1)S(1)} copy-done((bf16[96,32,2,2,2]{0,4,3,2,1:T(2,128)(2,1)S(1)}, bf16[96,32,2,2,2]{0,4,3,2,1:T(2,128)(2,1)}, u32[]{:S(2)}) %copy-start.4) | copy-done | bytes 49176
  22.3 0.9 %collective-permute-done.3.high_ref = bf16[288,256]{1,0:T(8,128)(2,1)S(1)} collective-permute-done((bf16[288,256]{1,0:T(8,128)(2,1)S(1)}, bf16[288,256]{1,0:T(8,128)(2,1)S(1)}, u32[]{:S(2)}, u32[]{:S(2)}) %collective-permute-start.3) | collective-permute-done | bytes 147488 | tf_op jit(solution)/shard_map/ppermute | solution.py:234
  23.2 2.0 %all-to-all-done.g_ref = bf16[8,16,1024]{2,1,0:T(8,128)(2,1)S(1)} async-done(((bf16[8,16,1024]{2,1,0:T(8,128)(2,1)}), bf16[8,16,1024]{2,1,0:T(8,128)(2,1)S(1)}, u32[]{:S(2)}, u32[]{:S(2)}) %all-to-all-start) | async-done | bytes 262176 | tf_op jit(solution)/shard_map/all_to_all | solution.py:228
  25.1 2.7 %shard_map.69 = bf16[32,16,384]{2,1,0:T(8,128)(2,1)S(1)} custom-call(bf16[288,256]{1,0:T(8,128)(2,1)S(1)} %collective-permute-done.2.low_ref, bf16[288,256]{1,0:T(8,128)(2,1)S(1)} %get-tuple-element.21.zero_ref, bf16[288,256]{1,0:T(8,128)(2,1)S(1)} %get-tuple-element.22.one_ref, bf16[288,256]{1,0:T(8,128)(2,1)S(1)} %collective-permute-done.3.high_ref, ...), custom_call_target="tpu_custom_call" | custom-call | tf_op jit(solution)/shard_map/pallas_call | solution.py:18
  27.9 19.8 %all_to_all.15.got_ref = bf16[32,16,384]{2,1,0:T(8,128)(2,1)S(1)} all-to-all(bf16[32,16,384]{2,1,0:T(8,128)(2,1)S(1)} %shard_map.69), channel_id=1, replica_groups=mesh['slab'=4,'brick'=8] {'slab','brick'}, dimensions={0} | all-to-all | bytes 786432 | tf_op jit(solution)/shard_map/all_to_all | solution.py:262
  47.6 0.7 %shard_map.70 = (bf16[32,16,128]{2,1,0:T(8,128)(2,1)}, bf16[8,16,256]{2,1,0:T(8,128)(2,1)S(1)}, bf16[8,16,256]{2,1,0:T(8,128)(2,1)S(1)}, bf16[8,16,256]{2,1,0:T(8,128)(2,1)S(1)}, bf16[8,16,256]{2,1,0:T(8,128)(2,1)S(1)}) custom-call(bf16[32,16,384]{2,1,0:T(8,128)(2,1)S(1)} %all_to_all.15.got_ref), custom_call_target="tpu_custom_call" | custom-call | tf_op jit(solution)/shard_map/pallas_call | solution.py:18
  48.3 2.6 %all-to-all-start.2 = ((bf16[32,16,128]{2,1,0:T(8,128)(2,1)}), bf16[32,16,128]{2,1,0:T(8,128)(2,1)S(1)}, u32[]{:S(2)}, u32[]{:S(2)}) async-start(bf16[32,16,128]{2,1,0:T(8,128)(2,1)} %get-tuple-element.30), calls=%async_computation.2 | async-start | bytes 262144 | tf_op jit(solution)/shard_map/all_to_all | solution.py:269
  51.1 1.7 %collective-permute-start.5 = (bf16[8,16,256]{2,1,0:T(8,128)(2,1)S(1)}, bf16[8,16,256]{2,1,0:T(8,128)(2,1)S(1)}, u32[]{:S(2)}, u32[]{:S(2)}) collective-permute-start(bf16[8,16,256]{2,1,0:T(8,128)(2,1)S(1)} %get-tuple-element.28), channel_id=1, source_target_pairs={{0,16},{8,24},{16,0},{24,8},{1,17},{9,25},{17,1},{25,9},{2,18},{10... | collective-permute-start | bytes 196616 | tf_op jit(solution)/shard_map/ppermute | solution.py:272
  52.9 3.6 %collective-permute-done.5.refs_2_ = bf16[8,16,256]{2,1,0:T(8,128)(2,1)S(1)} collective-permute-done((bf16[8,16,256]{2,1,0:T(8,128)(2,1)S(1)}, bf16[8,16,256]{2,1,0:T(8,128)(2,1)S(1)}, u32[]{:S(2)}, u32[]{:S(2)}) %collective-permute-start.5) | collective-permute-done | bytes 65568 | tf_op jit(solution)/shard_map/ppermute | solution.py:272
  56.5 1.2 %collective-permute-done.6.refs_3_ = bf16[8,16,256]{2,1,0:T(8,128)(2,1)S(1)} collective-permute-done((bf16[8,16,256]{2,1,0:T(8,128)(2,1)S(1)}, bf16[8,16,256]{2,1,0:T(8,128)(2,1)S(1)}, u32[]{:S(2)}, u32[]{:S(2)}) %collective-permute-start.6) | collective-permute-done | bytes 65568 | tf_op jit(solution)/shard_map/ppermute | solution.py:272
  57.7 0.7 %shard_map.71 = bf16[12,8192]{1,0:T(8,128)(2,1)} custom-call(bf16[8,16,256]{2,1,0:T(8,128)(2,1)S(1)} %get-tuple-element.26.refs_0_, bf16[8,16,256]{2,1,0:T(8,128)(2,1)S(1)} %collective-permute-done.4.refs_1_, bf16[8,16,256]{2,1,0:T(8,128)(2,1)S(1)} %collective-permute-done.5.refs_2_, bf16[8,16,256]{2,1,0:T(8,128)(2,1)S(1)} %collective-permute-done.6.refs_3_), custom_call_target="tpu_custom_call" | custom-call | tf_op jit(solution)/shard_map/pallas_call | solution.py:18
  58.5 0.2 all-to-all-done.2
  58.8 0.7 %copy.35 = f32[32,16,3,3,3]{0,1,4,3,2:T(8,128)} copy(f32[32,16,3,3,3]{0,2,1,4,3:T(4,128)S(1)} %bitcast.28) | data formatting | bytes 110592
  59.5 0.7 %slice.13 = f32[16,16,128]{2,1,0:T(8,128)} slice(bf16[32,16,128]{2,1,0:T(8,128)(2,1)S(1)} %all-to-all-done.2), slice={[9:25], [0:16], [0:128]} | slice | bytes 262144 | tf_op jit(solution)/shard_map/slice | solution.py:283
  (35 shorter events, 1.8 us)
Async XLA Ops:
  0.6 18.9 %copy-start = (bf16[32,16,3,3,3]{0,1,4,3,2:T(8,128)(2,1)S(1)}, bf16[32,16,3,3,3]{0,1,4,3,2:T(8,128)(2,1)}, u32[]{:S(2)}) copy-start(bf16[32,16,3,3,3]{0,1,4,3,2:T(8,128)(2,1)} %param.5) | copy-start | bytes 82948
  0.6 1.0 %copy-start.1 = (bf16[16,2,16,256]{3,2,1,0:T(8,128)(2,1)S(1)}, bf16[16,2,16,256]{3,2,1,0:T(8,128)(2,1)}, u32[]{:S(2)}) copy-start(bf16[16,2,16,256]{3,2,1,0:T(8,128)(2,1)} %v_ref.3) | copy-start | bytes 786436
  1.6 0.9 %copy-start.3 = (bf16[12,1,8192]{2,0,1:T(8,128)(2,1)S(1)}, bf16[12,1,8192]{2,0,1:T(8,128)(2,1)}, u32[]{:S(2)}) copy-start(bf16[12,1,8192]{2,0,1:T(8,128)(2,1)} %param.7) | copy-start | bytes 589828
  3.4 13.3 %collective-permute-start = (bf16[16,512]{1,0:T(8,128)(2,1)S(1)}, bf16[16,512]{1,0:T(8,128)(2,1)S(1)}, u32[]{:S(2)}, u32[]{:S(2)}) collective-permute-start(bf16[16,512]{1,0:T(8,128)(2,1)S(1)} %get-tuple-element.17), channel_id=1, source_target_pairs={{0,1},{1,2},{2,3},{3,4},{4,5},{5,6},{6,7},{8,9},{9,10},{10,11},{11... | collective-permute-start | bytes 49160 | tf_op jit(solution)/shard_map/ppermute | solution.py:226
  8.2 8.4 %collective-permute-start.1 = (bf16[16,512]{1,0:T(8,128)(2,1)S(1)}, bf16[16,512]{1,0:T(8,128)(2,1)S(1)}, u32[]{:S(2)}, u32[]{:S(2)}) collective-permute-start(bf16[16,512]{1,0:T(8,128)(2,1)S(1)} %get-tuple-element.18), channel_id=1, source_target_pairs={{1,0},{2,1},{3,2},{4,3},{5,4},{6,5},{7,6},{9,8},{10,9},{11,10},{12... | collective-permute-start | bytes 49160 | tf_op jit(solution)/shard_map/ppermute | solution.py:227
  9.5 7.1 %copy-start.2 = (bf16[16,2,16,256]{3,2,1,0:T(8,128)(2,1)S(1)}, bf16[16,2,16,256]{3,2,1,0:T(8,128)(2,1)}, u32[]{:S(2)}) copy-start(bf16[16,2,16,256]{3,2,1,0:T(8,128)(2,1)} %v_ref.3) | copy-start | bytes 786436
  9.5 15.6 %all-to-all-start = ((bf16[8,16,1024]{2,1,0:T(8,128)(2,1)}), bf16[8,16,1024]{2,1,0:T(8,128)(2,1)S(1)}, u32[]{:S(2)}, u32[]{:S(2)}) async-start(bf16[8,16,1024]{2,1,0:T(8,128)(2,1)} %get-tuple-element.23), calls=%async_computation | async-start | bytes 524288 | tf_op jit(solution)/shard_map/all_to_all | solution.py:228
  16.9 5.4 %collective-permute-start.2 = (bf16[288,256]{1,0:T(8,128)(2,1)S(1)}, bf16[288,256]{1,0:T(8,128)(2,1)S(1)}, u32[]{:S(2)}, u32[]{:S(2)}) collective-permute-start(bf16[288,256]{1,0:T(8,128)(2,1)S(1)} %get-tuple-element.22.one_ref), channel_id=1, source_target_pairs={{0,8},{8,16},{16,24},{1,9},{9,17},{17,25},{2,10},{10,18},{18,26},{... | collective-permute-start | bytes 442376 | tf_op jit(solution)/shard_map/ppermute | solution.py:233
  18.2 5.0 %collective-permute-start.3 = (bf16[288,256]{1,0:T(8,128)(2,1)S(1)}, bf16[288,256]{1,0:T(8,128)(2,1)S(1)}, u32[]{:S(2)}, u32[]{:S(2)}) collective-permute-start(bf16[288,256]{1,0:T(8,128)(2,1)S(1)} %get-tuple-element.21.zero_ref), channel_id=1, source_target_pairs={{8,0},{16,8},{24,16},{9,1},{17,9},{25,17},{10,2},{18,10},{26,18},{... | collective-permute-start | bytes 442376 | tf_op jit(solution)/shard_map/ppermute | solution.py:234
  20.9 0.8 %copy-start.4 = (bf16[96,32,2,2,2]{0,4,3,2,1:T(2,128)(2,1)S(1)}, bf16[96,32,2,2,2]{0,4,3,2,1:T(2,128)(2,1)}, u32[]{:S(2)}) copy-start(bf16[96,32,2,2,2]{0,4,3,2,1:T(2,128)(2,1)} %param.6) | copy-start | bytes 147460
  48.3 10.3 %all-to-all-start.2 = ((bf16[32,16,128]{2,1,0:T(8,128)(2,1)}), bf16[32,16,128]{2,1,0:T(8,128)(2,1)S(1)}, u32[]{:S(2)}, u32[]{:S(2)}) async-start(bf16[32,16,128]{2,1,0:T(8,128)(2,1)} %get-tuple-element.30), calls=%async_computation.2 | async-start | bytes 262144 | tf_op jit(solution)/shard_map/all_to_all | solution.py:269
  50.9 2.0 %collective-permute-start.4 = (bf16[8,16,256]{2,1,0:T(8,128)(2,1)S(1)}, bf16[8,16,256]{2,1,0:T(8,128)(2,1)S(1)}, u32[]{:S(2)}, u32[]{:S(2)}) collective-permute-start(bf16[8,16,256]{2,1,0:T(8,128)(2,1)S(1)} %get-tuple-element.27), channel_id=1, source_target_pairs={{0,8},{8,0},{16,24},{24,16},{1,9},{9,1},{17,25},{25,17},{2,10},{10... | collective-permute-start | bytes 196616 | tf_op jit(solution)/shard_map/ppermute | solution.py:272
  51.1 5.4 %collective-permute-start.5 = (bf16[8,16,256]{2,1,0:T(8,128)(2,1)S(1)}, bf16[8,16,256]{2,1,0:T(8,128)(2,1)S(1)}, u32[]{:S(2)}, u32[]{:S(2)}) collective-permute-start(bf16[8,16,256]{2,1,0:T(8,128)(2,1)S(1)} %get-tuple-element.28), channel_id=1, source_target_pairs={{0,16},{8,24},{16,0},{24,8},{1,17},{9,25},{17,1},{25,9},{2,18},{10... | collective-permute-start | bytes 196616 | tf_op jit(solution)/shard_map/ppermute | solution.py:272
  52.8 5.0 %collective-permute-start.6 = (bf16[8,16,256]{2,1,0:T(8,128)(2,1)S(1)}, bf16[8,16,256]{2,1,0:T(8,128)(2,1)S(1)}, u32[]{:S(2)}, u32[]{:S(2)}) collective-permute-start(bf16[8,16,256]{2,1,0:T(8,128)(2,1)S(1)} %get-tuple-element.29), channel_id=1, source_target_pairs={{0,24},{8,16},{16,8},{24,0},{1,25},{9,17},{17,9},{25,1},{2,26},{10... | collective-permute-start | bytes 196616 | tf_op jit(solution)/shard_map/ppermute | solution.py:272

commit v2 on v1

v2 whole, which is shorter than its diff:
```python
import functools

import jax
import jax.numpy as jnp
from jax import lax
from jax.experimental import pallas as pl
from jax.experimental.pallas import tpu as pltpu
from jax.sharding import PartitionSpec as P

bf16 = jnp.bfloat16
f32 = jnp.float32
ALL = ("slab", "brick")
LIMIT = 40 * 1024 * 1024
GRAD_BLOCKS = 9 + 16


def call(body, outs, *args, scratch=(), hbm=(), hbm_outs=()):
    vmem, anywhere = (pl.BlockSpec(memory_space=s) for s in (pltpu.VMEM, pl.ANY))
    return pl.pallas_call(
        body,
        out_shape=outs,
        in_specs=[anywhere if i in hbm else vmem for i in range(len(args))],
        out_specs=tuple(anywhere if i in hbm_outs else vmem for i in range(len(outs))),
        scratch_shapes=list(scratch),
        compiler_params=pltpu.CompilerParams(vmem_limit_bytes=LIMIT),
    )(*args)


def one_hot(shape, source_of_row):
    rows = lax.broadcasted_iota(jnp.int32, shape, 0)
    cols = lax.broadcasted_iota(jnp.int32, shape, 1)
    return jnp.where(cols == source_of_row(rows), 1.0, 0.0).astype(bf16)


def dot(a, b):
    return jnp.dot(a, b, preferred_element_type=f32)


def dot_nt(a, b):
    return lax.dot_general(a, b, (((1,), (1,)), ((), ())), preferred_element_type=f32)


def is_even(axis):
    return lax.axis_index(axis) % 2 == 0


def pack_kernel(v_ref, u_ref, near_ref, far_ref, turned_ref, cot_ref, held, v_sems, u_sems):
    channels, depth, rows, cols = v_ref.shape
    bricks, _, cells = cot_ref.shape
    v_copies = [
        pltpu.make_async_copy(v_ref.at[:, a], held.at[a], v_sems.at[a]) for a in range(depth)
    ]
    u_copies = [
        pltpu.make_async_copy(
            u_ref.at[:, pl.ds(b * cells, cells)], cot_ref.at[b], u_sems.at[b]
        )
        for b in range(bricks)
    ]
    for copy in v_copies + u_copies:
        copy.start()
    swap = one_hot(
        (channels * rows, channels * rows), lambda r: (r % channels) * rows + r // channels
    )
    for copy in v_copies:
        copy.wait()
    planes = [held[a].reshape(channels * rows, cols) for a in range(depth)]
    turned = dot(swap, jnp.concatenate(planes, axis=1)).astype(bf16)
    turned_ref[...] = turned
    first, last = turned[:channels], turned[(rows - 1) * channels :]
    even = is_even("brick")
    near_ref[...] = jnp.where(even, last, first)
    far_ref[...] = jnp.where(even, first, last)
    for copy in u_copies:
        copy.wait()


def face_kernel(turned_ref, near_ref, far_ref, send_near_ref, send_far_ref):
    channels = near_ref.shape[0]
    inner, cols = turned_ref.shape[0], turned_ref.shape[1] // 2
    even = is_even("brick")
    before = jnp.where(even, far_ref[...], near_ref[...])
    after = jnp.where(even, near_ref[...], far_ref[...])
    even = is_even("slab")
    for out_ref, upper in ((send_near_ref, even), (send_far_ref, jnp.logical_not(even))):
        for rows, block in (
            (slice(0, channels), before),
            (slice(channels, channels + inner), turned_ref[...]),
            (slice(channels + inner, inner + 2 * channels), after),
        ):
            out_ref[rows] = jnp.where(upper, block[:, cols:], block[:, :cols])


def main_kernel(
    chunks,
    got_near_ref,
    near_ref,
    far_ref,
    got_far_ref,
    g_ref,
    w1_ref,
    w2p_ref,
    w2t_ref,
    send_ref,
    d_ref,
    x_ref,
):
    rows, channels, half = d_ref.shape[0] - 2, d_ref.shape[3], d_ref.shape[4]
    cols = 2 * half
    bricks, own_filters, cells = g_ref.shape
    slabs = send_ref.shape[0] // bricks
    filters = w2t_ref.shape[1]
    padded = w2p_ref.shape[0] // bricks
    at = lax.broadcasted_iota(jnp.int32, (cols, 4 * half), 0)
    lane = lax.broadcasted_iota(jnp.int32, (cols, 4 * half), 1)
    spread = jnp.where(at == 2 * (lane % half) + lane // half - 1, 1.0, 0.0).astype(bf16)
    even = is_even("slab")
    for i, plane_ref in enumerate((got_near_ref, near_ref, far_ref, got_far_ref)):
        a = jnp.where(even, 3 - i, i)
        inner = dot(plane_ref[...], spread).astype(bf16)
        for e in range(4):
            piece = slice(e * half, (e + 1) * half)
            d_ref[:, a, e] = inner[:, piece].reshape(rows + 2, channels, half)
    for j in range(rows // 2):
        window = d_ref[2 * j : 2 * j + 4].reshape(64 * channels, half)
        x_ref[:, j * half : (j + 1) * half] = window
    gradient = jnp.concatenate([g_ref[b].astype(f32) for b in range(bricks)], axis=0)
    gradient = gradient.astype(bf16)

    pre = dot(w1_ref[...], x_ref[...])
    sigma = jax.nn.sigmoid(pre)
    hidden = (pre * sigma).astype(bf16)
    result = dot(w2p_ref[...], hidden)
    width = cells // chunks
    used = own_filters * (width // 128)
    for t in range(slabs):
        for b in range(bricks):
            pieces = [
                result[b * padded : b * padded + own_filters, at : at + 128]
                for at in range(t * width, (t + 1) * width, 128)
                if t < chunks
            ]
            filler = send_ref.shape[1] - 16 - (used if pieces else 0)
            if filler:
                pieces.append(jnp.zeros((filler, 128), f32))
            send_ref[t * bricks + b, 16:] = jnp.concatenate(pieces, axis=0).astype(bf16)
    back = dot(w2t_ref[...], gradient)
    delta = (back * sigma * (1.0 + pre * (1.0 - sigma))).astype(bf16)
    mid = hidden.shape[0] // 8
    natural = one_hot(
        (8 * mid, 8 * mid),
        lambda s: (s % 2) * (4 * mid) + ((s // 2) % 4) * mid + s // 8,
    )
    ordered = dot(natural, hidden).astype(bf16)
    grad_two = dot_nt(ordered, gradient)
    moments = dot_nt(x_ref[...], delta).reshape(4, 4, 4, channels, 8 * mid)
    by_r = moments[:, :, 0:3, :, : 4 * mid] + moments[:, :, 1:4, :, 4 * mid :]
    group = lax.broadcasted_iota(jnp.int32, (9 * channels, 4 * mid), 1) // mid
    total = jnp.zeros((9 * channels, 4 * mid), f32)
    for shift in range(-3, 3):
        moved = jnp.zeros((9 * channels, 4 * mid), f32)
        for a in range(3):
            source = a - shift
            if 0 <= source < 4:
                p, q = source // 2, source % 2
                piece = by_r[q : q + 3, a + p].reshape(9 * channels, 4 * mid)
                moved = jnp.where(group == source, piece, moved)
        amount = (shift * mid) % (4 * mid)
        total = total + (pltpu.roll(moved, amount, 1) if amount else moved)
    send_ref[0:9, :16] = total.astype(bf16).reshape(9, channels, 4 * mid)
    send_ref[9:25, :16, :filters] = grad_two.astype(bf16).reshape(16, -1, filters)
    send_ref[9:25, :16, filters:] = jnp.zeros((16, 16, 128 - filters), bf16)
    send_ref[25:, :16] = jnp.zeros((slabs * bricks - 25, 16, 128), bf16)


def sum_kernel(got_ref, share_ref, *piece_refs):
    devices = got_ref.shape[0]
    bricks = piece_refs[0].shape[0]
    total = got_ref[0, :16].astype(f32)
    for d in range(1, devices):
        total = total + got_ref[d, :16].astype(f32)
    total = total.astype(bf16)
    for d in range(devices):
        share_ref[d] = total
    me = lax.axis_index("slab")
    for k, piece_ref in enumerate(piece_refs):
        start = jnp.bitwise_xor(me, k) * bricks
        piece_ref[...] = got_ref[pl.ds(start, bricks), 16:]


def final_kernel(chunks, whole_ref, *refs):
    out_ref, one_ref, two_ref = refs[-3:]
    own_filters = out_ref.shape[0]
    bricks = refs[0].shape[0]
    width = out_ref.shape[1] // (bricks * chunks)
    me = lax.axis_index("slab")
    for k, piece_ref in enumerate(refs[:-3]):
        source = jnp.bitwise_xor(me, k)

        @pl.when(source < chunks)
        def _():
            for b in range(bricks):
                piece = piece_ref[b].astype(f32)
                for u in range(width // 128):
                    start = pl.multiple_of((b * chunks + source) * width + u * 128, 128)
                    rows = piece[u * own_filters : (u + 1) * own_filters]
                    out_ref[:, pl.ds(start, 128)] = rows.astype(bf16)

    mid = one_ref.shape[4]
    for b in range(3):
        for e in range(3):
            block = whole_ref[3 * b + e].astype(f32)
            for a in range(3):
                one_ref[a, b, e] = block[:, a * mid : (a + 1) * mid]
    two = whole_ref[9:25].astype(f32).reshape(two_ref.shape[0], 128)
    two_ref[...] = two[:, : two_ref.shape[1]]


def swaps(count):
    near, far = ([(i, i + 1) for i in range(s, count - 1, 2)] for s in (0, 1))
    return [pairs + [(j, i) for i, j in pairs] for pairs in (near, far)]


def place_kernel(kernel_one):
    base = jnp.transpose(kernel_one, (0, 3, 2, 4, 1))
    out = base.shape[0]
    pieces = []
    for r in (0, 1):
        for p in (0, 1):
            for q in (0, 1):
                pads = ((0, 0), (q, 1 - q), (p, 1 - p), (r, 1 - r), (0, 0))
                pieces.append(jnp.pad(base, pads).reshape(out, -1))
    return jnp.concatenate(pieces, axis=0)


def per_device(volume, kernel_one, kernel_two, upstream):
    channels, _, rows, cols = volume.shape
    bricks, slabs = lax.axis_size("brick"), lax.axis_size("slab")
    devices = bricks * slabs
    filters, mid = kernel_two.shape[:2]
    own_filters = filters // bricks
    padded = -(-own_filters // 16) * 16
    cells = (rows // 2) * (cols // 2)

    chunks = min(slabs, cells // 128)

    edge = jax.ShapeDtypeStruct((channels, 2 * cols), bf16)
    near, far, turned, cotangent = call(
        pack_kernel,
        (
            edge,
            edge,
            jax.ShapeDtypeStruct((rows * channels, 2 * cols), bf16),
            jax.ShapeDtypeStruct((bricks, own_filters, cells), bf16),
        ),
        volume,
        upstream.reshape(own_filters, -1),
        scratch=(
            pltpu.VMEM((2, channels, rows, cols), bf16),
            pltpu.SemaphoreType.DMA((2,)),
            pltpu.SemaphoreType.DMA((bricks,)),
        ),
        hbm=(0, 1),
        hbm_outs=(3,),
    )
    near_pairs, far_pairs = swaps(bricks)
    far = lax.ppermute(far, "brick", far_pairs)
    near = lax.ppermute(near, "brick", near_pairs)
    cotangent = lax.all_to_all(cotangent, "brick", 0, 0, tiled=True)

    plane = jax.ShapeDtypeStruct(((rows + 2) * channels, cols), bf16)
    near, far = call(face_kernel, (plane, plane), turned, near, far)
    near_pairs, far_pairs = swaps(slabs)
    got_far = lax.ppermute(far, "slab", far_pairs)
    got_near = lax.ppermute(near, "slab", near_pairs)

    near, far, kernel_one, kernel_two = lax.optimization_barrier(
        (near, far, kernel_one, kernel_two)
    )
    weights_one = place_kernel(kernel_one)
    weights_two = jnp.transpose(kernel_two, (0, 4, 2, 3, 1)).reshape(filters, 8 * mid)
    grouped = weights_two.reshape(bricks, own_filters, 8 * mid)
    grouped = jnp.pad(grouped, ((0, 0), (0, padded - own_filters), (0, 0)))
    grouped = grouped.reshape(bricks * padded, 8 * mid)

    width = cells // chunks
    chunk_rows = -(-own_filters * width // 128 // 8) * 8
    (send,) = call(
        functools.partial(main_kernel, chunks),
        (jax.ShapeDtypeStruct((devices, 16 + chunk_rows, 128), bf16),),
        got_near,
        near,
        far,
        got_far,
        cotangent,
        weights_one,
        grouped,
        weights_two.T,
        scratch=(
            pltpu.VMEM((rows + 2, 4, 4, channels, cols // 2), bf16),
            pltpu.VMEM((64 * channels, cells), bf16),
        ),
    )
    got = lax.all_to_all(send, ALL, 0, 0, tiled=True)
    piece = jax.ShapeDtypeStruct((bricks, chunk_rows, 128), bf16)
    share, *pieces = call(
        sum_kernel,
        (jax.ShapeDtypeStruct((devices, 16, 128), bf16),) + (piece,) * slabs,
        got,
    )
    whole = lax.all_to_all(share, ALL, 0, 0, tiled=True)
    for k in range(1, slabs):
        pairs = [(i, i ^ k) for i in range(slabs)]
        pieces[k] = lax.ppermute(pieces[k], "slab", pairs)
    output, one, two = call(
        functools.partial(final_kernel, chunks),
        (
            jax.ShapeDtypeStruct((own_filters, bricks * cells), bf16),
            jax.ShapeDtypeStruct((3, 3, 3, channels, mid), f32),
            jax.ShapeDtypeStruct((8 * mid, filters), f32),
        ),
        whole,
        *pieces,
    )
    output = output.reshape(own_filters, 1, -1)
    grad_one = jnp.transpose(one, (4, 3, 0, 1, 2))
    grad_two = jnp.transpose(two.reshape(mid, 2, 2, 2, filters), (4, 0, 1, 2, 3))
    return output, grad_one, grad_two


def solution(mesh):
    in_specs = (P(None, "slab", "brick", None), P(), P(), P("brick", "slab", None))
    out_specs = (P("brick", "slab", None), P(), P())
    return jax.shard_map(
        per_device, mesh=mesh, in_specs=in_specs, out_specs=out_specs, check_vma=False
    )
```

time: 60.7 us -> 54.4 us (0.90)
  starting transfers between devices: 20.4 us -> 16.6 us
  blocking collectives: 19.8 us -> 16.1 us
  waiting for transfers between devices: 7.91 us -> 10.7 us
  local copies, waits for them, and re-layouts: 6.13 us -> 4.59 us
    ppermute x7, starting transfers between devices: 10.7 us -> 6.38 us  [the longest x1 3.03 us: per_device(): near = lax.ppermute(near, 'brick', near_pairs)]
    all_to_all x1, blocking collectives: 19.8 us -> 16.1 us  [per_device(): got = lax.all_to_all(send, ALL, 0, 0, tiled=True)]
    all_to_all x1, waiting for transfers between devices: 1.96 us -> 4.9 us  [per_device(): cotangent = lax.all_to_all(cotangent, 'brick', 0, 0, tiled=True)]
    ppermute x7, waiting for transfers between devices: 5.77 us -> 4.07 us  [the longest x3 4.06 us: per_device(): pieces[k] = lax.ppermute(pieces[k], 'slab', pairs)]
    all_to_all x1, waiting for transfers between devices: 0.18 us -> 1.72 us  [per_device(): whole = lax.all_to_all(share, ALL, 0, 0, tiled=True)]
    unnamed x18 -> x15, local copies, waits for them, and re-layouts: 3.51 us -> 2.8 us
    slice x2 -> x0, local copies, waits for them, and re-layouts: 0.67 us -> none  [the longest x1 0.66 us: per_device(): two = whole[9:25].reshape(8 * mid, 128)[:, :filters]]
  transfers between devices with their start and end apart: 9 -> 9, of which waited for: 5 -> 4; matrix products, arithmetic and copies ran while one was open for 3% -> 3% of each run, Pallas kernels for 2% -> 0%
where the time goes in v2:
time: 54.4 us; the launch traced here: 54 us
  starting transfers between devices  16.6 us (31%)
  blocking collectives  16.1 us (30%)
  waiting for transfers between devices  10.7 us (20%)
  Pallas kernels  5.28 us (10%)
  local copies, waits for them, and re-layouts  4.59 us (8%)
  between operations  0.85 us (2%)
    all_to_all x1, blocking collectives, per_device(): got = lax.all_to_all(send, ALL, 0, 0, tiled=True)  16.1 us
    all_to_all x1, starting transfers between devices, per_device(): cotangent = lax.all_to_all(cotangent, 'brick', 0, 0, tiled=True)  7.6 us
    pallas_call x5, Pallas kernels, call(): pl.pallas_call(body, out_shape=outs, in_specs=[anywhere if i in hbm else...  5.28 us
    all_to_all x1, waiting for transfers between devices, per_device(): cotangent = lax.all_to_all(cotangent, 'brick', 0, 0, tiled=True)  4.9 us
    ppermute x3, waiting for transfers between devices, per_device(): pieces[k] = lax.ppermute(pieces[k], 'slab', pairs)  4.06 us
    ppermute x1, starting transfers between devices, per_device(): near = lax.ppermute(near, 'brick', near_pairs)  3.03 us
    unnamed x15, local copies, waits for them, and re-layouts  2.8 us
    all_to_all x1, starting transfers between devices, per_device(): whole = lax.all_to_all(share, ALL, 0, 0, tiled=True)  2.58 us
  transfers between devices with their start and end apart: 9, of which 4 were waited for; matrix products, arithmetic and copies ran while one was open for 3% of the time, Pallas kernels for 0%

profile of v2, /device:TPU:0, one launch (start us, length us, event | category | flops | bytes accessed | tf_op | source)
XLA Modules:
  0.0 54.0 jit_solution(16148430363454491250)
XLA Ops:
  0.7 1.0 %copy-done.1 = bf16[16,2,16,256]{3,2,1,0:T(8,128)(2,1)S(1)} copy-done((bf16[16,2,16,256]{3,2,1,0:T(8,128)(2,1)S(1)}, bf16[16,2,16,256]{3,2,1,0:T(8,128)(2,1)}, u32[]{:S(2)}) %copy-start.1) | copy-done | bytes 262168
  1.6 0.9 %copy-done.2 = bf16[12,1,8192]{2,0,1:T(8,128)(2,1)S(1)} copy-done((bf16[12,1,8192]{2,0,1:T(8,128)(2,1)S(1)}, bf16[12,1,8192]{2,0,1:T(8,128)(2,1)}, u32[]{:S(2)}) %copy-start.2) | copy-done | bytes 196632
  2.6 0.8 %shard_map.67 = (bf16[16,512]{1,0:T(8,128)(2,1)S(1)}, bf16[16,512]{1,0:T(8,128)(2,1)S(1)}, bf16[256,512]{1,0:T(8,128)(2,1)S(1)}, bf16[8,12,1024]{2,1,0:T(8,128)(2,1)}) custom-call(bf16[16,2,16,256]{3,2,1,0:T(8,128)(2,1)S(1)} %copy-done.1, bf16[12,8192]{1,0:T(8,128)(2,1)S(1)} %bitcast.25), custom_call_target="tpu_custom_call" | custom-call | tf_op jit(solution)/shard_map/pallas_call | solution.py:19
  3.4 3.0 %collective-permute-start = (bf16[16,512]{1,0:T(8,128)(2,1)S(1)}, bf16[16,512]{1,0:T(8,128)(2,1)S(1)}, u32[]{:S(2)}, u32[]{:S(2)}) collective-permute-start(bf16[16,512]{1,0:T(8,128)(2,1)S(1)} %get-tuple-element.22), channel_id=1, source_target_pairs={{0,1},{2,3},{4,5},{6,7},{1,0},{3,2},{5,4},{7,6},{8,9},{10,11},{12,... | collective-permute-start | bytes 49160 | tf_op jit(solution)/shard_map/ppermute | solution.py:267
  6.4 0.7 %collective-permute-start.1 = (bf16[16,512]{1,0:T(8,128)(2,1)S(1)}, bf16[16,512]{1,0:T(8,128)(2,1)S(1)}, u32[]{:S(2)}, u32[]{:S(2)}) collective-permute-start(bf16[16,512]{1,0:T(8,128)(2,1)S(1)} %get-tuple-element.23), channel_id=1, source_target_pairs={{1,2},{3,4},{5,6},{2,1},{4,3},{6,5},{9,10},{11,12},{13,14},{10,9},... | collective-permute-start | bytes 49160 | tf_op jit(solution)/shard_map/ppermute | solution.py:266
  7.1 7.6 %all-to-all-start = ((bf16[8,12,1024]{2,1,0:T(8,128)(2,1)}), bf16[8,12,1024]{2,1,0:T(8,128)(2,1)S(1)}, u32[]{:S(2)}, u32[]{:S(2)}) async-start(bf16[8,12,1024]{2,1,0:T(8,128)(2,1)} %get-tuple-element.28), calls=%async_computation | async-start | bytes 524288 | tf_op jit(solution)/shard_map/all_to_all | solution.py:268
  14.8 0.7 %collective-permute-start.3 = (bf16[288,256]{1,0:T(8,128)(2,1)S(1)}, bf16[288,256]{1,0:T(8,128)(2,1)S(1)}, u32[]{:S(2)}, u32[]{:S(2)}) collective-permute-start(bf16[288,256]{1,0:T(8,128)(2,1)S(1)} %get-tuple-element.27.far_ref), channel_id=1, source_target_pairs={{8,16},{16,8},{9,17},{17,9},{10,18},{18,10},{11,19},{19,11},{12,20... | collective-permute-start | bytes 442376 | tf_op jit(solution)/shard_map/ppermute | solution.py:273
  15.5 0.5 fusion
  16.1 0.1 copy.27
  16.8 0.1 copy.29
  17.0 0.8 %copy-done.3 = bf16[96,32,2,2,2]{0,4,3,2,1:T(2,128)(2,1)S(1)} copy-done((bf16[96,32,2,2,2]{0,4,3,2,1:T(2,128)(2,1)S(1)}, bf16[96,32,2,2,2]{0,4,3,2,1:T(2,128)(2,1)}, u32[]{:S(2)}) %copy-start.3) | copy-done | bytes 49176
  17.8 0.2 copy.32
  18.0 0.2 reshape_reshape.3
  18.3 4.9 %all-to-all-done.g_ref = bf16[8,12,1024]{2,1,0:T(8,128)(2,1)S(1)} async-done(((bf16[8,12,1024]{2,1,0:T(8,128)(2,1)}), bf16[8,12,1024]{2,1,0:T(8,128)(2,1)S(1)}, u32[]{:S(2)}, u32[]{:S(2)}) %all-to-all-start) | async-done | bytes 196640 | tf_op jit(solution)/shard_map/all_to_all | solution.py:268
  23.2 2.8 %shard_map.69 = bf16[32,40,128]{2,1,0:T(8,128)(2,1)S(1)} custom-call(bf16[288,256]{1,0:T(8,128)(2,1)S(1)} %collective-permute-done.2.got_near_ref, bf16[288,256]{1,0:T(8,128)(2,1)S(1)} %get-tuple-element.26.near_ref, bf16[288,256]{1,0:T(8,128)(2,1)S(1)} %get-tuple-element.27.far_ref, bf16[288,256]{1,0:T(8,128)(2,1)S(1)} %collective-permute-done.3.got_far_ref, ...), custom_call_target="tpu_custom_call" | custom-call | tf_op jit(solution)/shard_map/pallas_call | solution.py:19
  26.0 16.1 %all_to_all.15.got_ref = bf16[32,40,128]{2,1,0:T(8,128)(2,1)S(1)} all-to-all(bf16[32,40,128]{2,1,0:T(8,128)(2,1)S(1)} %shard_map.69), channel_id=1, replica_groups=mesh['slab'=4,'brick'=8] {'slab','brick'}, dimensions={0} | all-to-all | bytes 655360 | tf_op jit(solution)/shard_map/all_to_all | solution.py:303
  42.1 0.7 %shard_map.70 = (bf16[32,16,128]{2,1,0:T(8,128)(2,1)}, bf16[8,24,128]{2,1,0:T(8,128)(2,1)S(1)}, bf16[8,24,128]{2,1,0:T(8,128)(2,1)S(1)}, bf16[8,24,128]{2,1,0:T(8,128)(2,1)S(1)}, bf16[8,24,128]{2,1,0:T(8,128)(2,1)S(1)}) custom-call(bf16[32,40,128]{2,1,0:T(8,128)(2,1)S(1)} %all_to_all.15.got_ref), custom_call_target="tpu_custom_call" | custom-call | tf_op jit(solution)/shard_map/pallas_call | solution.py:19
  42.8 2.6 %all-to-all-start.2 = ((bf16[32,16,128]{2,1,0:T(8,128)(2,1)}), bf16[32,16,128]{2,1,0:T(8,128)(2,1)S(1)}, u32[]{:S(2)}, u32[]{:S(2)}) async-start(bf16[32,16,128]{2,1,0:T(8,128)(2,1)} %get-tuple-element.31), calls=%async_computation.2 | async-start | bytes 262144 | tf_op jit(solution)/shard_map/all_to_all | solution.py:310
  45.4 0.2 collective-permute-start.4
  45.5 1.7 %collective-permute-start.5 = (bf16[8,24,128]{2,1,0:T(8,128)(2,1)S(1)}, bf16[8,24,128]{2,1,0:T(8,128)(2,1)S(1)}, u32[]{:S(2)}, u32[]{:S(2)}) collective-permute-start(bf16[8,24,128]{2,1,0:T(8,128)(2,1)S(1)} %get-tuple-element.34), channel_id=1, source_target_pairs={{0,16},{8,24},{16,0},{24,8},{1,17},{9,25},{17,1},{25,9},{2,18},{10... | collective-permute-start | bytes 147464 | tf_op jit(solution)/shard_map/ppermute | solution.py:313
  47.3 2.8 %collective-permute-done.5.refs_2_ = bf16[8,24,128]{2,1,0:T(8,128)(2,1)S(1)} collective-permute-done((bf16[8,24,128]{2,1,0:T(8,128)(2,1)S(1)}, bf16[8,24,128]{2,1,0:T(8,128)(2,1)S(1)}, u32[]{:S(2)}, u32[]{:S(2)}) %collective-permute-start.5) | collective-permute-done | bytes 49184 | tf_op jit(solution)/shard_map/ppermute | solution.py:313
  50.1 1.2 %collective-permute-done.6.refs_3_ = bf16[8,24,128]{2,1,0:T(8,128)(2,1)S(1)} collective-permute-done((bf16[8,24,128]{2,1,0:T(8,128)(2,1)S(1)}, bf16[8,24,128]{2,1,0:T(8,128)(2,1)S(1)}, u32[]{:S(2)}, u32[]{:S(2)}) %collective-permute-start.6) | collective-permute-done | bytes 49184 | tf_op jit(solution)/shard_map/ppermute | solution.py:313
  51.4 1.7 %all-to-all-done.2.whole_ref = bf16[32,16,128]{2,1,0:T(8,128)(2,1)S(1)} async-done(((bf16[32,16,128]{2,1,0:T(8,128)(2,1)}), bf16[32,16,128]{2,1,0:T(8,128)(2,1)S(1)}, u32[]{:S(2)}, u32[]{:S(2)}) %all-to-all-start.2) | async-done | bytes 131104 | tf_op jit(solution)/shard_map/all_to_all | solution.py:310
  53.1 0.9 %shard_map.71 = (bf16[12,8192]{1,0:T(8,128)(2,1)}, f32[3,3,3,16,32]{4,3,2,1,0:T(8,128)}, f32[256,96]{1,0:T(8,128)}) custom-call(bf16[32,16,128]{2,1,0:T(8,128)(2,1)S(1)} %all-to-all-done.2.whole_ref, bf16[8,24,128]{2,1,0:T(8,128)(2,1)S(1)} %get-tuple-element.32.refs_0_, bf16[8,24,128]{2,1,0:T(8,128)(2,1)S(1)} %collective-permute-done.4.refs_1_, ...), custom_call_target="tpu_custom_call" | custom-call | tf_op jit(solution)/shard_map/pallas_call | solution.py:19
  (29 shorter events, 1.0 us)
Async XLA Ops:
  0.6 14.9 %copy-start = (bf16[32,16,3,3,3]{0,1,4,3,2:T(8,128)(2,1)S(1)}, bf16[32,16,3,3,3]{0,1,4,3,2:T(8,128)(2,1)}, u32[]{:S(2)}) copy-start(bf16[32,16,3,3,3]{0,1,4,3,2:T(8,128)(2,1)} %param.5) | copy-start | bytes 82948
  0.6 1.0 %copy-start.1 = (bf16[16,2,16,256]{3,2,1,0:T(8,128)(2,1)S(1)}, bf16[16,2,16,256]{3,2,1,0:T(8,128)(2,1)}, u32[]{:S(2)}) copy-start(bf16[16,2,16,256]{3,2,1,0:T(8,128)(2,1)} %v_ref.1) | copy-start | bytes 786436
  1.6 0.9 %copy-start.2 = (bf16[12,1,8192]{2,0,1:T(8,128)(2,1)S(1)}, bf16[12,1,8192]{2,0,1:T(8,128)(2,1)}, u32[]{:S(2)}) copy-start(bf16[12,1,8192]{2,0,1:T(8,128)(2,1)} %param.7) | copy-start | bytes 589828
  3.4 11.3 %collective-permute-start = (bf16[16,512]{1,0:T(8,128)(2,1)S(1)}, bf16[16,512]{1,0:T(8,128)(2,1)S(1)}, u32[]{:S(2)}, u32[]{:S(2)}) collective-permute-start(bf16[16,512]{1,0:T(8,128)(2,1)S(1)} %get-tuple-element.22), channel_id=1, source_target_pairs={{0,1},{2,3},{4,5},{6,7},{1,0},{3,2},{5,4},{7,6},{8,9},{10,11},{12,... | collective-permute-start | bytes 49160 | tf_op jit(solution)/shard_map/ppermute | solution.py:267
  6.4 8.3 %collective-permute-start.1 = (bf16[16,512]{1,0:T(8,128)(2,1)S(1)}, bf16[16,512]{1,0:T(8,128)(2,1)S(1)}, u32[]{:S(2)}, u32[]{:S(2)}) collective-permute-start(bf16[16,512]{1,0:T(8,128)(2,1)S(1)} %get-tuple-element.23), channel_id=1, source_target_pairs={{1,2},{3,4},{5,6},{2,1},{4,3},{6,5},{9,10},{11,12},{13,14},{10,9},... | collective-permute-start | bytes 49160 | tf_op jit(solution)/shard_map/ppermute | solution.py:266
  7.1 16.1 %all-to-all-start = ((bf16[8,12,1024]{2,1,0:T(8,128)(2,1)}), bf16[8,12,1024]{2,1,0:T(8,128)(2,1)S(1)}, u32[]{:S(2)}, u32[]{:S(2)}) async-start(bf16[8,12,1024]{2,1,0:T(8,128)(2,1)} %get-tuple-element.28), calls=%async_computation | async-start | bytes 524288 | tf_op jit(solution)/shard_map/all_to_all | solution.py:268
  14.8 3.5 %collective-permute-start.2 = (bf16[288,256]{1,0:T(8,128)(2,1)S(1)}, bf16[288,256]{1,0:T(8,128)(2,1)S(1)}, u32[]{:S(2)}, u32[]{:S(2)}) collective-permute-start(bf16[288,256]{1,0:T(8,128)(2,1)S(1)} %get-tuple-element.26.near_ref), channel_id=1, source_target_pairs={{0,8},{16,24},{8,0},{24,16},{1,9},{17,25},{9,1},{25,17},{2,10},{18... | collective-permute-start | bytes 442376 | tf_op jit(solution)/shard_map/ppermute | solution.py:274
  14.8 3.5 %collective-permute-start.3 = (bf16[288,256]{1,0:T(8,128)(2,1)S(1)}, bf16[288,256]{1,0:T(8,128)(2,1)S(1)}, u32[]{:S(2)}, u32[]{:S(2)}) collective-permute-start(bf16[288,256]{1,0:T(8,128)(2,1)S(1)} %get-tuple-element.27.far_ref), channel_id=1, source_target_pairs={{8,16},{16,8},{9,17},{17,9},{10,18},{18,10},{11,19},{19,11},{12,20... | collective-permute-start | bytes 442376 | tf_op jit(solution)/shard_map/ppermute | solution.py:273
  16.9 0.8 %copy-start.3 = (bf16[96,32,2,2,2]{0,4,3,2,1:T(2,128)(2,1)S(1)}, bf16[96,32,2,2,2]{0,4,3,2,1:T(2,128)(2,1)}, u32[]{:S(2)}) copy-start(bf16[96,32,2,2,2]{0,4,3,2,1:T(2,128)(2,1)} %param.6) | copy-start | bytes 147460
  42.8 10.3 %all-to-all-start.2 = ((bf16[32,16,128]{2,1,0:T(8,128)(2,1)}), bf16[32,16,128]{2,1,0:T(8,128)(2,1)S(1)}, u32[]{:S(2)}, u32[]{:S(2)}) async-start(bf16[32,16,128]{2,1,0:T(8,128)(2,1)} %get-tuple-element.31), calls=%async_computation.2 | async-start | bytes 262144 | tf_op jit(solution)/shard_map/all_to_all | solution.py:310
  45.4 2.0 %collective-permute-start.4 = (bf16[8,24,128]{2,1,0:T(8,128)(2,1)S(1)}, bf16[8,24,128]{2,1,0:T(8,128)(2,1)S(1)}, u32[]{:S(2)}, u32[]{:S(2)}) collective-permute-start(bf16[8,24,128]{2,1,0:T(8,128)(2,1)S(1)} %get-tuple-element.33), channel_id=1, source_target_pairs={{0,8},{8,0},{16,24},{24,16},{1,9},{9,1},{17,25},{25,17},{2,10},{10... | collective-permute-start | bytes 147464 | tf_op jit(solution)/shard_map/ppermute | solution.py:313
  45.5 4.6 %collective-permute-start.5 = (bf16[8,24,128]{2,1,0:T(8,128)(2,1)S(1)}, bf16[8,24,128]{2,1,0:T(8,128)(2,1)S(1)}, u32[]{:S(2)}, u32[]{:S(2)}) collective-permute-start(bf16[8,24,128]{2,1,0:T(8,128)(2,1)S(1)} %get-tuple-element.34), channel_id=1, source_target_pairs={{0,16},{8,24},{16,0},{24,8},{1,17},{9,25},{17,1},{25,9},{2,18},{10... | collective-permute-start | bytes 147464 | tf_op jit(solution)/shard_map/ppermute | solution.py:313
  47.2 4.2 %collective-permute-start.6 = (bf16[8,24,128]{2,1,0:T(8,128)(2,1)S(1)}, bf16[8,24,128]{2,1,0:T(8,128)(2,1)S(1)}, u32[]{:S(2)}, u32[]{:S(2)}) collective-permute-start(bf16[8,24,128]{2,1,0:T(8,128)(2,1)S(1)} %get-tuple-element.35), channel_id=1, source_target_pairs={{0,24},{8,16},{16,8},{24,0},{1,25},{9,17},{17,9},{25,1},{2,26},{10... | collective-permute-start | bytes 147464 | tf_op jit(solution)/shard_map/ppermute | solution.py:313

commit v3 on v2

--- a/solution.py
+++ b/solution.py
@@ -14,13 +14,13 @@
 GRAD_BLOCKS = 9 + 16
 
 
-def call(body, outs, *args, scratch=(), hbm=(), hbm_outs=()):
-    vmem, anywhere = (pl.BlockSpec(memory_space=s) for s in (pltpu.VMEM, pl.ANY))
+def call(body, outs, *args, scratch=()):
+    vmem = pl.BlockSpec(memory_space=pltpu.VMEM)
     return pl.pallas_call(
         body,
         out_shape=outs,
-        in_specs=[anywhere if i in hbm else vmem for i in range(len(args))],
-        out_specs=tuple(anywhere if i in hbm_outs else vmem for i in range(len(outs))),
+        in_specs=[vmem] * len(args),
+        out_specs=(vmem,) * len(outs),
         scratch_shapes=list(scratch),
         compiler_params=pltpu.CompilerParams(vmem_limit_bytes=LIMIT),
     )(*args)
@@ -44,34 +44,57 @@
     return lax.axis_index(axis) % 2 == 0
 
 
-def pack_kernel(v_ref, u_ref, near_ref, far_ref, turned_ref, cot_ref, held, v_sems, u_sems):
+def edge_kernel(v_ref, near_ref, far_ref, turned_ref):
     channels, depth, rows, cols = v_ref.shape
-    bricks, _, cells = cot_ref.shape
-    v_copies = [
-        pltpu.make_async_copy(v_ref.at[:, a], held.at[a], v_sems.at[a]) for a in range(depth)
-    ]
-    u_copies = [
-        pltpu.make_async_copy(
-            u_ref.at[:, pl.ds(b * cells, cells)], cot_ref.at[b], u_sems.at[b]
-        )
-        for b in range(bricks)
-    ]
-    for copy in v_copies + u_copies:
-        copy.start()
     swap = one_hot(
         (channels * rows, channels * rows), lambda r: (r % channels) * rows + r // channels
     )
-    for copy in v_copies:
-        copy.wait()
-    planes = [held[a].reshape(channels * rows, cols) for a in range(depth)]
+    planes = [v_ref[:, a].reshape(channels * rows, cols) for a in range(depth)]
     turned = dot(swap, jnp.concatenate(planes, axis=1)).astype(bf16)
     turned_ref[...] = turned
     first, last = turned[:channels], turned[(rows - 1) * channels :]
     even = is_even("brick")
     near_ref[...] = jnp.where(even, last, first)
     far_ref[...] = jnp.where(even, first, last)
-    for copy in u_copies:
-        copy.wait()
+
+
+def folding(filters):
+    left = filters % 8
+    return filters // 8, left, 8 // left if left and 8 % left == 0 else 1
+
+
+def block_width(filters, cells):
+    groups, left, fold = folding(filters)
+    return groups * cells + (cells // fold if left else 0)
+
+
+def block_kernel(u_ref, out_ref):
+    filters = u_ref.shape[0]
+    bricks = out_ref.shape[0]
+    cells = u_ref.shape[1] // bricks
+    groups, left, fold = folding(filters)
+    part = cells // fold
+    for b in range(bricks):
+        block = u_ref[:, b * cells : (b + 1) * cells].astype(f32)
+        for g in range(groups):
+            rows = block[g * 8 : (g + 1) * 8]
+            out_ref[b, :, g * cells : (g + 1) * cells] = rows.astype(bf16)
+        if left:
+            rest = [block[groups * 8 :, i * part : (i + 1) * part] for i in range(fold)]
+            if left * fold < 8:
+                rest.append(jnp.zeros((8 - left * fold, part), f32))
+            out_ref[b, :, groups * cells :] = jnp.concatenate(rest, axis=0).astype(bf16)
+
+
+def unfold(block, filters, cells):
+    groups, left, fold = folding(filters)
+    part = cells // fold
+    pieces = [block[:, g * cells : (g + 1) * cells] for g in range(groups)]
+    if left:
+        rest = block[:, groups * cells :]
+        rest = [rest[i * left : (i + 1) * left] for i in range(fold)]
+        pieces.append(jnp.concatenate(rest, axis=1))
+    return pieces
 
 
 def face_kernel(turned_ref, near_ref, far_ref, send_near_ref, send_far_ref):
@@ -106,7 +129,8 @@
 ):
     rows, channels, half = d_ref.shape[0] - 2, d_ref.shape[3], d_ref.shape[4]
     cols = 2 * half
-    bricks, own_filters, cells = g_ref.shape
+    bricks = g_ref.shape[0]
+    own_filters, cells = w2t_ref.shape[1] // bricks, x_ref.shape[1]
     slabs = send_ref.shape[0] // bricks
     filters = w2t_ref.shape[1]
     padded = w2p_ref.shape[0] // bricks
@@ -123,7 +147,10 @@
     for j in range(rows // 2):
         window = d_ref[2 * j : 2 * j + 4].reshape(64 * channels, half)
         x_ref[:, j * half : (j + 1) * half] = window
-    gradient = jnp.concatenate([g_ref[b].astype(f32) for b in range(bricks)], axis=0)
+    blocks = []
+    for b in range(bricks):
+        blocks.extend(unfold(g_ref[b].astype(f32), own_filters, cells))
+    gradient = jnp.concatenate(blocks, axis=0)
     gradient = gradient.astype(bf16)
 
     pre = dot(w1_ref[...], x_ref[...])
@@ -244,23 +271,15 @@
     chunks = min(slabs, cells // 128)
 
     edge = jax.ShapeDtypeStruct((channels, 2 * cols), bf16)
-    near, far, turned, cotangent = call(
-        pack_kernel,
-        (
-            edge,
-            edge,
-            jax.ShapeDtypeStruct((rows * channels, 2 * cols), bf16),
-            jax.ShapeDtypeStruct((bricks, own_filters, cells), bf16),
-        ),
+    near, far, turned = call(
+        edge_kernel,
+        (edge, edge, jax.ShapeDtypeStruct((rows * channels, 2 * cols), bf16)),
         volume,
+    )
+    (cotangent,) = call(
+        block_kernel,
+        (jax.ShapeDtypeStruct((bricks, 8, block_width(own_filters, cells)), bf16),),
         upstream.reshape(own_filters, -1),
-        scratch=(
-            pltpu.VMEM((2, channels, rows, cols), bf16),
-            pltpu.SemaphoreType.DMA((2,)),
-            pltpu.SemaphoreType.DMA((bricks,)),
-        ),
-        hbm=(0, 1),
-        hbm_outs=(3,),
     )
     near_pairs, far_pairs = swaps(bricks)
     far = lax.ppermute(far, "brick", far_pairs)

time: 54.4 us -> 53.6 us (0.985)
  local copies, waits for them, and re-layouts: 4.59 us -> 3.66 us
  waiting for transfers between devices: 10.7 us -> 9.96 us
  blocking collectives: 16.1 us -> 16.8 us
    unnamed x15, local copies, waits for them, and re-layouts: 2.8 us -> 1.87 us
    all_to_all x1, waiting for transfers between devices: 4.9 us -> 4.17 us  [per_device(): cotangent = lax.all_to_all(cotangent, 'brick', 0, 0, tiled=True)]
    all_to_all x1, blocking collectives: 16.1 us -> 16.8 us  [per_device(): got = lax.all_to_all(send, ALL, 0, 0, tiled=True)]
    pallas_call x5 -> x6, Pallas kernels: 5.28 us -> 5.4 us  [call(): pl.pallas_call(body, out_shape=outs, in_specs=[vmem] * len(args), out_spe...]
  transfers between devices with their start and end apart: 9 -> 9, of which waited for: 4 -> 4; matrix products, arithmetic and copies ran while one was open for 3% -> 3% of each run, Pallas kernels for 0% -> 1%
where the time goes in v3:
time: 53.6 us; the launch traced here: 53.2 us
  blocking collectives  16.8 us (31%)
  starting transfers between devices  16.5 us (31%)
  waiting for transfers between devices  9.96 us (19%)
  Pallas kernels  5.4 us (10%)
  local copies, waits for them, and re-layouts  3.66 us (7%)
  between operations  0.87 us (2%)
    all_to_all x1, blocking collectives, per_device(): got = lax.all_to_all(send, ALL, 0, 0, tiled=True)  16.8 us
    all_to_all x1, starting transfers between devices, per_device(): cotangent = lax.all_to_all(cotangent, 'brick', 0, 0, tiled=True)  7.59 us
    pallas_call x6, Pallas kernels, call(): pl.pallas_call(body, out_shape=outs, in_specs=[vmem] * len(args), out_spe...  5.4 us
    all_to_all x1, waiting for transfers between devices, per_device(): cotangent = lax.all_to_all(cotangent, 'brick', 0, 0, tiled=True)  4.17 us
    ppermute x3, waiting for transfers between devices, per_device(): pieces[k] = lax.ppermute(pieces[k], 'slab', pairs)  4.06 us
    ppermute x1, starting transfers between devices, per_device(): near = lax.ppermute(near, 'brick', near_pairs)  3.03 us
    all_to_all x1, starting transfers between devices, per_device(): whole = lax.all_to_all(share, ALL, 0, 0, tiled=True)  2.58 us
    ppermute x3, starting transfers between devices, per_device(): pieces[k] = lax.ppermute(pieces[k], 'slab', pairs)  1.96 us
  transfers between devices with their start and end apart: 9, of which 4 were waited for; matrix products, arithmetic and copies ran while one was open for 3% of the time, Pallas kernels for 1%

profile of v3, /device:TPU:0, one launch (start us, length us, event | category | flops | bytes accessed | tf_op | source)
XLA Modules:
  0.0 53.2 jit_solution(13609498584910469541)
XLA Ops:
  0.7 1.0 %copy-done.2 = bf16[16,2,16,256]{3,2,1,0:T(8,128)(2,1)S(1)} copy-done((bf16[16,2,16,256]{3,2,1,0:T(8,128)(2,1)S(1)}, bf16[16,2,16,256]{3,2,1,0:T(8,128)(2,1)}, u32[]{:S(2)}) %copy-start.2) | copy-done | bytes 262168
  1.7 0.2 shard_map.67
  1.9 3.0 %collective-permute-start = (bf16[16,512]{1,0:T(8,128)(2,1)S(1)}, bf16[16,512]{1,0:T(8,128)(2,1)S(1)}, u32[]{:S(2)}, u32[]{:S(2)}) collective-permute-start(bf16[16,512]{1,0:T(8,128)(2,1)S(1)} %get-tuple-element.21), channel_id=1, source_target_pairs={{0,1},{2,3},{4,5},{6,7},{1,0},{3,2},{5,4},{7,6},{8,9},{10,11},{12,... | collective-permute-start | bytes 49160 | tf_op jit(solution)/shard_map/ppermute | solution.py:286
  4.9 0.7 %collective-permute-start.1 = (bf16[16,512]{1,0:T(8,128)(2,1)S(1)}, bf16[16,512]{1,0:T(8,128)(2,1)S(1)}, u32[]{:S(2)}, u32[]{:S(2)}) collective-permute-start(bf16[16,512]{1,0:T(8,128)(2,1)S(1)} %get-tuple-element.22), channel_id=1, source_target_pairs={{1,2},{3,4},{5,6},{2,1},{4,3},{6,5},{9,10},{11,12},{13,14},{10,9},... | collective-permute-start | bytes 49160 | tf_op jit(solution)/shard_map/ppermute | solution.py:285
  5.6 0.7 %shard_map.69 = bf16[8,8,1536]{2,1,0:T(8,128)(2,1)} custom-call(bf16[12,8192]{1,0:T(8,128)(2,1)S(1)} %bitcast.25), custom_call_target="tpu_custom_call" | custom-call | tf_op jit(solution)/shard_map/pallas_call | solution.py:19
  6.3 7.6 %all-to-all-start = ((bf16[8,8,1536]{2,1,0:T(8,128)(2,1)}), bf16[8,8,1536]{2,1,0:T(8,128)(2,1)S(1)}, u32[]{:S(2)}, u32[]{:S(2)}) async-start(bf16[8,8,1536]{2,1,0:T(8,128)(2,1)} %shard_map.69), calls=%async_computation | async-start | bytes 393216 | tf_op jit(solution)/shard_map/all_to_all | solution.py:287
  14.0 0.7 %collective-permute-start.3 = (bf16[288,256]{1,0:T(8,128)(2,1)S(1)}, bf16[288,256]{1,0:T(8,128)(2,1)S(1)}, u32[]{:S(2)}, u32[]{:S(2)}) collective-permute-start(bf16[288,256]{1,0:T(8,128)(2,1)S(1)} %get-tuple-element.26.far_ref), channel_id=1, source_target_pairs={{8,16},{16,8},{9,17},{17,9},{10,18},{18,10},{11,19},{19,11},{12,20... | collective-permute-start | bytes 442376 | tf_op jit(solution)/shard_map/ppermute | solution.py:292
  14.7 0.5 fusion
  15.4 0.1 copy.26
  15.6 0.1 copy.27
  16.2 0.8 %copy-done.3 = bf16[96,32,2,2,2]{0,4,3,2,1:T(2,128)(2,1)S(1)} copy-done((bf16[96,32,2,2,2]{0,4,3,2,1:T(2,128)(2,1)S(1)}, bf16[96,32,2,2,2]{0,4,3,2,1:T(2,128)(2,1)}, u32[]{:S(2)}) %copy-start.3) | copy-done | bytes 49176
  17.0 0.2 copy.32
  17.3 0.2 reshape_reshape.3
  17.5 4.2 %all-to-all-done.g_ref = bf16[8,8,1536]{2,1,0:T(8,128)(2,1)S(1)} async-done(((bf16[8,8,1536]{2,1,0:T(8,128)(2,1)}), bf16[8,8,1536]{2,1,0:T(8,128)(2,1)S(1)}, u32[]{:S(2)}, u32[]{:S(2)}) %all-to-all-start) | async-done | bytes 196640 | tf_op jit(solution)/shard_map/all_to_all | solution.py:287
  21.7 2.8 %shard_map.70 = bf16[32,40,128]{2,1,0:T(8,128)(2,1)S(1)} custom-call(bf16[288,256]{1,0:T(8,128)(2,1)S(1)} %collective-permute-done.2.got_near_ref, bf16[288,256]{1,0:T(8,128)(2,1)S(1)} %get-tuple-element.25.near_ref, bf16[288,256]{1,0:T(8,128)(2,1)S(1)} %get-tuple-element.26.far_ref, bf16[288,256]{1,0:T(8,128)(2,1)S(1)} %collective-permute-done.3.got_far_ref, ...), custom_call_target="tpu_custom_call" | custom-call | tf_op jit(solution)/shard_map/pallas_call | solution.py:19
  24.5 16.8 %all_to_all.15.got_ref = bf16[32,40,128]{2,1,0:T(8,128)(2,1)S(1)} all-to-all(bf16[32,40,128]{2,1,0:T(8,128)(2,1)S(1)} %shard_map.70), channel_id=1, replica_groups=mesh['slab'=4,'brick'=8] {'slab','brick'}, dimensions={0} | all-to-all | bytes 655360 | tf_op jit(solution)/shard_map/all_to_all | solution.py:322
  41.3 0.7 %shard_map.71 = (bf16[32,16,128]{2,1,0:T(8,128)(2,1)}, bf16[8,24,128]{2,1,0:T(8,128)(2,1)S(1)}, bf16[8,24,128]{2,1,0:T(8,128)(2,1)S(1)}, bf16[8,24,128]{2,1,0:T(8,128)(2,1)S(1)}, bf16[8,24,128]{2,1,0:T(8,128)(2,1)S(1)}) custom-call(bf16[32,40,128]{2,1,0:T(8,128)(2,1)S(1)} %all_to_all.15.got_ref), custom_call_target="tpu_custom_call" | custom-call | tf_op jit(solution)/shard_map/pallas_call | solution.py:19
  42.0 2.6 %all-to-all-start.2 = ((bf16[32,16,128]{2,1,0:T(8,128)(2,1)}), bf16[32,16,128]{2,1,0:T(8,128)(2,1)S(1)}, u32[]{:S(2)}, u32[]{:S(2)}) async-start(bf16[32,16,128]{2,1,0:T(8,128)(2,1)} %get-tuple-element.29), calls=%async_computation.2 | async-start | bytes 262144 | tf_op jit(solution)/shard_map/all_to_all | solution.py:329
  44.6 0.2 collective-permute-start.4
  44.7 1.7 %collective-permute-start.5 = (bf16[8,24,128]{2,1,0:T(8,128)(2,1)S(1)}, bf16[8,24,128]{2,1,0:T(8,128)(2,1)S(1)}, u32[]{:S(2)}, u32[]{:S(2)}) collective-permute-start(bf16[8,24,128]{2,1,0:T(8,128)(2,1)S(1)} %get-tuple-element.32), channel_id=1, source_target_pairs={{0,16},{8,24},{16,0},{24,8},{1,17},{9,25},{17,1},{25,9},{2,18},{10... | collective-permute-start | bytes 147464 | tf_op jit(solution)/shard_map/ppermute | solution.py:332
  46.5 2.8 %collective-permute-done.5.refs_2_ = bf16[8,24,128]{2,1,0:T(8,128)(2,1)S(1)} collective-permute-done((bf16[8,24,128]{2,1,0:T(8,128)(2,1)S(1)}, bf16[8,24,128]{2,1,0:T(8,128)(2,1)S(1)}, u32[]{:S(2)}, u32[]{:S(2)}) %collective-permute-start.5) | collective-permute-done | bytes 49184 | tf_op jit(solution)/shard_map/ppermute | solution.py:332
  49.3 1.2 %collective-permute-done.6.refs_3_ = bf16[8,24,128]{2,1,0:T(8,128)(2,1)S(1)} collective-permute-done((bf16[8,24,128]{2,1,0:T(8,128)(2,1)S(1)}, bf16[8,24,128]{2,1,0:T(8,128)(2,1)S(1)}, u32[]{:S(2)}, u32[]{:S(2)}) %collective-permute-start.6) | collective-permute-done | bytes 49184 | tf_op jit(solution)/shard_map/ppermute | solution.py:332
  50.6 1.7 %all-to-all-done.2.whole_ref = bf16[32,16,128]{2,1,0:T(8,128)(2,1)S(1)} async-done(((bf16[32,16,128]{2,1,0:T(8,128)(2,1)}), bf16[32,16,128]{2,1,0:T(8,128)(2,1)S(1)}, u32[]{:S(2)}, u32[]{:S(2)}) %all-to-all-start.2) | async-done | bytes 131104 | tf_op jit(solution)/shard_map/all_to_all | solution.py:329
  52.3 0.9 %shard_map.72 = (bf16[12,8192]{1,0:T(8,128)(2,1)}, f32[3,3,3,16,32]{4,3,2,1,0:T(8,128)}, f32[256,96]{1,0:T(8,128)}) custom-call(bf16[32,16,128]{2,1,0:T(8,128)(2,1)S(1)} %all-to-all-done.2.whole_ref, bf16[8,24,128]{2,1,0:T(8,128)(2,1)S(1)} %get-tuple-element.30.refs_0_, bf16[8,24,128]{2,1,0:T(8,128)(2,1)S(1)} %collective-permute-done.4.refs_1_, ...), custom_call_target="tpu_custom_call" | custom-call | tf_op jit(solution)/shard_map/pallas_call | solution.py:19
  (30 shorter events, 1.0 us)
Async XLA Ops:
  0.6 14.1 %copy-start = (bf16[32,16,3,3,3]{0,1,4,3,2:T(8,128)(2,1)S(1)}, bf16[32,16,3,3,3]{0,1,4,3,2:T(8,128)(2,1)}, u32[]{:S(2)}) copy-start(bf16[32,16,3,3,3]{0,1,4,3,2:T(8,128)(2,1)} %param.5) | copy-start | bytes 82948
  0.6 4.9 %copy-start.1 = (bf16[12,1,8192]{2,0,1:T(8,128)(2,1)S(1)}, bf16[12,1,8192]{2,0,1:T(8,128)(2,1)}, u32[]{:S(2)}) copy-start(bf16[12,1,8192]{2,0,1:T(8,128)(2,1)} %param.7) | copy-start | bytes 589828
  0.7 1.0 %copy-start.2 = (bf16[16,2,16,256]{3,2,1,0:T(8,128)(2,1)S(1)}, bf16[16,2,16,256]{3,2,1,0:T(8,128)(2,1)}, u32[]{:S(2)}) copy-start(bf16[16,2,16,256]{3,2,1,0:T(8,128)(2,1)} %v_ref.1) | copy-start | bytes 786436
  1.9 12.0 %collective-permute-start = (bf16[16,512]{1,0:T(8,128)(2,1)S(1)}, bf16[16,512]{1,0:T(8,128)(2,1)S(1)}, u32[]{:S(2)}, u32[]{:S(2)}) collective-permute-start(bf16[16,512]{1,0:T(8,128)(2,1)S(1)} %get-tuple-element.21), channel_id=1, source_target_pairs={{0,1},{2,3},{4,5},{6,7},{1,0},{3,2},{5,4},{7,6},{8,9},{10,11},{12,... | collective-permute-start | bytes 49160 | tf_op jit(solution)/shard_map/ppermute | solution.py:286
  4.9 9.0 %collective-permute-start.1 = (bf16[16,512]{1,0:T(8,128)(2,1)S(1)}, bf16[16,512]{1,0:T(8,128)(2,1)S(1)}, u32[]{:S(2)}, u32[]{:S(2)}) collective-permute-start(bf16[16,512]{1,0:T(8,128)(2,1)S(1)} %get-tuple-element.22), channel_id=1, source_target_pairs={{1,2},{3,4},{5,6},{2,1},{4,3},{6,5},{9,10},{11,12},{13,14},{10,9},... | collective-permute-start | bytes 49160 | tf_op jit(solution)/shard_map/ppermute | solution.py:285
  6.3 15.4 %all-to-all-start = ((bf16[8,8,1536]{2,1,0:T(8,128)(2,1)}), bf16[8,8,1536]{2,1,0:T(8,128)(2,1)S(1)}, u32[]{:S(2)}, u32[]{:S(2)}) async-start(bf16[8,8,1536]{2,1,0:T(8,128)(2,1)} %shard_map.69), calls=%async_computation | async-start | bytes 393216 | tf_op jit(solution)/shard_map/all_to_all | solution.py:287
  13.9 3.5 %collective-permute-start.2 = (bf16[288,256]{1,0:T(8,128)(2,1)S(1)}, bf16[288,256]{1,0:T(8,128)(2,1)S(1)}, u32[]{:S(2)}, u32[]{:S(2)}) collective-permute-start(bf16[288,256]{1,0:T(8,128)(2,1)S(1)} %get-tuple-element.25.near_ref), channel_id=1, source_target_pairs={{0,8},{16,24},{8,0},{24,16},{1,9},{17,25},{9,1},{25,17},{2,10},{18... | collective-permute-start | bytes 442376 | tf_op jit(solution)/shard_map/ppermute | solution.py:293
  14.0 3.5 %collective-permute-start.3 = (bf16[288,256]{1,0:T(8,128)(2,1)S(1)}, bf16[288,256]{1,0:T(8,128)(2,1)S(1)}, u32[]{:S(2)}, u32[]{:S(2)}) collective-permute-start(bf16[288,256]{1,0:T(8,128)(2,1)S(1)} %get-tuple-element.26.far_ref), channel_id=1, source_target_pairs={{8,16},{16,8},{9,17},{17,9},{10,18},{18,10},{11,19},{19,11},{12,20... | collective-permute-start | bytes 442376 | tf_op jit(solution)/shard_map/ppermute | solution.py:292
  16.1 0.8 %copy-start.3 = (bf16[96,32,2,2,2]{0,4,3,2,1:T(2,128)(2,1)S(1)}, bf16[96,32,2,2,2]{0,4,3,2,1:T(2,128)(2,1)}, u32[]{:S(2)}) copy-start(bf16[96,32,2,2,2]{0,4,3,2,1:T(2,128)(2,1)} %param.6) | copy-start | bytes 147460
  42.0 10.3 %all-to-all-start.2 = ((bf16[32,16,128]{2,1,0:T(8,128)(2,1)}), bf16[32,16,128]{2,1,0:T(8,128)(2,1)S(1)}, u32[]{:S(2)}, u32[]{:S(2)}) async-start(bf16[32,16,128]{2,1,0:T(8,128)(2,1)} %get-tuple-element.29), calls=%async_computation.2 | async-start | bytes 262144 | tf_op jit(solution)/shard_map/all_to_all | solution.py:329
  44.6 2.0 %collective-permute-start.4 = (bf16[8,24,128]{2,1,0:T(8,128)(2,1)S(1)}, bf16[8,24,128]{2,1,0:T(8,128)(2,1)S(1)}, u32[]{:S(2)}, u32[]{:S(2)}) collective-permute-start(bf16[8,24,128]{2,1,0:T(8,128)(2,1)S(1)} %get-tuple-element.31), channel_id=1, source_target_pairs={{0,8},{8,0},{16,24},{24,16},{1,9},{9,1},{17,25},{25,17},{2,10},{10... | collective-permute-start | bytes 147464 | tf_op jit(solution)/shard_map/ppermute | solution.py:332
  44.7 4.6 %collective-permute-start.5 = (bf16[8,24,128]{2,1,0:T(8,128)(2,1)S(1)}, bf16[8,24,128]{2,1,0:T(8,128)(2,1)S(1)}, u32[]{:S(2)}, u32[]{:S(2)}) collective-permute-start(bf16[8,24,128]{2,1,0:T(8,128)(2,1)S(1)} %get-tuple-element.32), channel_id=1, source_target_pairs={{0,16},{8,24},{16,0},{24,8},{1,17},{9,25},{17,1},{25,9},{2,18},{10... | collective-permute-start | bytes 147464 | tf_op jit(solution)/shard_map/ppermute | solution.py:332
  46.4 4.2 %collective-permute-start.6 = (bf16[8,24,128]{2,1,0:T(8,128)(2,1)S(1)}, bf16[8,24,128]{2,1,0:T(8,128)(2,1)S(1)}, u32[]{:S(2)}, u32[]{:S(2)}) collective-permute-start(bf16[8,24,128]{2,1,0:T(8,128)(2,1)S(1)} %get-tuple-element.33), channel_id=1, source_target_pairs={{0,24},{8,16},{16,8},{24,0},{1,25},{9,17},{17,9},{25,1},{2,26},{10... | collective-permute-start | bytes 147464 | tf_op jit(solution)/shard_map/ppermute | solution.py:332

commit v4 on v3

--- a/solution.py
+++ b/solution.py
@@ -11,10 +11,11 @@
 f32 = jnp.float32
 ALL = ("slab", "brick")
 LIMIT = 40 * 1024 * 1024
+BESIDE = 6_000_000_000
 GRAD_BLOCKS = 9 + 16
 
 
-def call(body, outs, *args, scratch=()):
+def call(body, outs, *args, scratch=(), flops=0):
     vmem = pl.BlockSpec(memory_space=pltpu.VMEM)
     return pl.pallas_call(
         body,
@@ -23,6 +24,9 @@
         out_specs=(vmem,) * len(outs),
         scratch_shapes=list(scratch),
         compiler_params=pltpu.CompilerParams(vmem_limit_bytes=LIMIT),
+        cost_estimate=pl.CostEstimate(flops=flops, bytes_accessed=0, transcendentals=0)
+        if flops
+        else None,
     )(*args)
 
 
@@ -113,65 +117,123 @@
             out_ref[rows] = jnp.where(upper, block[:, cols:], block[:, :cols])
 
 
+def weights_kernel(own_filters, one_ref, two_ref, early_ref, late_ref, w2p_ref, w2t_ref, tall_ref):
+    channels, mid = one_ref.shape[0] // 27, one_ref.shape[1]
+    size = 8 * mid
+    spread = one_hot((mid, 4 * mid), lambda r: r)
+    for g in range(1, 4):
+        spread = spread + one_hot((mid, 4 * mid), lambda r, g=g: r + g * mid)
+    wide = dot(one_ref[...], spread)
+    group = lax.broadcasted_iota(jnp.int32, (channels, 4 * mid), 1) // mid
+    even = is_even("slab")
+    for a in range(4):
+        first = jnp.where(even, 3 - a, a) * (16 * channels)
+        for b in range(4):
+            for e in range(4):
+                rows = pl.ds(pl.multiple_of(first + (b * 4 + e) * channels, 16), channels)
+                for r in range(2):
+                    tile = jnp.zeros((channels, 4 * mid), f32)
+                    for p in range(2):
+                        for q in range(2):
+                            z, y, x = a - p, b - q, e - r
+                            if 0 <= z < 3 and 0 <= y < 3 and 0 <= x < 3:
+                                at = ((z * 3 + y) * 3 + x) * channels
+                                piece = wide[at : at + channels]
+                                tile = jnp.where(group == p * 2 + q, piece, tile)
+                    tall_ref[rows, r * 4 * mid : (r + 1) * 4 * mid] = tile.astype(bf16)
+    placed = dot_nt(one_hot((size, size), lambda s: s), tall_ref[...]).astype(bf16)
+    early_ref[...] = placed[:, : 48 * channels]
+    late_ref[...] = placed[:, 48 * channels :]
+    order = one_hot(
+        (size, size), lambda s: (s % mid) * 8 + ((s // mid) % 4) * 2 + s // (4 * mid)
+    )
+    turned = dot(order, two_ref[...]).astype(bf16)
+    w2t_ref[...] = turned
+    padded = -(-own_filters // 16) * 16
+    expand = one_hot(
+        (w2p_ref.shape[0], two_ref.shape[1]),
+        lambda s: jnp.where(
+            s % padded < own_filters, (s // padded) * own_filters + s % padded, -1
+        ),
+    )
+    w2p_ref[...] = dot_nt(expand, turned).astype(bf16)
+
+
+def widen(plane, channels):
+    cols = plane.shape[1]
+    half = cols // 2
+    at = lax.broadcasted_iota(jnp.int32, (cols, 4 * half), 0)
+    lane = lax.broadcasted_iota(jnp.int32, (cols, 4 * half), 1)
+    spread = jnp.where(at == 2 * (lane % half) + lane // half - 1, 1.0, 0.0).astype(bf16)
+    wide = dot(plane, spread).astype(bf16)
+    pieces = [wide[:, e * half : (e + 1) * half].reshape(-1, channels, half) for e in range(4)]
+    return jnp.concatenate(pieces, axis=1)
+
+
+def fill_patches(x_ref, wide_ref):
+    planes, _, size, half = wide_ref.shape
+    for i in range(planes):
+        for j in range(x_ref.shape[1] // half):
+            for b in range(4):
+                row = (i * 4 + b) * size
+                x_ref[row : row + size, j * half : (j + 1) * half] = wide_ref[i, 2 * j + b]
+
+
+def early_kernel(got_ref, near_ref, far_ref, w1_ref, wide_ref, part_ref, x_ref):
+    channels = wide_ref.shape[2] // 4
+    for i, plane_ref in enumerate((got_ref, near_ref, far_ref)):
+        wide_ref[i] = widen(plane_ref[...], channels)
+    fill_patches(x_ref, wide_ref)
+    part_ref[...] = dot(w1_ref[...], x_ref[...])
+
+
 def main_kernel(
     chunks,
-    got_near_ref,
-    near_ref,
-    far_ref,
-    got_far_ref,
+    own_filters,
+    got_ref,
+    wide_ref,
+    part_ref,
     g_ref,
     w1_ref,
     w2p_ref,
     w2t_ref,
     send_ref,
-    d_ref,
+    far_wide_ref,
+    far_ref,
     x_ref,
+    sums_ref,
 ):
-    rows, channels, half = d_ref.shape[0] - 2, d_ref.shape[3], d_ref.shape[4]
-    cols = 2 * half
-    bricks = g_ref.shape[0]
-    own_filters, cells = w2t_ref.shape[1] // bricks, x_ref.shape[1]
-    slabs = send_ref.shape[0] // bricks
-    filters = w2t_ref.shape[1]
+    filters, cells = w2t_ref.shape[1], x_ref.shape[1]
+    channels = far_ref.shape[0] // 16
+    bricks = filters // own_filters
     padded = w2p_ref.shape[0] // bricks
-    at = lax.broadcasted_iota(jnp.int32, (cols, 4 * half), 0)
-    lane = lax.broadcasted_iota(jnp.int32, (cols, 4 * half), 1)
-    spread = jnp.where(at == 2 * (lane % half) + lane // half - 1, 1.0, 0.0).astype(bf16)
-    even = is_even("slab")
-    for i, plane_ref in enumerate((got_near_ref, near_ref, far_ref, got_far_ref)):
-        a = jnp.where(even, 3 - i, i)
-        inner = dot(plane_ref[...], spread).astype(bf16)
-        for e in range(4):
-            piece = slice(e * half, (e + 1) * half)
-            d_ref[:, a, e] = inner[:, piece].reshape(rows + 2, channels, half)
-    for j in range(rows // 2):
-        window = d_ref[2 * j : 2 * j + 4].reshape(64 * channels, half)
-        x_ref[:, j * half : (j + 1) * half] = window
+    slots = send_ref.shape[0]
+    far_wide_ref[0] = widen(got_ref[...], channels)
+    fill_patches(far_ref, far_wide_ref)
+    fill_patches(x_ref, wide_ref)
     blocks = []
     for b in range(bricks):
         blocks.extend(unfold(g_ref[b].astype(f32), own_filters, cells))
-    gradient = jnp.concatenate(blocks, axis=0)
-    gradient = gradient.astype(bf16)
-
-    pre = dot(w1_ref[...], x_ref[...])
+    gradient = jnp.concatenate(blocks, axis=0).astype(bf16)
+    pre = part_ref[...] + dot(w1_ref[...], far_ref[...])
     sigma = jax.nn.sigmoid(pre)
     hidden = (pre * sigma).astype(bf16)
+    back = dot(w2t_ref[...], gradient)
+    delta = (back * sigma * (1.0 + pre * (1.0 - sigma))).astype(bf16)
     result = dot(w2p_ref[...], hidden)
     width = cells // chunks
     used = own_filters * (width // 128)
-    for t in range(slabs):
-        for b in range(bricks):
-            pieces = [
-                result[b * padded : b * padded + own_filters, at : at + 128]
-                for at in range(t * width, (t + 1) * width, 128)
-                if t < chunks
-            ]
-            filler = send_ref.shape[1] - 16 - (used if pieces else 0)
-            if filler:
-                pieces.append(jnp.zeros((filler, 128), f32))
-            send_ref[t * bricks + b, 16:] = jnp.concatenate(pieces, axis=0).astype(bf16)
-    back = dot(w2t_ref[...], gradient)
-    delta = (back * sigma * (1.0 + pre * (1.0 - sigma))).astype(bf16)
+    for place in range(slots):
+        t, b = place // bricks, place % bricks
+        pieces = [
+            result[b * padded : b * padded + own_filters, at : at + 128]
+            for at in range(t * width, (t + 1) * width, 128)
+            if t < chunks
+        ]
+        filler = send_ref.shape[1] - 16 - (used if pieces else 0)
+        if filler:
+            pieces.append(jnp.zeros((filler, 128), f32))
+        send_ref[place, 16:] = jnp.concatenate(pieces, axis=0).astype(bf16)
     mid = hidden.shape[0] // 8
     natural = one_hot(
         (8 * mid, 8 * mid),
@@ -179,24 +241,28 @@
     )
     ordered = dot(natural, hidden).astype(bf16)
     grad_two = dot_nt(ordered, gradient)
-    moments = dot_nt(x_ref[...], delta).reshape(4, 4, 4, channels, 8 * mid)
-    by_r = moments[:, :, 0:3, :, : 4 * mid] + moments[:, :, 1:4, :, 4 * mid :]
+    for at, patches_ref in ((0, x_ref), (3, far_ref)):
+        moments = dot_nt(patches_ref[...], delta).reshape(-1, 4, 4, channels, 8 * mid)
+        by_r = moments[:, :, 0:3, :, : 4 * mid] + moments[:, :, 1:4, :, 4 * mid :]
+        sums_ref[at : at + by_r.shape[0]] = by_r.reshape(-1, 4, 3 * channels, 4 * mid)
     group = lax.broadcasted_iota(jnp.int32, (9 * channels, 4 * mid), 1) // mid
     total = jnp.zeros((9 * channels, 4 * mid), f32)
+    even = is_even("slab")
     for shift in range(-3, 3):
         moved = jnp.zeros((9 * channels, 4 * mid), f32)
         for a in range(3):
             source = a - shift
             if 0 <= source < 4:
                 p, q = source // 2, source % 2
-                piece = by_r[q : q + 3, a + p].reshape(9 * channels, 4 * mid)
+                plane = jnp.where(even, 3 - a - p, a + p)
+                piece = sums_ref[plane, q : q + 3].reshape(9 * channels, 4 * mid)
                 moved = jnp.where(group == source, piece, moved)
         amount = (shift * mid) % (4 * mid)
         total = total + (pltpu.roll(moved, amount, 1) if amount else moved)
     send_ref[0:9, :16] = total.astype(bf16).reshape(9, channels, 4 * mid)
     send_ref[9:25, :16, :filters] = grad_two.astype(bf16).reshape(16, -1, filters)
     send_ref[9:25, :16, filters:] = jnp.zeros((16, 16, 128 - filters), bf16)
-    send_ref[25:, :16] = jnp.zeros((slabs * bricks - 25, 16, 128), bf16)
+    send_ref[25:, :16] = jnp.zeros((slots - 25, 16, 128), bf16)
 
 
 def sum_kernel(got_ref, share_ref, *piece_refs):
@@ -247,18 +313,6 @@
     return [pairs + [(j, i) for i, j in pairs] for pairs in (near, far)]
 
 
-def place_kernel(kernel_one):
-    base = jnp.transpose(kernel_one, (0, 3, 2, 4, 1))
-    out = base.shape[0]
-    pieces = []
-    for r in (0, 1):
-        for p in (0, 1):
-            for q in (0, 1):
-                pads = ((0, 0), (q, 1 - q), (p, 1 - p), (r, 1 - r), (0, 0))
-                pieces.append(jnp.pad(base, pads).reshape(out, -1))
-    return jnp.concatenate(pieces, axis=0)
-
-
 def per_device(volume, kernel_one, kernel_two, upstream):
     channels, _, rows, cols = volume.shape
     bricks, slabs = lax.axis_size("brick"), lax.axis_size("slab")
@@ -276,6 +330,7 @@
         (edge, edge, jax.ShapeDtypeStruct((rows * channels, 2 * cols), bf16)),
         volume,
     )
+    near, far, turned, upstream = lax.optimization_barrier((near, far, turned, upstream))
     (cotangent,) = call(
         block_kernel,
         (jax.ShapeDtypeStruct((bricks, 8, block_width(own_filters, cells)), bf16),),
@@ -295,28 +350,50 @@
     near, far, kernel_one, kernel_two = lax.optimization_barrier(
         (near, far, kernel_one, kernel_two)
     )
-    weights_one = place_kernel(kernel_one)
-    weights_two = jnp.transpose(kernel_two, (0, 4, 2, 3, 1)).reshape(filters, 8 * mid)
-    grouped = weights_two.reshape(bricks, own_filters, 8 * mid)
-    grouped = jnp.pad(grouped, ((0, 0), (0, padded - own_filters), (0, 0)))
-    grouped = grouped.reshape(bricks * padded, 8 * mid)
-
+    w1_early, w1_late, w2p, w2t = call(
+        functools.partial(weights_kernel, own_filters),
+        (
+            jax.ShapeDtypeStruct((8 * mid, 48 * channels), bf16),
+            jax.ShapeDtypeStruct((8 * mid, 16 * channels), bf16),
+            jax.ShapeDtypeStruct((bricks * padded, 8 * mid), bf16),
+            jax.ShapeDtypeStruct((8 * mid, filters), bf16),
+        ),
+        jnp.transpose(kernel_one, (2, 3, 4, 1, 0)).reshape(27 * channels, mid),
+        jnp.transpose(kernel_two, (1, 2, 3, 4, 0)).reshape(8 * mid, filters),
+        scratch=(pltpu.VMEM((64 * channels, 8 * mid), bf16),),
+        flops=BESIDE,
+    )
+    tall, half = rows + 2, cols // 2
+    wide, part = call(
+        early_kernel,
+        (
+            jax.ShapeDtypeStruct((3, tall, 4 * channels, half), bf16),
+            jax.ShapeDtypeStruct((8 * mid, cells), f32),
+        ),
+        got_near,
+        near,
+        far,
+        w1_early,
+        scratch=(pltpu.VMEM((48 * channels, cells), bf16),),
+        flops=BESIDE,
+    )
     width = cells // chunks
     chunk_rows = -(-own_filters * width // 128 // 8) * 8
     (send,) = call(
-        functools.partial(main_kernel, chunks),
+        functools.partial(main_kernel, chunks, own_filters),
         (jax.ShapeDtypeStruct((devices, 16 + chunk_rows, 128), bf16),),
-        got_near,
-        near,
-        far,
         got_far,
+        wide,
+        part,
         cotangent,
-        weights_one,
-        grouped,
-        weights_two.T,
+        w1_late,
+        w2p,
+        w2t,
         scratch=(
-            pltpu.VMEM((rows + 2, 4, 4, channels, cols // 2), bf16),
-            pltpu.VMEM((64 * channels, cells), bf16),
+            pltpu.VMEM((1, tall, 4 * channels, half), bf16),
+            pltpu.VMEM((16 * channels, cells), bf16),
+            pltpu.VMEM((48 * channels, cells), bf16),
+            pltpu.VMEM((4, 4, 3 * channels, 4 * mid), f32),
         ),
     )
     got = lax.all_to_all(send, ALL, 0, 0, tiled=True)

time: 53.6 us -> 52.8 us (0.985)
  local copies, waits for them, and re-layouts: 3.66 us -> 1.05 us
  Pallas kernels: 5.4 us -> 6.35 us
  waiting for transfers between devices: 9.96 us -> 10.9 us
    reshape x8 -> x0, local copies, waits for them, and re-layouts: 0.99 us -> none  [place_kernel(): pieces.append(jnp.pad(base, pads).reshape(out, -1))]
    all_to_all x1, waiting for transfers between devices: 4.17 us -> 5.13 us  [per_device(): cotangent = lax.all_to_all(cotangent, 'brick', 0, 0, tiled=True)]
    pallas_call x6 -> x8, Pallas kernels: 5.4 us -> 6.35 us  [call(): pl.pallas_call(body, out_shape=outs, in_specs=[vmem] * len(args), out_spe...]
    unnamed x15 -> x8, local copies, waits for them, and re-layouts: 1.87 us -> 1.05 us
  transfers between devices with their start and end apart: 9 -> 9, of which waited for: 4 -> 4; matrix products, arithmetic and copies ran while one was open for 3% -> 0% of each run, Pallas kernels for 1% -> 5%
where the time goes in v4:
time: 52.8 us; the launch traced here: 52.4 us
  blocking collectives  16.8 us (32%)
  starting transfers between devices  16.5 us (31%)
  waiting for transfers between devices  10.9 us (21%)
  Pallas kernels  6.35 us (12%)
  local copies, waits for them, and re-layouts  1.05 us (2%)
  between operations  0.77 us (1%)
    all_to_all x1, blocking collectives, per_device(): got = lax.all_to_all(send, ALL, 0, 0, tiled=True)  16.8 us
    all_to_all x1, starting transfers between devices, per_device(): cotangent = lax.all_to_all(cotangent, 'brick', 0, 0, tiled=True)  7.59 us
    pallas_call x8, Pallas kernels, call(): pl.pallas_call(body, out_shape=outs, in_specs=[vmem] * len(args), out_spe...  6.35 us
    all_to_all x1, waiting for transfers between devices, per_device(): cotangent = lax.all_to_all(cotangent, 'brick', 0, 0, tiled=True)  5.13 us
    ppermute x3, waiting for transfers between devices, per_device(): pieces[k] = lax.ppermute(pieces[k], 'slab', pairs)  4.06 us
    ppermute x1, starting transfers between devices, per_device(): near = lax.ppermute(near, 'brick', near_pairs)  3.03 us
    all_to_all x1, starting transfers between devices, per_device(): whole = lax.all_to_all(share, ALL, 0, 0, tiled=True)  2.58 us
    ppermute x3, starting transfers between devices, per_device(): pieces[k] = lax.ppermute(pieces[k], 'slab', pairs)  1.96 us
  transfers between devices with their start and end apart: 9, of which 4 were waited for; matrix products, arithmetic and copies ran while one was open for 0% of the time, Pallas kernels for 5%

profile of v4, /device:TPU:0, one launch (start us, length us, event | category | flops | bytes accessed | tf_op | source)
XLA Modules:
  0.0 52.4 jit_solution(17462729070208416399)
XLA Ops:
  0.6 1.0 %copy-done.1 = bf16[16,2,16,256]{3,2,1,0:T(8,128)(2,1)S(1)} copy-done((bf16[16,2,16,256]{3,2,1,0:T(8,128)(2,1)S(1)}, bf16[16,2,16,256]{3,2,1,0:T(8,128)(2,1)}, u32[]{:S(2)}) %copy-start.1) | copy-done | bytes 262168
  1.6 0.2 shard_map.67
  1.9 3.0 %collective-permute-start = (bf16[16,512]{1,0:T(8,128)(2,1)S(1)}, bf16[16,512]{1,0:T(8,128)(2,1)S(1)}, u32[]{:S(2)}, u32[]{:S(2)}) collective-permute-start(bf16[16,512]{1,0:T(8,128)(2,1)S(1)} %get-tuple-element.34), channel_id=1, source_target_pairs={{0,1},{2,3},{4,5},{6,7},{1,0},{3,2},{5,4},{7,6},{8,9},{10,11},{12,... | collective-permute-start | bytes 49160 | tf_op jit(solution)/shard_map/ppermute | solution.py:341
  4.9 0.7 %collective-permute-start.1 = (bf16[16,512]{1,0:T(8,128)(2,1)S(1)}, bf16[16,512]{1,0:T(8,128)(2,1)S(1)}, u32[]{:S(2)}, u32[]{:S(2)}) collective-permute-start(bf16[16,512]{1,0:T(8,128)(2,1)S(1)} %get-tuple-element.35), channel_id=1, source_target_pairs={{1,2},{3,4},{5,6},{2,1},{4,3},{6,5},{9,10},{11,12},{13,14},{10,9},... | collective-permute-start | bytes 49160 | tf_op jit(solution)/shard_map/ppermute | solution.py:340
  5.6 0.7 %shard_map.71 = bf16[8,8,1536]{2,1,0:T(8,128)(2,1)} custom-call(bf16[12,8192]{1,0:T(8,128)(2,1)S(1)} %bitcast.12), custom_call_target="tpu_custom_call" | custom-call | tf_op jit(solution)/shard_map/pallas_call | solution.py:20
  6.3 7.6 %all-to-all-start = ((bf16[8,8,1536]{2,1,0:T(8,128)(2,1)}), bf16[8,8,1536]{2,1,0:T(8,128)(2,1)S(1)}, u32[]{:S(2)}, u32[]{:S(2)}) async-start(bf16[8,8,1536]{2,1,0:T(8,128)(2,1)} %shard_map.71), calls=%async_computation | async-start | bytes 393216 | tf_op jit(solution)/shard_map/all_to_all | solution.py:342
  13.9 0.0 copy-start.3
  13.9 0.1 collective-permute-start.3
  14.0 0.7 %collective-permute-start.2 = (bf16[288,256]{1,0:T(8,128)(2,1)S(1)}, bf16[288,256]{1,0:T(8,128)(2,1)S(1)}, u32[]{:S(2)}, u32[]{:S(2)}) collective-permute-start(bf16[288,256]{1,0:T(8,128)(2,1)S(1)} %get-tuple-element.39.far_ref), channel_id=1, source_target_pairs={{8,16},{16,8},{9,17},{17,9},{10,18},{18,10},{11,19},{19,11},{12,20... | collective-permute-start | bytes 442376 | tf_op jit(solution)/shard_map/ppermute | solution.py:347
  14.7 0.1 copy-done.2
  14.8 0.8 %shard_map.69 = (bf16[256,768]{1,0:T(8,128)(2,1)S(1)}, bf16[256,256]{1,0:T(8,128)(2,1)S(1)}, bf16[128,256]{1,0:T(8,128)(2,1)S(1)}, bf16[256,96]{1,0:T(8,128)(2,1)S(1)}) custom-call(bf16[432,32]{1,0:T(8,128)(2,1)S(1)} %bitcast.13, bf16[256,96]{1,0:T(8,128)(2,1)S(1)} %bitcast.14), custom_call_target="tpu_custom_call" | custom-call | flops 6000000000 | tf_op jit(solution)/shard_map/pallas_call | solution.py:20
  15.5 1.0 %shard_map.70 = (bf16[3,18,64,128]{3,2,1,0:T(8,128)(2,1)S(1)}, f32[256,1024]{1,0:T(8,128)S(1)}) custom-call(bf16[288,256]{1,0:T(8,128)(2,1)S(1)} %collective-permute-done.3.got_ref, bf16[288,256]{1,0:T(8,128)(2,1)S(1)} %get-tuple-element.38.near_ref, bf16[288,256]{1,0:T(8,128)(2,1)S(1)} %get-tuple-element.39.far_ref, ...), custom_call_target="tpu_custom_call" | custom-call | flops 6000000000 | tf_op jit(solution)/shard_map/pallas_call | solution.py:20
  16.5 5.1 %all-to-all-done.g_ref = bf16[8,8,1536]{2,1,0:T(8,128)(2,1)S(1)} async-done(((bf16[8,8,1536]{2,1,0:T(8,128)(2,1)}), bf16[8,8,1536]{2,1,0:T(8,128)(2,1)S(1)}, u32[]{:S(2)}, u32[]{:S(2)}) %all-to-all-start) | async-done | bytes 196640 | tf_op jit(solution)/shard_map/all_to_all | solution.py:342
  21.6 2.1 %shard_map.72 = bf16[32,40,128]{2,1,0:T(8,128)(2,1)S(1)} custom-call(bf16[288,256]{1,0:T(8,128)(2,1)S(1)} %collective-permute-done.2.got_ref, bf16[3,18,64,128]{3,2,1,0:T(8,128)(2,1)S(1)} %get-tuple-element.43.wide_ref, f32[256,1024]{1,0:T(8,128)S(1)} %get-tuple-element.44.part_ref, bf16[8,8,1536]{2,1,0:T(8,128)(2,1)S(1)} %all-to-all-done.g_ref, ...), custom_call_target="tpu_custom_call" | custom-call | tf_op jit(solution)/shard_map/pallas_call | solution.py:20
  23.7 16.8 %all_to_all.15.got_ref = bf16[32,40,128]{2,1,0:T(8,128)(2,1)S(1)} all-to-all(bf16[32,40,128]{2,1,0:T(8,128)(2,1)S(1)} %shard_map.72), channel_id=1, replica_groups=mesh['slab'=4,'brick'=8] {'slab','brick'}, dimensions={0} | all-to-all | bytes 655360 | tf_op jit(solution)/shard_map/all_to_all | solution.py:399
  40.5 0.7 %shard_map.73 = (bf16[32,16,128]{2,1,0:T(8,128)(2,1)}, bf16[8,24,128]{2,1,0:T(8,128)(2,1)S(1)}, bf16[8,24,128]{2,1,0:T(8,128)(2,1)S(1)}, bf16[8,24,128]{2,1,0:T(8,128)(2,1)S(1)}, bf16[8,24,128]{2,1,0:T(8,128)(2,1)S(1)}) custom-call(bf16[32,40,128]{2,1,0:T(8,128)(2,1)S(1)} %all_to_all.15.got_ref), custom_call_target="tpu_custom_call" | custom-call | tf_op jit(solution)/shard_map/pallas_call | solution.py:20
  41.2 2.6 %all-to-all-start.2 = ((bf16[32,16,128]{2,1,0:T(8,128)(2,1)}), bf16[32,16,128]{2,1,0:T(8,128)(2,1)S(1)}, u32[]{:S(2)}, u32[]{:S(2)}) async-start(bf16[32,16,128]{2,1,0:T(8,128)(2,1)} %get-tuple-element.49), calls=%async_computation.2 | async-start | bytes 262144 | tf_op jit(solution)/shard_map/all_to_all | solution.py:406
  43.8 0.2 collective-permute-start.4
  44.0 1.7 %collective-permute-start.5 = (bf16[8,24,128]{2,1,0:T(8,128)(2,1)S(1)}, bf16[8,24,128]{2,1,0:T(8,128)(2,1)S(1)}, u32[]{:S(2)}, u32[]{:S(2)}) collective-permute-start(bf16[8,24,128]{2,1,0:T(8,128)(2,1)S(1)} %get-tuple-element.52), channel_id=1, source_target_pairs={{0,16},{8,24},{16,0},{24,8},{1,17},{9,25},{17,1},{25,9},{2,18},{10... | collective-permute-start | bytes 147464 | tf_op jit(solution)/shard_map/ppermute | solution.py:409
  45.6 0.1 collective-permute-start.6
  45.7 2.8 %collective-permute-done.5.refs_2_ = bf16[8,24,128]{2,1,0:T(8,128)(2,1)S(1)} collective-permute-done((bf16[8,24,128]{2,1,0:T(8,128)(2,1)S(1)}, bf16[8,24,128]{2,1,0:T(8,128)(2,1)S(1)}, u32[]{:S(2)}, u32[]{:S(2)}) %collective-permute-start.5) | collective-permute-done | bytes 49184 | tf_op jit(solution)/shard_map/ppermute | solution.py:409
  48.6 1.2 %collective-permute-done.6.refs_3_ = bf16[8,24,128]{2,1,0:T(8,128)(2,1)S(1)} collective-permute-done((bf16[8,24,128]{2,1,0:T(8,128)(2,1)S(1)}, bf16[8,24,128]{2,1,0:T(8,128)(2,1)S(1)}, u32[]{:S(2)}, u32[]{:S(2)}) %collective-permute-start.6) | collective-permute-done | bytes 49184 | tf_op jit(solution)/shard_map/ppermute | solution.py:409
  49.8 1.7 %all-to-all-done.2.whole_ref = bf16[32,16,128]{2,1,0:T(8,128)(2,1)S(1)} async-done(((bf16[32,16,128]{2,1,0:T(8,128)(2,1)}), bf16[32,16,128]{2,1,0:T(8,128)(2,1)S(1)}, u32[]{:S(2)}, u32[]{:S(2)}) %all-to-all-start.2) | async-done | bytes 131104 | tf_op jit(solution)/shard_map/all_to_all | solution.py:406
  51.5 0.9 %shard_map.74 = (bf16[12,8192]{1,0:T(8,128)(2,1)}, f32[3,3,3,16,32]{4,3,2,1,0:T(8,128)}, f32[256,96]{1,0:T(8,128)}) custom-call(bf16[32,16,128]{2,1,0:T(8,128)(2,1)S(1)} %all-to-all-done.2.whole_ref, bf16[8,24,128]{2,1,0:T(8,128)(2,1)S(1)} %get-tuple-element.50.refs_0_, bf16[8,24,128]{2,1,0:T(8,128)(2,1)S(1)} %collective-permute-done.4.refs_1_, ...), custom_call_target="tpu_custom_call" | custom-call | tf_op jit(solution)/shard_map/pallas_call | solution.py:20
  (11 shorter events, 0.1 us)
Async XLA Ops:
  0.6 4.9 %copy-start = (bf16[12,1,8192]{2,0,1:T(8,128)(2,1)S(1)}, bf16[12,1,8192]{2,0,1:T(8,128)(2,1)}, u32[]{:S(2)}) copy-start(bf16[12,1,8192]{2,0,1:T(8,128)(2,1)} %param.7) | copy-start | bytes 589828
  0.6 1.0 %copy-start.1 = (bf16[16,2,16,256]{3,2,1,0:T(8,128)(2,1)S(1)}, bf16[16,2,16,256]{3,2,1,0:T(8,128)(2,1)}, u32[]{:S(2)}) copy-start(bf16[16,2,16,256]{3,2,1,0:T(8,128)(2,1)} %v_ref.1) | copy-start | bytes 786436
  1.9 12.0 %collective-permute-start = (bf16[16,512]{1,0:T(8,128)(2,1)S(1)}, bf16[16,512]{1,0:T(8,128)(2,1)S(1)}, u32[]{:S(2)}, u32[]{:S(2)}) collective-permute-start(bf16[16,512]{1,0:T(8,128)(2,1)S(1)} %get-tuple-element.34), channel_id=1, source_target_pairs={{0,1},{2,3},{4,5},{6,7},{1,0},{3,2},{5,4},{7,6},{8,9},{10,11},{12,... | collective-permute-start | bytes 49160 | tf_op jit(solution)/shard_map/ppermute | solution.py:341
  4.9 9.0 %collective-permute-start.1 = (bf16[16,512]{1,0:T(8,128)(2,1)S(1)}, bf16[16,512]{1,0:T(8,128)(2,1)S(1)}, u32[]{:S(2)}, u32[]{:S(2)}) collective-permute-start(bf16[16,512]{1,0:T(8,128)(2,1)S(1)} %get-tuple-element.35), channel_id=1, source_target_pairs={{1,2},{3,4},{5,6},{2,1},{4,3},{6,5},{9,10},{11,12},{13,14},{10,9},... | collective-permute-start | bytes 49160 | tf_op jit(solution)/shard_map/ppermute | solution.py:340
  6.3 15.4 %all-to-all-start = ((bf16[8,8,1536]{2,1,0:T(8,128)(2,1)}), bf16[8,8,1536]{2,1,0:T(8,128)(2,1)S(1)}, u32[]{:S(2)}, u32[]{:S(2)}) async-start(bf16[8,8,1536]{2,1,0:T(8,128)(2,1)} %shard_map.71), calls=%async_computation | async-start | bytes 393216 | tf_op jit(solution)/shard_map/all_to_all | solution.py:342
  13.9 0.9 %copy-start.2 = (bf16[32,16,3,3,3]{0,1,4,3,2:T(8,128)(2,1)S(1)}, bf16[32,16,3,3,3]{0,1,4,3,2:T(8,128)(2,1)}, u32[]{:S(2)}) copy-start(bf16[32,16,3,3,3]{0,1,4,3,2:T(8,128)(2,1)} %param.5) | copy-start | bytes 82948
  13.9 0.9 %copy-start.3 = (bf16[96,32,2,2,2]{0,4,3,2,1:T(2,128)(2,1)S(1)}, bf16[96,32,2,2,2]{0,4,3,2,1:T(2,128)(2,1)}, u32[]{:S(2)}) copy-start(bf16[96,32,2,2,2]{0,4,3,2,1:T(2,128)(2,1)} %param.6) | copy-start | bytes 147460
  13.9 1.6 %collective-permute-start.3 = (bf16[288,256]{1,0:T(8,128)(2,1)S(1)}, bf16[288,256]{1,0:T(8,128)(2,1)S(1)}, u32[]{:S(2)}, u32[]{:S(2)}) collective-permute-start(bf16[288,256]{1,0:T(8,128)(2,1)S(1)} %get-tuple-element.38.near_ref), channel_id=1, source_target_pairs={{0,8},{16,24},{8,0},{24,16},{1,9},{17,25},{9,1},{25,17},{2,10},{18... | collective-permute-start | bytes 442376 | tf_op jit(solution)/shard_map/ppermute | solution.py:348
  14.0 2.5 %collective-permute-start.2 = (bf16[288,256]{1,0:T(8,128)(2,1)S(1)}, bf16[288,256]{1,0:T(8,128)(2,1)S(1)}, u32[]{:S(2)}, u32[]{:S(2)}) collective-permute-start(bf16[288,256]{1,0:T(8,128)(2,1)S(1)} %get-tuple-element.39.far_ref), channel_id=1, source_target_pairs={{8,16},{16,8},{9,17},{17,9},{10,18},{18,10},{11,19},{19,11},{12,20... | collective-permute-start | bytes 442376 | tf_op jit(solution)/shard_map/ppermute | solution.py:347
  41.2 10.3 %all-to-all-start.2 = ((bf16[32,16,128]{2,1,0:T(8,128)(2,1)}), bf16[32,16,128]{2,1,0:T(8,128)(2,1)S(1)}, u32[]{:S(2)}, u32[]{:S(2)}) async-start(bf16[32,16,128]{2,1,0:T(8,128)(2,1)} %get-tuple-element.49), calls=%async_computation.2 | async-start | bytes 262144 | tf_op jit(solution)/shard_map/all_to_all | solution.py:406
  43.8 2.0 %collective-permute-start.4 = (bf16[8,24,128]{2,1,0:T(8,128)(2,1)S(1)}, bf16[8,24,128]{2,1,0:T(8,128)(2,1)S(1)}, u32[]{:S(2)}, u32[]{:S(2)}) collective-permute-start(bf16[8,24,128]{2,1,0:T(8,128)(2,1)S(1)} %get-tuple-element.51), channel_id=1, source_target_pairs={{0,8},{8,0},{16,24},{24,16},{1,9},{9,1},{17,25},{25,17},{2,10},{10... | collective-permute-start | bytes 147464 | tf_op jit(solution)/shard_map/ppermute | solution.py:409
  44.0 4.6 %collective-permute-start.5 = (bf16[8,24,128]{2,1,0:T(8,128)(2,1)S(1)}, bf16[8,24,128]{2,1,0:T(8,128)(2,1)S(1)}, u32[]{:S(2)}, u32[]{:S(2)}) collective-permute-start(bf16[8,24,128]{2,1,0:T(8,128)(2,1)S(1)} %get-tuple-element.52), channel_id=1, source_target_pairs={{0,16},{8,24},{16,0},{24,8},{1,17},{9,25},{17,1},{25,9},{2,18},{10... | collective-permute-start | bytes 147464 | tf_op jit(solution)/shard_map/ppermute | solution.py:409
  45.6 4.2 %collective-permute-start.6 = (bf16[8,24,128]{2,1,0:T(8,128)(2,1)S(1)}, bf16[8,24,128]{2,1,0:T(8,128)(2,1)S(1)}, u32[]{:S(2)}, u32[]{:S(2)}) collective-permute-start(bf16[8,24,128]{2,1,0:T(8,128)(2,1)S(1)} %get-tuple-element.53), channel_id=1, source_target_pairs={{0,24},{8,16},{16,8},{24,0},{1,25},{9,17},{17,9},{25,1},{2,26},{10... | collective-permute-start | bytes 147464 | tf_op jit(solution)/shard_map/ppermute | solution.py:409

commit v5 on v4

--- a/solution.py
+++ b/solution.py
@@ -179,7 +179,17 @@
                 x_ref[row : row + size, j * half : (j + 1) * half] = wide_ref[i, 2 * j + b]
 
 
-def early_kernel(got_ref, near_ref, far_ref, w1_ref, wide_ref, part_ref, x_ref):
+def early_kernel(
+    got_ref, near_ref, far_ref, g_ref, w1_ref, w2t_ref, wide_ref, part_ref, back_ref, grad_ref, x_ref
+):
+    filters, cells = grad_ref.shape
+    bricks = g_ref.shape[0]
+    blocks = []
+    for b in range(bricks):
+        blocks.extend(unfold(g_ref[b].astype(f32), filters // bricks, cells))
+    gradient = jnp.concatenate(blocks, axis=0).astype(bf16)
+    grad_ref[...] = gradient
+    back_ref[...] = dot(w2t_ref[...], gradient)
     channels = wide_ref.shape[2] // 4
     for i, plane_ref in enumerate((got_ref, near_ref, far_ref)):
         wide_ref[i] = widen(plane_ref[...], channels)
@@ -193,17 +203,17 @@
     got_ref,
     wide_ref,
     part_ref,
-    g_ref,
+    back_ref,
+    grad_ref,
     w1_ref,
     w2p_ref,
-    w2t_ref,
     send_ref,
     far_wide_ref,
     far_ref,
     x_ref,
     sums_ref,
 ):
-    filters, cells = w2t_ref.shape[1], x_ref.shape[1]
+    filters, cells = grad_ref.shape
     channels = far_ref.shape[0] // 16
     bricks = filters // own_filters
     padded = w2p_ref.shape[0] // bricks
@@ -211,15 +221,10 @@
     far_wide_ref[0] = widen(got_ref[...], channels)
     fill_patches(far_ref, far_wide_ref)
     fill_patches(x_ref, wide_ref)
-    blocks = []
-    for b in range(bricks):
-        blocks.extend(unfold(g_ref[b].astype(f32), own_filters, cells))
-    gradient = jnp.concatenate(blocks, axis=0).astype(bf16)
     pre = part_ref[...] + dot(w1_ref[...], far_ref[...])
     sigma = jax.nn.sigmoid(pre)
     hidden = (pre * sigma).astype(bf16)
-    back = dot(w2t_ref[...], gradient)
-    delta = (back * sigma * (1.0 + pre * (1.0 - sigma))).astype(bf16)
+    delta = (back_ref[...] * sigma * (1.0 + pre * (1.0 - sigma))).astype(bf16)
     result = dot(w2p_ref[...], hidden)
     width = cells // chunks
     used = own_filters * (width // 128)
@@ -240,7 +245,7 @@
         lambda s: (s % 2) * (4 * mid) + ((s // 2) % 4) * mid + s // 8,
     )
     ordered = dot(natural, hidden).astype(bf16)
-    grad_two = dot_nt(ordered, gradient)
+    grad_two = dot_nt(ordered, grad_ref[...])
     for at, patches_ref in ((0, x_ref), (3, far_ref)):
         moments = dot_nt(patches_ref[...], delta).reshape(-1, 4, 4, channels, 8 * mid)
         by_r = moments[:, :, 0:3, :, : 4 * mid] + moments[:, :, 1:4, :, 4 * mid :]
@@ -364,16 +369,20 @@
         flops=BESIDE,
     )
     tall, half = rows + 2, cols // 2
-    wide, part = call(
+    wide, part, back, gradient = call(
         early_kernel,
         (
             jax.ShapeDtypeStruct((3, tall, 4 * channels, half), bf16),
             jax.ShapeDtypeStruct((8 * mid, cells), f32),
+            jax.ShapeDtypeStruct((8 * mid, cells), f32),
+            jax.ShapeDtypeStruct((filters, cells), bf16),
         ),
         got_near,
         near,
         far,
+        cotangent,
         w1_early,
+        w2t,
         scratch=(pltpu.VMEM((48 * channels, cells), bf16),),
         flops=BESIDE,
     )
@@ -385,10 +394,10 @@
         got_far,
         wide,
         part,
-        cotangent,
+        back,
+        gradient,
         w1_late,
         w2p,
-        w2t,
         scratch=(
             pltpu.VMEM((1, tall, 4 * channels, half), bf16),
             pltpu.VMEM((16 * channels, cells), bf16),

time: 52.8 us -> 52.6 us (level)
  blocking collectives: 16.8 us -> 15.7 us
  waiting for transfers between devices: 10.9 us -> 11.9 us
    all_to_all x1, blocking collectives: 16.8 us -> 15.7 us  [per_device(): got = lax.all_to_all(send, ALL, 0, 0, tiled=True)]
    all_to_all x1, waiting for transfers between devices: 5.13 us -> 6.12 us  [per_device(): cotangent = lax.all_to_all(cotangent, 'brick', 0, 0, tiled=True)]
where the time goes in v5:
time: 52.6 us; the launch traced here: 52.2 us
  starting transfers between devices  16.5 us (31%)
  blocking collectives  15.7 us (30%)
  waiting for transfers between devices  11.9 us (23%)
  Pallas kernels  6.27 us (12%)
  local copies, waits for them, and re-layouts  1.05 us (2%)
  between operations  0.77 us (1%)
    all_to_all x1, blocking collectives, per_device(): got = lax.all_to_all(send, ALL, 0, 0, tiled=True)  15.7 us
    all_to_all x1, starting transfers between devices, per_device(): cotangent = lax.all_to_all(cotangent, 'brick', 0, 0, tiled=True)  7.59 us
    pallas_call x8, Pallas kernels, call(): pl.pallas_call(body, out_shape=outs, in_specs=[vmem] * len(args), out_spe...  6.27 us
    all_to_all x1, waiting for transfers between devices, per_device(): cotangent = lax.all_to_all(cotangent, 'brick', 0, 0, tiled=True)  6.12 us
    ppermute x3, waiting for transfers between devices, per_device(): pieces[k] = lax.ppermute(pieces[k], 'slab', pairs)  4.06 us
    ppermute x1, starting transfers between devices, per_device(): near = lax.ppermute(near, 'brick', near_pairs)  3.03 us
    all_to_all x1, starting transfers between devices, per_device(): whole = lax.all_to_all(share, ALL, 0, 0, tiled=True)  2.58 us
    ppermute x3, starting transfers between devices, per_device(): pieces[k] = lax.ppermute(pieces[k], 'slab', pairs)  1.96 us
  transfers between devices with their start and end apart: 9, of which 4 were waited for; matrix products, arithmetic and copies ran while one was open for 0% of the time, Pallas kernels for 5%

profile of v5, /device:TPU:0, one launch (start us, length us, event | category | flops | bytes accessed | tf_op | source)
XLA Modules:
  0.0 52.2 jit_solution(6337328707209721353)
XLA Ops:
  0.6 1.0 %copy-done.1 = bf16[16,2,16,256]{3,2,1,0:T(8,128)(2,1)S(1)} copy-done((bf16[16,2,16,256]{3,2,1,0:T(8,128)(2,1)S(1)}, bf16[16,2,16,256]{3,2,1,0:T(8,128)(2,1)}, u32[]{:S(2)}) %copy-start.1) | copy-done | bytes 262168
  1.6 0.2 shard_map.67
  1.9 3.0 %collective-permute-start = (bf16[16,512]{1,0:T(8,128)(2,1)S(1)}, bf16[16,512]{1,0:T(8,128)(2,1)S(1)}, u32[]{:S(2)}, u32[]{:S(2)}) collective-permute-start(bf16[16,512]{1,0:T(8,128)(2,1)S(1)} %get-tuple-element.36), channel_id=1, source_target_pairs={{0,1},{2,3},{4,5},{6,7},{1,0},{3,2},{5,4},{7,6},{8,9},{10,11},{12,... | collective-permute-start | bytes 49160 | tf_op jit(solution)/shard_map/ppermute | solution.py:346
  4.9 0.7 %collective-permute-start.1 = (bf16[16,512]{1,0:T(8,128)(2,1)S(1)}, bf16[16,512]{1,0:T(8,128)(2,1)S(1)}, u32[]{:S(2)}, u32[]{:S(2)}) collective-permute-start(bf16[16,512]{1,0:T(8,128)(2,1)S(1)} %get-tuple-element.37), channel_id=1, source_target_pairs={{1,2},{3,4},{5,6},{2,1},{4,3},{6,5},{9,10},{11,12},{13,14},{10,9},... | collective-permute-start | bytes 49160 | tf_op jit(solution)/shard_map/ppermute | solution.py:345
  5.6 0.7 %shard_map.69 = bf16[8,8,1536]{2,1,0:T(8,128)(2,1)} custom-call(bf16[12,8192]{1,0:T(8,128)(2,1)S(1)} %bitcast.12), custom_call_target="tpu_custom_call" | custom-call | tf_op jit(solution)/shard_map/pallas_call | solution.py:20
  6.3 7.6 %all-to-all-start = ((bf16[8,8,1536]{2,1,0:T(8,128)(2,1)}), bf16[8,8,1536]{2,1,0:T(8,128)(2,1)S(1)}, u32[]{:S(2)}, u32[]{:S(2)}) async-start(bf16[8,8,1536]{2,1,0:T(8,128)(2,1)} %shard_map.69), calls=%async_computation | async-start | bytes 393216 | tf_op jit(solution)/shard_map/all_to_all | solution.py:347
  13.9 0.0 copy-start.3
  13.9 0.1 collective-permute-start.3
  14.0 0.7 %collective-permute-start.2 = (bf16[288,256]{1,0:T(8,128)(2,1)S(1)}, bf16[288,256]{1,0:T(8,128)(2,1)S(1)}, u32[]{:S(2)}, u32[]{:S(2)}) collective-permute-start(bf16[288,256]{1,0:T(8,128)(2,1)S(1)} %get-tuple-element.41.far_ref), channel_id=1, source_target_pairs={{8,16},{16,8},{9,17},{17,9},{10,18},{18,10},{11,19},{19,11},{12,20... | collective-permute-start | bytes 442376 | tf_op jit(solution)/shard_map/ppermute | solution.py:352
  14.7 0.1 copy-done.2
  14.8 0.8 %shard_map.70 = (bf16[256,768]{1,0:T(8,128)(2,1)S(1)}, bf16[256,256]{1,0:T(8,128)(2,1)S(1)}, bf16[128,256]{1,0:T(8,128)(2,1)S(1)}, bf16[256,96]{1,0:T(8,128)(2,1)S(1)}) custom-call(bf16[432,32]{1,0:T(8,128)(2,1)S(1)} %bitcast.13, bf16[256,96]{1,0:T(8,128)(2,1)S(1)} %bitcast.14), custom_call_target="tpu_custom_call" | custom-call | flops 6000000000 | tf_op jit(solution)/shard_map/pallas_call | solution.py:20
  15.5 6.1 %all-to-all-done.g_ref = bf16[8,8,1536]{2,1,0:T(8,128)(2,1)S(1)} async-done(((bf16[8,8,1536]{2,1,0:T(8,128)(2,1)}), bf16[8,8,1536]{2,1,0:T(8,128)(2,1)S(1)}, u32[]{:S(2)}, u32[]{:S(2)}) %all-to-all-start) | async-done | bytes 196640 | tf_op jit(solution)/shard_map/all_to_all | solution.py:347
  21.6 1.1 %shard_map.71 = (bf16[3,18,64,128]{3,2,1,0:T(8,128)(2,1)S(1)}, f32[256,1024]{1,0:T(8,128)S(1)}, f32[256,1024]{1,0:T(8,128)S(1)}, bf16[96,1024]{1,0:T(8,128)(2,1)S(1)}) custom-call(bf16[288,256]{1,0:T(8,128)(2,1)S(1)} %collective-permute-done.3.got_ref, bf16[288,256]{1,0:T(8,128)(2,1)S(1)} %get-tuple-element.40.near_ref, ...), custom_call_target="tpu_custom_call" | custom-call | flops 6000000000 | tf_op jit(solution)/shard_map/pallas_call | solution.py:20
  22.7 1.9 %shard_map.72 = bf16[32,40,128]{2,1,0:T(8,128)(2,1)S(1)} custom-call(bf16[288,256]{1,0:T(8,128)(2,1)S(1)} %collective-permute-done.2.got_ref, bf16[3,18,64,128]{3,2,1,0:T(8,128)(2,1)S(1)} %get-tuple-element.47.wide_ref, f32[256,1024]{1,0:T(8,128)S(1)} %get-tuple-element.48.part_ref, f32[256,1024]{1,0:T(8,128)S(1)} %get-tuple-element.49.back_ref, ...), custom_call_target="tpu_custom_call" | custom-call | tf_op jit(solution)/shard_map/pallas_call | solution.py:20
  24.6 15.7 %all_to_all.15.got_ref = bf16[32,40,128]{2,1,0:T(8,128)(2,1)S(1)} all-to-all(bf16[32,40,128]{2,1,0:T(8,128)(2,1)S(1)} %shard_map.72), channel_id=1, replica_groups=mesh['slab'=4,'brick'=8] {'slab','brick'}, dimensions={0} | all-to-all | bytes 655360 | tf_op jit(solution)/shard_map/all_to_all | solution.py:408
  40.3 0.7 %shard_map.73 = (bf16[32,16,128]{2,1,0:T(8,128)(2,1)}, bf16[8,24,128]{2,1,0:T(8,128)(2,1)S(1)}, bf16[8,24,128]{2,1,0:T(8,128)(2,1)S(1)}, bf16[8,24,128]{2,1,0:T(8,128)(2,1)S(1)}, bf16[8,24,128]{2,1,0:T(8,128)(2,1)S(1)}) custom-call(bf16[32,40,128]{2,1,0:T(8,128)(2,1)S(1)} %all_to_all.15.got_ref), custom_call_target="tpu_custom_call" | custom-call | tf_op jit(solution)/shard_map/pallas_call | solution.py:20
  41.0 2.6 %all-to-all-start.2 = ((bf16[32,16,128]{2,1,0:T(8,128)(2,1)}), bf16[32,16,128]{2,1,0:T(8,128)(2,1)S(1)}, u32[]{:S(2)}, u32[]{:S(2)}) async-start(bf16[32,16,128]{2,1,0:T(8,128)(2,1)} %get-tuple-element.53), calls=%async_computation.2 | async-start | bytes 262144 | tf_op jit(solution)/shard_map/all_to_all | solution.py:415
  43.6 0.2 collective-permute-start.4
  43.8 1.7 %collective-permute-start.5 = (bf16[8,24,128]{2,1,0:T(8,128)(2,1)S(1)}, bf16[8,24,128]{2,1,0:T(8,128)(2,1)S(1)}, u32[]{:S(2)}, u32[]{:S(2)}) collective-permute-start(bf16[8,24,128]{2,1,0:T(8,128)(2,1)S(1)} %get-tuple-element.56), channel_id=1, source_target_pairs={{0,16},{8,24},{16,0},{24,8},{1,17},{9,25},{17,1},{25,9},{2,18},{10... | collective-permute-start | bytes 147464 | tf_op jit(solution)/shard_map/ppermute | solution.py:418
  45.4 0.1 collective-permute-start.6
  45.5 2.8 %collective-permute-done.5.refs_2_ = bf16[8,24,128]{2,1,0:T(8,128)(2,1)S(1)} collective-permute-done((bf16[8,24,128]{2,1,0:T(8,128)(2,1)S(1)}, bf16[8,24,128]{2,1,0:T(8,128)(2,1)S(1)}, u32[]{:S(2)}, u32[]{:S(2)}) %collective-permute-start.5) | collective-permute-done | bytes 49184 | tf_op jit(solution)/shard_map/ppermute | solution.py:418
  48.4 1.2 %collective-permute-done.6.refs_3_ = bf16[8,24,128]{2,1,0:T(8,128)(2,1)S(1)} collective-permute-done((bf16[8,24,128]{2,1,0:T(8,128)(2,1)S(1)}, bf16[8,24,128]{2,1,0:T(8,128)(2,1)S(1)}, u32[]{:S(2)}, u32[]{:S(2)}) %collective-permute-start.6) | collective-permute-done | bytes 49184 | tf_op jit(solution)/shard_map/ppermute | solution.py:418
  49.6 1.7 %all-to-all-done.2.whole_ref = bf16[32,16,128]{2,1,0:T(8,128)(2,1)S(1)} async-done(((bf16[32,16,128]{2,1,0:T(8,128)(2,1)}), bf16[32,16,128]{2,1,0:T(8,128)(2,1)S(1)}, u32[]{:S(2)}, u32[]{:S(2)}) %all-to-all-start.2) | async-done | bytes 131104 | tf_op jit(solution)/shard_map/all_to_all | solution.py:415
  51.3 0.9 %shard_map.74 = (bf16[12,8192]{1,0:T(8,128)(2,1)}, f32[3,3,3,16,32]{4,3,2,1,0:T(8,128)}, f32[256,96]{1,0:T(8,128)}) custom-call(bf16[32,16,128]{2,1,0:T(8,128)(2,1)S(1)} %all-to-all-done.2.whole_ref, bf16[8,24,128]{2,1,0:T(8,128)(2,1)S(1)} %get-tuple-element.54.refs_0_, bf16[8,24,128]{2,1,0:T(8,128)(2,1)S(1)} %collective-permute-done.4.refs_1_, ...), custom_call_target="tpu_custom_call" | custom-call | tf_op jit(solution)/shard_map/pallas_call | solution.py:20
  (11 shorter events, 0.1 us)
Async XLA Ops:
  0.6 4.9 %copy-start = (bf16[12,1,8192]{2,0,1:T(8,128)(2,1)S(1)}, bf16[12,1,8192]{2,0,1:T(8,128)(2,1)}, u32[]{:S(2)}) copy-start(bf16[12,1,8192]{2,0,1:T(8,128)(2,1)} %param.7) | copy-start | bytes 589828
  0.6 1.0 %copy-start.1 = (bf16[16,2,16,256]{3,2,1,0:T(8,128)(2,1)S(1)}, bf16[16,2,16,256]{3,2,1,0:T(8,128)(2,1)}, u32[]{:S(2)}) copy-start(bf16[16,2,16,256]{3,2,1,0:T(8,128)(2,1)} %v_ref.1) | copy-start | bytes 786436
  1.9 12.0 %collective-permute-start = (bf16[16,512]{1,0:T(8,128)(2,1)S(1)}, bf16[16,512]{1,0:T(8,128)(2,1)S(1)}, u32[]{:S(2)}, u32[]{:S(2)}) collective-permute-start(bf16[16,512]{1,0:T(8,128)(2,1)S(1)} %get-tuple-element.36), channel_id=1, source_target_pairs={{0,1},{2,3},{4,5},{6,7},{1,0},{3,2},{5,4},{7,6},{8,9},{10,11},{12,... | collective-permute-start | bytes 49160 | tf_op jit(solution)/shard_map/ppermute | solution.py:346
  4.9 9.0 %collective-permute-start.1 = (bf16[16,512]{1,0:T(8,128)(2,1)S(1)}, bf16[16,512]{1,0:T(8,128)(2,1)S(1)}, u32[]{:S(2)}, u32[]{:S(2)}) collective-permute-start(bf16[16,512]{1,0:T(8,128)(2,1)S(1)} %get-tuple-element.37), channel_id=1, source_target_pairs={{1,2},{3,4},{5,6},{2,1},{4,3},{6,5},{9,10},{11,12},{13,14},{10,9},... | collective-permute-start | bytes 49160 | tf_op jit(solution)/shard_map/ppermute | solution.py:345
  6.3 15.4 %all-to-all-start = ((bf16[8,8,1536]{2,1,0:T(8,128)(2,1)}), bf16[8,8,1536]{2,1,0:T(8,128)(2,1)S(1)}, u32[]{:S(2)}, u32[]{:S(2)}) async-start(bf16[8,8,1536]{2,1,0:T(8,128)(2,1)} %shard_map.69), calls=%async_computation | async-start | bytes 393216 | tf_op jit(solution)/shard_map/all_to_all | solution.py:347
  13.9 0.9 %copy-start.2 = (bf16[32,16,3,3,3]{0,1,4,3,2:T(8,128)(2,1)S(1)}, bf16[32,16,3,3,3]{0,1,4,3,2:T(8,128)(2,1)}, u32[]{:S(2)}) copy-start(bf16[32,16,3,3,3]{0,1,4,3,2:T(8,128)(2,1)} %param.5) | copy-start | bytes 82948
  13.9 0.9 %copy-start.3 = (bf16[96,32,2,2,2]{0,4,3,2,1:T(2,128)(2,1)S(1)}, bf16[96,32,2,2,2]{0,4,3,2,1:T(2,128)(2,1)}, u32[]{:S(2)}) copy-start(bf16[96,32,2,2,2]{0,4,3,2,1:T(2,128)(2,1)} %param.6) | copy-start | bytes 147460
  13.9 1.6 %collective-permute-start.3 = (bf16[288,256]{1,0:T(8,128)(2,1)S(1)}, bf16[288,256]{1,0:T(8,128)(2,1)S(1)}, u32[]{:S(2)}, u32[]{:S(2)}) collective-permute-start(bf16[288,256]{1,0:T(8,128)(2,1)S(1)} %get-tuple-element.40.near_ref), channel_id=1, source_target_pairs={{0,8},{16,24},{8,0},{24,16},{1,9},{17,25},{9,1},{25,17},{2,10},{18... | collective-permute-start | bytes 442376 | tf_op jit(solution)/shard_map/ppermute | solution.py:353
  14.0 8.7 %collective-permute-start.2 = (bf16[288,256]{1,0:T(8,128)(2,1)S(1)}, bf16[288,256]{1,0:T(8,128)(2,1)S(1)}, u32[]{:S(2)}, u32[]{:S(2)}) collective-permute-start(bf16[288,256]{1,0:T(8,128)(2,1)S(1)} %get-tuple-element.41.far_ref), channel_id=1, source_target_pairs={{8,16},{16,8},{9,17},{17,9},{10,18},{18,10},{11,19},{19,11},{12,20... | collective-permute-start | bytes 442376 | tf_op jit(solution)/shard_map/ppermute | solution.py:352
  41.0 10.3 %all-to-all-start.2 = ((bf16[32,16,128]{2,1,0:T(8,128)(2,1)}), bf16[32,16,128]{2,1,0:T(8,128)(2,1)S(1)}, u32[]{:S(2)}, u32[]{:S(2)}) async-start(bf16[32,16,128]{2,1,0:T(8,128)(2,1)} %get-tuple-element.53), calls=%async_computation.2 | async-start | bytes 262144 | tf_op jit(solution)/shard_map/all_to_all | solution.py:415
  43.6 2.0 %collective-permute-start.4 = (bf16[8,24,128]{2,1,0:T(8,128)(2,1)S(1)}, bf16[8,24,128]{2,1,0:T(8,128)(2,1)S(1)}, u32[]{:S(2)}, u32[]{:S(2)}) collective-permute-start(bf16[8,24,128]{2,1,0:T(8,128)(2,1)S(1)} %get-tuple-element.55), channel_id=1, source_target_pairs={{0,8},{8,0},{16,24},{24,16},{1,9},{9,1},{17,25},{25,17},{2,10},{10... | collective-permute-start | bytes 147464 | tf_op jit(solution)/shard_map/ppermute | solution.py:418
  43.8 4.6 %collective-permute-start.5 = (bf16[8,24,128]{2,1,0:T(8,128)(2,1)S(1)}, bf16[8,24,128]{2,1,0:T(8,128)(2,1)S(1)}, u32[]{:S(2)}, u32[]{:S(2)}) collective-permute-start(bf16[8,24,128]{2,1,0:T(8,128)(2,1)S(1)} %get-tuple-element.56), channel_id=1, source_target_pairs={{0,16},{8,24},{16,0},{24,8},{1,17},{9,25},{17,1},{25,9},{2,18},{10... | collective-permute-start | bytes 147464 | tf_op jit(solution)/shard_map/ppermute | solution.py:418
  45.4 4.2 %collective-permute-start.6 = (bf16[8,24,128]{2,1,0:T(8,128)(2,1)S(1)}, bf16[8,24,128]{2,1,0:T(8,128)(2,1)S(1)}, u32[]{:S(2)}, u32[]{:S(2)}) collective-permute-start(bf16[8,24,128]{2,1,0:T(8,128)(2,1)S(1)} %get-tuple-element.57), channel_id=1, source_target_pairs={{0,24},{8,16},{16,8},{24,0},{1,25},{9,17},{17,9},{25,1},{2,26},{10... | collective-permute-start | bytes 147464 | tf_op jit(solution)/shard_map/ppermute | solution.py:418

commit v6 on v5

--- a/solution.py
+++ b/solution.py
@@ -48,15 +48,23 @@
     return lax.axis_index(axis) % 2 == 0
 
 
-def edge_kernel(v_ref, near_ref, far_ref, turned_ref):
+def plane_kernel(v_ref, near_ref, far_ref):
     channels, depth, rows, cols = v_ref.shape
     swap = one_hot(
         (channels * rows, channels * rows), lambda r: (r % channels) * rows + r // channels
     )
     planes = [v_ref[:, a].reshape(channels * rows, cols) for a in range(depth)]
     turned = dot(swap, jnp.concatenate(planes, axis=1)).astype(bf16)
-    turned_ref[...] = turned
-    first, last = turned[:channels], turned[(rows - 1) * channels :]
+    even = is_even("slab")
+    near_ref[...] = jnp.where(even, turned[:, cols:], turned[:, :cols])
+    far_ref[...] = jnp.where(even, turned[:, :cols], turned[:, cols:])
+
+
+def edge_kernel(a_ref, b_ref, c_ref, d_ref, near_ref, far_ref):
+    channels = near_ref.shape[0]
+    planes = (a_ref, b_ref, c_ref, d_ref)
+    first = jnp.concatenate([ref[:channels] for ref in planes], axis=1)
+    last = jnp.concatenate([ref[ref.shape[0] - channels :] for ref in planes], axis=1)
     even = is_even("brick")
     near_ref[...] = jnp.where(even, last, first)
     far_ref[...] = jnp.where(even, first, last)
@@ -127,10 +135,10 @@
     group = lax.broadcasted_iota(jnp.int32, (channels, 4 * mid), 1) // mid
     even = is_even("slab")
     for a in range(4):
-        first = jnp.where(even, 3 - a, a) * (16 * channels)
+        first = jnp.where(even, 3 - a, a) * (4 * channels)
         for b in range(4):
             for e in range(4):
-                rows = pl.ds(pl.multiple_of(first + (b * 4 + e) * channels, 16), channels)
+                rows = pl.ds(pl.multiple_of(first + (16 * b + e) * channels, 16), channels)
                 for r in range(2):
                     tile = jnp.zeros((channels, 4 * mid), f32)
                     for p in range(2):
@@ -142,8 +150,9 @@
                                 tile = jnp.where(group == p * 2 + q, piece, tile)
                     tall_ref[rows, r * 4 * mid : (r + 1) * 4 * mid] = tile.astype(bf16)
     placed = dot_nt(one_hot((size, size), lambda s: s), tall_ref[...]).astype(bf16)
-    early_ref[...] = placed[:, : 48 * channels]
-    late_ref[...] = placed[:, 48 * channels :]
+    early_ref[...] = placed
+    late_ref[0] = placed[:, : 16 * channels]
+    late_ref[1] = placed[:, 48 * channels :]
     order = one_hot(
         (size, size), lambda s: (s % mid) * 8 + ((s // mid) % 4) * 2 + s // (4 * mid)
     )
@@ -171,16 +180,29 @@
 
 
 def fill_patches(x_ref, wide_ref):
-    planes, _, size, half = wide_ref.shape
-    for i in range(planes):
-        for j in range(x_ref.shape[1] // half):
-            for b in range(4):
-                row = (i * 4 + b) * size
-                x_ref[row : row + size, j * half : (j + 1) * half] = wide_ref[i, 2 * j + b]
+    planes, rows, size, half = wide_ref.shape
+    for j in range(rows // 2):
+        for b in range(4):
+            y = 2 * j + b - 1
+            if 0 <= y < rows:
+                for i in range(planes):
+                    row = (b * 4 + i) * size
+                    x_ref[row : row + size, j * half : (j + 1) * half] = wide_ref[i, y]
 
 
 def early_kernel(
-    got_ref, near_ref, far_ref, g_ref, w1_ref, w2t_ref, wide_ref, part_ref, back_ref, grad_ref, x_ref
+    a_ref,
+    b_ref,
+    c_ref,
+    d_ref,
+    g_ref,
+    w1_ref,
+    w2t_ref,
+    wide_ref,
+    part_ref,
+    back_ref,
+    grad_ref,
+    x_ref,
 ):
     filters, cells = grad_ref.shape
     bricks = g_ref.shape[0]
@@ -190,9 +212,12 @@
     gradient = jnp.concatenate(blocks, axis=0).astype(bf16)
     grad_ref[...] = gradient
     back_ref[...] = dot(w2t_ref[...], gradient)
-    channels = wide_ref.shape[2] // 4
-    for i, plane_ref in enumerate((got_ref, near_ref, far_ref)):
-        wide_ref[i] = widen(plane_ref[...], channels)
+    size, half = wide_ref.shape[2:]
+    for i, plane_ref in enumerate((a_ref, b_ref, c_ref, d_ref)):
+        wide_ref[i] = widen(plane_ref[...], size // 4)
+    edge = jnp.zeros((4 * size, half), bf16)
+    x_ref[: 4 * size, :half] = edge
+    x_ref[12 * size :, cells - half :] = edge
     fill_patches(x_ref, wide_ref)
     part_ref[...] = dot(w1_ref[...], x_ref[...])
 
@@ -200,7 +225,8 @@
 def main_kernel(
     chunks,
     own_filters,
-    got_ref,
+    near_ref,
+    far_ref,
     wide_ref,
     part_ref,
     back_ref,
@@ -208,20 +234,32 @@
     w1_ref,
     w2p_ref,
     send_ref,
-    far_wide_ref,
-    far_ref,
     x_ref,
     sums_ref,
 ):
     filters, cells = grad_ref.shape
-    channels = far_ref.shape[0] // 16
+    channels = near_ref.shape[0]
     bricks = filters // own_filters
     padded = w2p_ref.shape[0] // bricks
     slots = send_ref.shape[0]
-    far_wide_ref[0] = widen(got_ref[...], channels)
-    fill_patches(far_ref, far_wide_ref)
     fill_patches(x_ref, wide_ref)
-    pre = part_ref[...] + dot(w1_ref[...], far_ref[...])
+    half = wide_ref.shape[3]
+    cols = 2 * half
+    even = is_even("brick")
+    before = jnp.where(even, far_ref[...], near_ref[...])
+    after = jnp.where(even, near_ref[...], far_ref[...])
+    edges = [e[:, i * cols : (i + 1) * cols] for e in (before, after) for i in range(4)]
+    edges = widen(jnp.concatenate(edges, axis=0), channels).reshape(2, 16 * channels, half)
+    x_ref[: 16 * channels, :half] = edges[0]
+    x_ref[48 * channels :, cells - half :] = edges[1]
+    pre = jnp.concatenate(
+        [
+            part_ref[:, :half] + dot(w1_ref[0], edges[0]),
+            part_ref[:, half : cells - half],
+            part_ref[:, cells - half :] + dot(w1_ref[1], edges[1]),
+        ],
+        axis=1,
+    )
     sigma = jax.nn.sigmoid(pre)
     hidden = (pre * sigma).astype(bf16)
     delta = (back_ref[...] * sigma * (1.0 + pre * (1.0 - sigma))).astype(bf16)
@@ -246,10 +284,10 @@
     )
     ordered = dot(natural, hidden).astype(bf16)
     grad_two = dot_nt(ordered, grad_ref[...])
-    for at, patches_ref in ((0, x_ref), (3, far_ref)):
-        moments = dot_nt(patches_ref[...], delta).reshape(-1, 4, 4, channels, 8 * mid)
-        by_r = moments[:, :, 0:3, :, : 4 * mid] + moments[:, :, 1:4, :, 4 * mid :]
-        sums_ref[at : at + by_r.shape[0]] = by_r.reshape(-1, 4, 3 * channels, 4 * mid)
+    moments = dot_nt(x_ref[...], delta).reshape(4, 4, 4, channels, 8 * mid)
+    by_r = moments[:, :, 0:3, :, : 4 * mid] + moments[:, :, 1:4, :, 4 * mid :]
+    for i in range(4):
+        sums_ref[i] = by_r[:, i].reshape(4, 3 * channels, 4 * mid)
     group = lax.broadcasted_iota(jnp.int32, (9 * channels, 4 * mid), 1) // mid
     total = jnp.zeros((9 * channels, 4 * mid), f32)
     even = is_even("slab")
@@ -329,28 +367,25 @@
 
     chunks = min(slabs, cells // 128)
 
-    edge = jax.ShapeDtypeStruct((channels, 2 * cols), bf16)
-    near, far, turned = call(
-        edge_kernel,
-        (edge, edge, jax.ShapeDtypeStruct((rows * channels, 2 * cols), bf16)),
-        volume,
-    )
-    near, far, turned, upstream = lax.optimization_barrier((near, far, turned, upstream))
+    plane = jax.ShapeDtypeStruct((rows * channels, cols), bf16)
+    near, far = call(plane_kernel, (plane, plane), volume)
+    near_pairs, far_pairs = swaps(slabs)
+    got_far = lax.ppermute(far, "slab", far_pairs)
+    got_near = lax.ppermute(near, "slab", near_pairs)
+    near, far, upstream = lax.optimization_barrier((near, far, upstream))
     (cotangent,) = call(
         block_kernel,
         (jax.ShapeDtypeStruct((bricks, 8, block_width(own_filters, cells)), bf16),),
         upstream.reshape(own_filters, -1),
     )
+    cotangent = lax.all_to_all(cotangent, "brick", 0, 0, tiled=True)
+
+    planes = (got_near, near, far, got_far)
+    edge = jax.ShapeDtypeStruct((channels, 4 * cols), bf16)
+    near, far = call(edge_kernel, (edge, edge), *planes)
     near_pairs, far_pairs = swaps(bricks)
-    far = lax.ppermute(far, "brick", far_pairs)
-    near = lax.ppermute(near, "brick", near_pairs)
-    cotangent = lax.all_to_all(cotangent, "brick", 0, 0, tiled=True)
-
-    plane = jax.ShapeDtypeStruct(((rows + 2) * channels, cols), bf16)
-    near, far = call(face_kernel, (plane, plane), turned, near, far)
-    near_pairs, far_pairs = swaps(slabs)
-    got_far = lax.ppermute(far, "slab", far_pairs)
-    got_near = lax.ppermute(near, "slab", near_pairs)
+    got_far = lax.ppermute(far, "brick", far_pairs)
+    got_near = lax.ppermute(near, "brick", near_pairs)
 
     near, far, kernel_one, kernel_two = lax.optimization_barrier(
         (near, far, kernel_one, kernel_two)
@@ -358,8 +393,8 @@
     w1_early, w1_late, w2p, w2t = call(
         functools.partial(weights_kernel, own_filters),
         (
-            jax.ShapeDtypeStruct((8 * mid, 48 * channels), bf16),
-            jax.ShapeDtypeStruct((8 * mid, 16 * channels), bf16),
+            jax.ShapeDtypeStruct((8 * mid, 64 * channels), bf16),
+            jax.ShapeDtypeStruct((2, 8 * mid, 16 * channels), bf16),
             jax.ShapeDtypeStruct((bricks * padded, 8 * mid), bf16),
             jax.ShapeDtypeStruct((8 * mid, filters), bf16),
         ),
@@ -368,22 +403,20 @@
         scratch=(pltpu.VMEM((64 * channels, 8 * mid), bf16),),
         flops=BESIDE,
     )
-    tall, half = rows + 2, cols // 2
+    patches = pltpu.VMEM((64 * channels, cells), bf16)
     wide, part, back, gradient = call(
         early_kernel,
         (
-            jax.ShapeDtypeStruct((3, tall, 4 * channels, half), bf16),
+            jax.ShapeDtypeStruct((4, rows, 4 * channels, cols // 2), bf16),
             jax.ShapeDtypeStruct((8 * mid, cells), f32),
             jax.ShapeDtypeStruct((8 * mid, cells), f32),
             jax.ShapeDtypeStruct((filters, cells), bf16),
         ),
-        got_near,
-        near,
-        far,
+        *planes,
         cotangent,
         w1_early,
         w2t,
-        scratch=(pltpu.VMEM((48 * channels, cells), bf16),),
+        scratch=(patches,),
         flops=BESIDE,
     )
     width = cells // chunks
@@ -391,6 +424,7 @@
     (send,) = call(
         functools.partial(main_kernel, chunks, own_filters),
         (jax.ShapeDtypeStruct((devices, 16 + chunk_rows, 128), bf16),),
+        got_near,
         got_far,
         wide,
         part,
@@ -398,12 +432,7 @@
         gradient,
         w1_late,
         w2p,
-        scratch=(
-            pltpu.VMEM((1, tall, 4 * channels, half), bf16),
-            pltpu.VMEM((16 * channels, cells), bf16),
-            pltpu.VMEM((48 * channels, cells), bf16),
-            pltpu.VMEM((4, 4, 3 * channels, 4 * mid), f32),
-        ),
+        scratch=(patches, pltpu.VMEM((4, 4, 3 * channels, 4 * mid), f32)),
     )
     got = lax.all_to_all(send, ALL, 0, 0, tiled=True)
     piece = jax.ShapeDtypeStruct((bricks, chunk_rows, 128), bf16)

time: 52.6 us -> 51.7 us (0.983)
  blocking collectives: 15.7 us -> 17.9 us
  waiting for transfers between devices: 11.9 us -> 10 us
  starting transfers between devices: 16.5 us -> 15.3 us
    all_to_all x1, blocking collectives: 15.7 us -> 17.9 us  [per_device(): got = lax.all_to_all(send, ALL, 0, 0, tiled=True)]
    all_to_all x1, waiting for transfers between devices: 6.12 us -> 4.23 us  [per_device(): cotangent = lax.all_to_all(cotangent, 'brick', 0, 0, tiled=True)]
    ppermute x2, starting transfers between devices: 3.68 us -> 2.72 us  [the longest x1 2.07 us: per_device(): got_near = lax.ppermute(near, 'brick', near_pairs)]
    all_to_all x1, starting transfers between devices: 7.59 us -> 6.85 us  [per_device(): cotangent = lax.all_to_all(cotangent, 'brick', 0, 0, tiled=True)]
  transfers between devices with their start and end apart: 9 -> 9, of which waited for: 4 -> 4; matrix products, arithmetic and copies ran while one was open for 0% -> 0% of each run, Pallas kernels for 5% -> 6%
where the time goes in v6:
time: 51.7 us; the launch traced here: 51.4 us
  blocking collectives  17.9 us (35%)
  starting transfers between devices  15.3 us (30%)
  waiting for transfers between devices  10 us (19%)
  Pallas kernels  6.35 us (12%)
  local copies, waits for them, and re-layouts  1 us (2%)
  between operations  0.78 us (2%)
    all_to_all x1, blocking collectives, per_device(): got = lax.all_to_all(send, ALL, 0, 0, tiled=True)  17.9 us
    all_to_all x1, starting transfers between devices, per_device(): cotangent = lax.all_to_all(cotangent, 'brick', 0, 0, tiled=True)  6.85 us
    pallas_call x8, Pallas kernels, call(): pl.pallas_call(body, out_shape=outs, in_specs=[vmem] * len(args), out_spe...  6.35 us
    all_to_all x1, waiting for transfers between devices, per_device(): cotangent = lax.all_to_all(cotangent, 'brick', 0, 0, tiled=True)  4.23 us
    ppermute x3, waiting for transfers between devices, per_device(): pieces[k] = lax.ppermute(pieces[k], 'slab', pairs)  4.06 us
    all_to_all x1, starting transfers between devices, per_device(): whole = lax.all_to_all(share, ALL, 0, 0, tiled=True)  2.58 us
    ppermute x1, starting transfers between devices, per_device(): got_near = lax.ppermute(near, 'brick', near_pairs)  2.07 us
    ppermute x3, starting transfers between devices, per_device(): pieces[k] = lax.ppermute(pieces[k], 'slab', pairs)  1.96 us
  transfers between devices with their start and end apart: 9, of which 4 were waited for; matrix products, arithmetic and copies ran while one was open for 0% of the time, Pallas kernels for 6%

profile of v6, /device:TPU:0, one launch (start us, length us, event | category | flops | bytes accessed | tf_op | source)
XLA Modules:
  0.0 51.4 jit_solution(9271337594337696233)
XLA Ops:
  0.6 1.0 %copy-done.1 = bf16[16,2,16,256]{3,2,1,0:T(8,128)(2,1)S(1)} copy-done((bf16[16,2,16,256]{3,2,1,0:T(8,128)(2,1)S(1)}, bf16[16,2,16,256]{3,2,1,0:T(8,128)(2,1)}, u32[]{:S(2)}) %copy-start.1) | copy-done | bytes 262168
  1.6 0.2 shard_map.67
  1.9 0.5 %collective-permute-start = (bf16[256,256]{1,0:T(8,128)(2,1)S(1)}, bf16[256,256]{1,0:T(8,128)(2,1)S(1)}, u32[]{:S(2)}, u32[]{:S(2)}) collective-permute-start(bf16[256,256]{1,0:T(8,128)(2,1)S(1)} %get-tuple-element.30.b_ref), channel_id=1, source_target_pairs={{0,8},{16,24},{8,0},{24,16},{1,9},{17,25},{9,1},{25,17},{2,10},{18... | collective-permute-start | bytes 393224 | tf_op jit(solution)/shard_map/ppermute | solution.py:374
  2.4 0.7 %collective-permute-start.1 = (bf16[256,256]{1,0:T(8,128)(2,1)S(1)}, bf16[256,256]{1,0:T(8,128)(2,1)S(1)}, u32[]{:S(2)}, u32[]{:S(2)}) collective-permute-start(bf16[256,256]{1,0:T(8,128)(2,1)S(1)} %get-tuple-element.31.c_ref), channel_id=1, source_target_pairs={{8,16},{16,8},{9,17},{17,9},{10,18},{18,10},{11,19},{19,11},{12,20... | collective-permute-start | bytes 393224 | tf_op jit(solution)/shard_map/ppermute | solution.py:373
  3.1 0.7 %shard_map.69 = bf16[8,8,1536]{2,1,0:T(8,128)(2,1)} custom-call(bf16[12,8192]{1,0:T(8,128)(2,1)S(1)} %bitcast.12), custom_call_target="tpu_custom_call" | custom-call | tf_op jit(solution)/shard_map/pallas_call | solution.py:20
  3.8 6.9 %all-to-all-start = ((bf16[8,8,1536]{2,1,0:T(8,128)(2,1)}), bf16[8,8,1536]{2,1,0:T(8,128)(2,1)S(1)}, u32[]{:S(2)}, u32[]{:S(2)}) async-start(bf16[8,8,1536]{2,1,0:T(8,128)(2,1)} %shard_map.69), calls=%async_computation | async-start | bytes 393216 | tf_op jit(solution)/shard_map/all_to_all | solution.py:381
  10.6 0.0 copy-start.3
  10.6 0.0 collective-permute-done.1.d_ref
  10.7 2.1 %collective-permute-start.2 = (bf16[16,1024]{1,0:T(8,128)(2,1)S(1)}, bf16[16,1024]{1,0:T(8,128)(2,1)S(1)}, u32[]{:S(2)}, u32[]{:S(2)}) collective-permute-start(bf16[16,1024]{1,0:T(8,128)(2,1)S(1)} %get-tuple-element.32), channel_id=1, source_target_pairs={{0,1},{2,3},{4,5},{6,7},{1,0},{3,2},{5,4},{7,6},{8,9},{10,11},{12,... | collective-permute-start | bytes 98312 | tf_op jit(solution)/shard_map/ppermute | solution.py:388
  12.8 0.7 %collective-permute-start.3 = (bf16[16,1024]{1,0:T(8,128)(2,1)S(1)}, bf16[16,1024]{1,0:T(8,128)(2,1)S(1)}, u32[]{:S(2)}, u32[]{:S(2)}) collective-permute-start(bf16[16,1024]{1,0:T(8,128)(2,1)S(1)} %get-tuple-element.33), channel_id=1, source_target_pairs={{1,2},{3,4},{5,6},{2,1},{4,3},{6,5},{9,10},{11,12},{13,14},{10,9},... | collective-permute-start | bytes 98312 | tf_op jit(solution)/shard_map/ppermute | solution.py:387
  13.4 0.8 %shard_map.70 = (bf16[256,1024]{1,0:T(8,128)(2,1)S(1)}, bf16[2,256,256]{2,1,0:T(8,128)(2,1)S(1)}, bf16[128,256]{1,0:T(8,128)(2,1)S(1)}, bf16[256,96]{1,0:T(8,128)(2,1)S(1)}) custom-call(bf16[432,32]{1,0:T(8,128)(2,1)S(1)} %bitcast.13, bf16[256,96]{1,0:T(8,128)(2,1)S(1)} %bitcast.14), custom_call_target="tpu_custom_call" | custom-call | flops 6000000000 | tf_op jit(solution)/shard_map/pallas_call | solution.py:20
  14.2 4.2 %all-to-all-done.g_ref = bf16[8,8,1536]{2,1,0:T(8,128)(2,1)S(1)} async-done(((bf16[8,8,1536]{2,1,0:T(8,128)(2,1)}), bf16[8,8,1536]{2,1,0:T(8,128)(2,1)S(1)}, u32[]{:S(2)}, u32[]{:S(2)}) %all-to-all-start) | async-done | bytes 196640 | tf_op jit(solution)/shard_map/all_to_all | solution.py:381
  18.4 1.4 %shard_map.71 = (bf16[4,16,64,128]{3,2,1,0:T(8,128)(2,1)S(1)}, f32[256,1024]{1,0:T(8,128)S(1)}, f32[256,1024]{1,0:T(8,128)S(1)}, bf16[96,1024]{1,0:T(8,128)(2,1)S(1)}) custom-call(bf16[256,256]{1,0:T(8,128)(2,1)S(1)} %collective-permute-done.a_ref, bf16[256,256]{1,0:T(8,128)(2,1)S(1)} %get-tuple-element.30.b_ref, ...), custom_call_target="tpu_custom_call" | custom-call | flops 6000000000 | tf_op jit(solution)/shard_map/pallas_call | solution.py:20
  19.9 1.6 %shard_map.72 = bf16[32,40,128]{2,1,0:T(8,128)(2,1)S(1)} custom-call(bf16[16,1024]{1,0:T(8,128)(2,1)S(1)} %collective-permute-done.2.near_ref, bf16[16,1024]{1,0:T(8,128)(2,1)S(1)} %collective-permute-done.3.far_ref, bf16[4,16,64,128]{3,2,1,0:T(8,128)(2,1)S(1)} %get-tuple-element.39.wide_ref, f32[256,1024]{1,0:T(8,128)S(1)} %get-tuple-element.40.part_ref, ...), custom_call_target="tpu_custom_call" | custom-call | tf_op jit(solution)/shard_map/pallas_call | solution.py:20
  21.5 17.9 %all_to_all.15.got_ref = bf16[32,40,128]{2,1,0:T(8,128)(2,1)S(1)} all-to-all(bf16[32,40,128]{2,1,0:T(8,128)(2,1)S(1)} %shard_map.72), channel_id=1, replica_groups=mesh['slab'=4,'brick'=8] {'slab','brick'}, dimensions={0} | all-to-all | bytes 655360 | tf_op jit(solution)/shard_map/all_to_all | solution.py:437
  39.4 0.7 %shard_map.73 = (bf16[32,16,128]{2,1,0:T(8,128)(2,1)}, bf16[8,24,128]{2,1,0:T(8,128)(2,1)S(1)}, bf16[8,24,128]{2,1,0:T(8,128)(2,1)S(1)}, bf16[8,24,128]{2,1,0:T(8,128)(2,1)S(1)}, bf16[8,24,128]{2,1,0:T(8,128)(2,1)S(1)}) custom-call(bf16[32,40,128]{2,1,0:T(8,128)(2,1)S(1)} %all_to_all.15.got_ref), custom_call_target="tpu_custom_call" | custom-call | tf_op jit(solution)/shard_map/pallas_call | solution.py:20
  40.1 2.6 %all-to-all-start.2 = ((bf16[32,16,128]{2,1,0:T(8,128)(2,1)}), bf16[32,16,128]{2,1,0:T(8,128)(2,1)S(1)}, u32[]{:S(2)}, u32[]{:S(2)}) async-start(bf16[32,16,128]{2,1,0:T(8,128)(2,1)} %get-tuple-element.45), calls=%async_computation.2 | async-start | bytes 262144 | tf_op jit(solution)/shard_map/all_to_all | solution.py:444
  42.7 0.2 collective-permute-start.4
  42.9 1.7 %collective-permute-start.5 = (bf16[8,24,128]{2,1,0:T(8,128)(2,1)S(1)}, bf16[8,24,128]{2,1,0:T(8,128)(2,1)S(1)}, u32[]{:S(2)}, u32[]{:S(2)}) collective-permute-start(bf16[8,24,128]{2,1,0:T(8,128)(2,1)S(1)} %get-tuple-element.48), channel_id=1, source_target_pairs={{0,16},{8,24},{16,0},{24,8},{1,17},{9,25},{17,1},{25,9},{2,18},{10... | collective-permute-start | bytes 147464 | tf_op jit(solution)/shard_map/ppermute | solution.py:447
  44.6 0.1 collective-permute-start.6
  44.7 2.8 %collective-permute-done.5.refs_2_ = bf16[8,24,128]{2,1,0:T(8,128)(2,1)S(1)} collective-permute-done((bf16[8,24,128]{2,1,0:T(8,128)(2,1)S(1)}, bf16[8,24,128]{2,1,0:T(8,128)(2,1)S(1)}, u32[]{:S(2)}, u32[]{:S(2)}) %collective-permute-start.5) | collective-permute-done | bytes 49184 | tf_op jit(solution)/shard_map/ppermute | solution.py:447
  47.5 1.2 %collective-permute-done.6.refs_3_ = bf16[8,24,128]{2,1,0:T(8,128)(2,1)S(1)} collective-permute-done((bf16[8,24,128]{2,1,0:T(8,128)(2,1)S(1)}, bf16[8,24,128]{2,1,0:T(8,128)(2,1)S(1)}, u32[]{:S(2)}, u32[]{:S(2)}) %collective-permute-start.6) | collective-permute-done | bytes 49184 | tf_op jit(solution)/shard_map/ppermute | solution.py:447
  48.7 1.7 %all-to-all-done.2.whole_ref = bf16[32,16,128]{2,1,0:T(8,128)(2,1)S(1)} async-done(((bf16[32,16,128]{2,1,0:T(8,128)(2,1)}), bf16[32,16,128]{2,1,0:T(8,128)(2,1)S(1)}, u32[]{:S(2)}, u32[]{:S(2)}) %all-to-all-start.2) | async-done | bytes 131104 | tf_op jit(solution)/shard_map/all_to_all | solution.py:444
  50.5 0.9 %shard_map.74 = (bf16[12,8192]{1,0:T(8,128)(2,1)}, f32[3,3,3,16,32]{4,3,2,1,0:T(8,128)}, f32[256,96]{1,0:T(8,128)}) custom-call(bf16[32,16,128]{2,1,0:T(8,128)(2,1)S(1)} %all-to-all-done.2.whole_ref, bf16[8,24,128]{2,1,0:T(8,128)(2,1)S(1)} %get-tuple-element.46.refs_0_, bf16[8,24,128]{2,1,0:T(8,128)(2,1)S(1)} %collective-permute-done.4.refs_1_, ...), custom_call_target="tpu_custom_call" | custom-call | tf_op jit(solution)/shard_map/pallas_call | solution.py:20
  (11 shorter events, 0.0 us)
Async XLA Ops:
  0.6 2.4 %copy-start = (bf16[12,1,8192]{2,0,1:T(8,128)(2,1)S(1)}, bf16[12,1,8192]{2,0,1:T(8,128)(2,1)}, u32[]{:S(2)}) copy-start(bf16[12,1,8192]{2,0,1:T(8,128)(2,1)} %param.7) | copy-start | bytes 589828
  0.6 1.0 %copy-start.1 = (bf16[16,2,16,256]{3,2,1,0:T(8,128)(2,1)S(1)}, bf16[16,2,16,256]{3,2,1,0:T(8,128)(2,1)}, u32[]{:S(2)}) copy-start(bf16[16,2,16,256]{3,2,1,0:T(8,128)(2,1)} %v_ref.1) | copy-start | bytes 786436
  1.9 8.8 %collective-permute-start = (bf16[256,256]{1,0:T(8,128)(2,1)S(1)}, bf16[256,256]{1,0:T(8,128)(2,1)S(1)}, u32[]{:S(2)}, u32[]{:S(2)}) collective-permute-start(bf16[256,256]{1,0:T(8,128)(2,1)S(1)} %get-tuple-element.30.b_ref), channel_id=1, source_target_pairs={{0,8},{16,24},{8,0},{24,16},{1,9},{17,25},{9,1},{25,17},{2,10},{18... | collective-permute-start | bytes 393224 | tf_op jit(solution)/shard_map/ppermute | solution.py:374
  2.4 8.3 %collective-permute-start.1 = (bf16[256,256]{1,0:T(8,128)(2,1)S(1)}, bf16[256,256]{1,0:T(8,128)(2,1)S(1)}, u32[]{:S(2)}, u32[]{:S(2)}) collective-permute-start(bf16[256,256]{1,0:T(8,128)(2,1)S(1)} %get-tuple-element.31.c_ref), channel_id=1, source_target_pairs={{8,16},{16,8},{9,17},{17,9},{10,18},{18,10},{11,19},{19,11},{12,20... | collective-permute-start | bytes 393224 | tf_op jit(solution)/shard_map/ppermute | solution.py:373
  3.8 14.7 %all-to-all-start = ((bf16[8,8,1536]{2,1,0:T(8,128)(2,1)}), bf16[8,8,1536]{2,1,0:T(8,128)(2,1)S(1)}, u32[]{:S(2)}, u32[]{:S(2)}) async-start(bf16[8,8,1536]{2,1,0:T(8,128)(2,1)} %shard_map.69), calls=%async_computation | async-start | bytes 393216 | tf_op jit(solution)/shard_map/all_to_all | solution.py:381
  10.6 2.8 %copy-start.2 = (bf16[32,16,3,3,3]{0,1,4,3,2:T(8,128)(2,1)S(1)}, bf16[32,16,3,3,3]{0,1,4,3,2:T(8,128)(2,1)}, u32[]{:S(2)}) copy-start(bf16[32,16,3,3,3]{0,1,4,3,2:T(8,128)(2,1)} %param.5) | copy-start | bytes 82948
  10.6 2.8 %copy-start.3 = (bf16[96,32,2,2,2]{0,4,3,2,1:T(2,128)(2,1)S(1)}, bf16[96,32,2,2,2]{0,4,3,2,1:T(2,128)(2,1)}, u32[]{:S(2)}) copy-start(bf16[96,32,2,2,2]{0,4,3,2,1:T(2,128)(2,1)} %param.6) | copy-start | bytes 147460
  10.7 9.2 %collective-permute-start.2 = (bf16[16,1024]{1,0:T(8,128)(2,1)S(1)}, bf16[16,1024]{1,0:T(8,128)(2,1)S(1)}, u32[]{:S(2)}, u32[]{:S(2)}) collective-permute-start(bf16[16,1024]{1,0:T(8,128)(2,1)S(1)} %get-tuple-element.32), channel_id=1, source_target_pairs={{0,1},{2,3},{4,5},{6,7},{1,0},{3,2},{5,4},{7,6},{8,9},{10,11},{12,... | collective-permute-start | bytes 98312 | tf_op jit(solution)/shard_map/ppermute | solution.py:388
  12.8 7.1 %collective-permute-start.3 = (bf16[16,1024]{1,0:T(8,128)(2,1)S(1)}, bf16[16,1024]{1,0:T(8,128)(2,1)S(1)}, u32[]{:S(2)}, u32[]{:S(2)}) collective-permute-start(bf16[16,1024]{1,0:T(8,128)(2,1)S(1)} %get-tuple-element.33), channel_id=1, source_target_pairs={{1,2},{3,4},{5,6},{2,1},{4,3},{6,5},{9,10},{11,12},{13,14},{10,9},... | collective-permute-start | bytes 98312 | tf_op jit(solution)/shard_map/ppermute | solution.py:387
  40.1 10.3 %all-to-all-start.2 = ((bf16[32,16,128]{2,1,0:T(8,128)(2,1)}), bf16[32,16,128]{2,1,0:T(8,128)(2,1)S(1)}, u32[]{:S(2)}, u32[]{:S(2)}) async-start(bf16[32,16,128]{2,1,0:T(8,128)(2,1)} %get-tuple-element.45), calls=%async_computation.2 | async-start | bytes 262144 | tf_op jit(solution)/shard_map/all_to_all | solution.py:444
  42.7 2.0 %collective-permute-start.4 = (bf16[8,24,128]{2,1,0:T(8,128)(2,1)S(1)}, bf16[8,24,128]{2,1,0:T(8,128)(2,1)S(1)}, u32[]{:S(2)}, u32[]{:S(2)}) collective-permute-start(bf16[8,24,128]{2,1,0:T(8,128)(2,1)S(1)} %get-tuple-element.47), channel_id=1, source_target_pairs={{0,8},{8,0},{16,24},{24,16},{1,9},{9,1},{17,25},{25,17},{2,10},{10... | collective-permute-start | bytes 147464 | tf_op jit(solution)/shard_map/ppermute | solution.py:447
  42.9 4.6 %collective-permute-start.5 = (bf16[8,24,128]{2,1,0:T(8,128)(2,1)S(1)}, bf16[8,24,128]{2,1,0:T(8,128)(2,1)S(1)}, u32[]{:S(2)}, u32[]{:S(2)}) collective-permute-start(bf16[8,24,128]{2,1,0:T(8,128)(2,1)S(1)} %get-tuple-element.48), channel_id=1, source_target_pairs={{0,16},{8,24},{16,0},{24,8},{1,17},{9,25},{17,1},{25,9},{2,18},{10... | collective-permute-start | bytes 147464 | tf_op jit(solution)/shard_map/ppermute | solution.py:447
  44.6 4.2 %collective-permute-start.6 = (bf16[8,24,128]{2,1,0:T(8,128)(2,1)S(1)}, bf16[8,24,128]{2,1,0:T(8,128)(2,1)S(1)}, u32[]{:S(2)}, u32[]{:S(2)}) collective-permute-start(bf16[8,24,128]{2,1,0:T(8,128)(2,1)S(1)} %get-tuple-element.49), channel_id=1, source_target_pairs={{0,24},{8,16},{16,8},{24,0},{1,25},{9,17},{17,9},{25,1},{2,26},{10... | collective-permute-start | bytes 147464 | tf_op jit(solution)/shard_map/ppermute | solution.py:447

commit v7 on v6

--- a/solution.py
+++ b/solution.py
@@ -60,14 +60,14 @@
     far_ref[...] = jnp.where(even, turned[:, :cols], turned[:, cols:])
 
 
-def edge_kernel(a_ref, b_ref, c_ref, d_ref, near_ref, far_ref):
-    channels = near_ref.shape[0]
+def edge_kernel(is_far, a_ref, b_ref, c_ref, d_ref, *refs):
+    out_ref = refs[-1]
+    channels = out_ref.shape[0]
     planes = (a_ref, b_ref, c_ref, d_ref)
     first = jnp.concatenate([ref[:channels] for ref in planes], axis=1)
     last = jnp.concatenate([ref[ref.shape[0] - channels :] for ref in planes], axis=1)
     even = is_even("brick")
-    near_ref[...] = jnp.where(even, last, first)
-    far_ref[...] = jnp.where(even, first, last)
+    out_ref[...] = jnp.where(even, first, last) if is_far else jnp.where(even, last, first)
 
 
 def folding(filters):
@@ -382,7 +382,8 @@
 
     planes = (got_near, near, far, got_far)
     edge = jax.ShapeDtypeStruct((channels, 4 * cols), bf16)
-    near, far = call(edge_kernel, (edge, edge), *planes)
+    (far,) = call(functools.partial(edge_kernel, True), (edge,), *planes)
+    (near,) = call(functools.partial(edge_kernel, False), (edge,), *planes, far)
     near_pairs, far_pairs = swaps(bricks)
     got_far = lax.ppermute(far, "brick", far_pairs)
     got_near = lax.ppermute(near, "brick", near_pairs)

time: 51.7 us -> 51 us (0.986)
  starting transfers between devices: 15.3 us -> 18.1 us
  waiting for transfers between devices: 10 us -> 7.25 us
  blocking collectives: 17.9 us -> 17.1 us
    all_to_all x1, waiting for transfers between devices: 4.23 us -> 1.46 us  [per_device(): cotangent = lax.all_to_all(cotangent, 'brick', 0, 0, tiled=True)]
    ppermute x1, starting transfers between devices: 2.07 us -> 4.79 us  [per_device(): got_near = lax.ppermute(near, 'brick', near_pairs)]
    all_to_all x1, blocking collectives: 17.9 us -> 17.1 us  [per_device(): got = lax.all_to_all(send, ALL, 0, 0, tiled=True)]
    pallas_call x8 -> x9, Pallas kernels: 6.35 us -> 6.36 us  [call(): pl.pallas_call(body, out_shape=outs, in_specs=[vmem] * len(args), out_spe...]
where the time goes in v7:
time: 51 us; the launch traced here: 50.7 us
  starting transfers between devices  18.1 us (35%)
  blocking collectives  17.1 us (34%)
  waiting for transfers between devices  7.25 us (14%)
  Pallas kernels  6.36 us (12%)
  local copies, waits for them, and re-layouts  1 us (2%)
  between operations  0.77 us (2%)
    all_to_all x1, blocking collectives, per_device(): got = lax.all_to_all(send, ALL, 0, 0, tiled=True)  17.1 us
    all_to_all x1, starting transfers between devices, per_device(): cotangent = lax.all_to_all(cotangent, 'brick', 0, 0, tiled=True)  6.85 us
    pallas_call x9, Pallas kernels, call(): pl.pallas_call(body, out_shape=outs, in_specs=[vmem] * len(args), out_spe...  6.36 us
    ppermute x1, starting transfers between devices, per_device(): got_near = lax.ppermute(near, 'brick', near_pairs)  4.79 us
    ppermute x3, waiting for transfers between devices, per_device(): pieces[k] = lax.ppermute(pieces[k], 'slab', pairs)  4.06 us
    all_to_all x1, starting transfers between devices, per_device(): whole = lax.all_to_all(share, ALL, 0, 0, tiled=True)  2.58 us
    ppermute x3, starting transfers between devices, per_device(): pieces[k] = lax.ppermute(pieces[k], 'slab', pairs)  1.96 us
    all_to_all x1, waiting for transfers between devices, per_device(): whole = lax.all_to_all(share, ALL, 0, 0, tiled=True)  1.72 us
  transfers between devices with their start and end apart: 9, of which 4 were waited for; matrix products, arithmetic and copies ran while one was open for 0% of the time, Pallas kernels for 6%

profile of v7, /device:TPU:0, one launch (start us, length us, event | category | flops | bytes accessed | tf_op | source)
XLA Modules:
  0.0 50.7 jit_solution(13705253305446310614)
XLA Ops:
  0.6 1.0 %copy-done.1 = bf16[16,2,16,256]{3,2,1,0:T(8,128)(2,1)S(1)} copy-done((bf16[16,2,16,256]{3,2,1,0:T(8,128)(2,1)S(1)}, bf16[16,2,16,256]{3,2,1,0:T(8,128)(2,1)}, u32[]{:S(2)}) %copy-start.1) | copy-done | bytes 262168
  1.6 0.2 shard_map.67
  1.9 0.5 %collective-permute-start = (bf16[256,256]{1,0:T(8,128)(2,1)S(1)}, bf16[256,256]{1,0:T(8,128)(2,1)S(1)}, u32[]{:S(2)}, u32[]{:S(2)}) collective-permute-start(bf16[256,256]{1,0:T(8,128)(2,1)S(1)} %get-tuple-element.28.b_ref), channel_id=1, source_target_pairs={{0,8},{16,24},{8,0},{24,16},{1,9},{17,25},{9,1},{25,17},{2,10},{18... | collective-permute-start | bytes 393224 | tf_op jit(solution)/shard_map/ppermute | solution.py:374
  2.4 0.7 %collective-permute-start.1 = (bf16[256,256]{1,0:T(8,128)(2,1)S(1)}, bf16[256,256]{1,0:T(8,128)(2,1)S(1)}, u32[]{:S(2)}, u32[]{:S(2)}) collective-permute-start(bf16[256,256]{1,0:T(8,128)(2,1)S(1)} %get-tuple-element.29.c_ref), channel_id=1, source_target_pairs={{8,16},{16,8},{9,17},{17,9},{10,18},{18,10},{11,19},{19,11},{12,20... | collective-permute-start | bytes 393224 | tf_op jit(solution)/shard_map/ppermute | solution.py:373
  3.1 0.7 %shard_map.70 = bf16[8,8,1536]{2,1,0:T(8,128)(2,1)} custom-call(bf16[12,8192]{1,0:T(8,128)(2,1)S(1)} %bitcast.12), custom_call_target="tpu_custom_call" | custom-call | tf_op jit(solution)/shard_map/pallas_call | solution.py:20
  3.8 6.9 %all-to-all-start = ((bf16[8,8,1536]{2,1,0:T(8,128)(2,1)}), bf16[8,8,1536]{2,1,0:T(8,128)(2,1)S(1)}, u32[]{:S(2)}, u32[]{:S(2)}) async-start(bf16[8,8,1536]{2,1,0:T(8,128)(2,1)} %shard_map.70), calls=%async_computation | async-start | bytes 393216 | tf_op jit(solution)/shard_map/all_to_all | solution.py:381
  10.7 0.0 copy-start.2
  10.7 0.0 copy-start.3
  10.7 0.8 %collective-permute-start.3 = (bf16[16,1024]{1,0:T(8,128)(2,1)S(1)}, bf16[16,1024]{1,0:T(8,128)(2,1)S(1)}, u32[]{:S(2)}, u32[]{:S(2)}) collective-permute-start(bf16[16,1024]{1,0:T(8,128)(2,1)S(1)} %shard_map.68.refs_0_), channel_id=1, source_target_pairs={{1,2},{3,4},{5,6},{2,1},{4,3},{6,5},{9,10},{11,12},{13,14},{10,9},... | collective-permute-start | bytes 98312 | tf_op jit(solution)/shard_map/ppermute | solution.py:388
  11.5 4.8 %collective-permute-start.2 = (bf16[16,1024]{1,0:T(8,128)(2,1)S(1)}, bf16[16,1024]{1,0:T(8,128)(2,1)S(1)}, u32[]{:S(2)}, u32[]{:S(2)}) collective-permute-start(bf16[16,1024]{1,0:T(8,128)(2,1)S(1)} %shard_map.69), channel_id=1, source_target_pairs={{0,1},{2,3},{4,5},{6,7},{1,0},{3,2},{5,4},{7,6},{8,9},{10,11},{12,... | collective-permute-start | bytes 98312 | tf_op jit(solution)/shard_map/ppermute | solution.py:389
  16.3 0.8 %shard_map.71 = (bf16[256,1024]{1,0:T(8,128)(2,1)S(1)}, bf16[2,256,256]{2,1,0:T(8,128)(2,1)S(1)}, bf16[128,256]{1,0:T(8,128)(2,1)S(1)}, bf16[256,96]{1,0:T(8,128)(2,1)S(1)}) custom-call(bf16[432,32]{1,0:T(8,128)(2,1)S(1)} %bitcast.13, bf16[256,96]{1,0:T(8,128)(2,1)S(1)} %bitcast.14), custom_call_target="tpu_custom_call" | custom-call | flops 6000000000 | tf_op jit(solution)/shard_map/pallas_call | solution.py:20
  17.1 1.5 %all-to-all-done.g_ref = bf16[8,8,1536]{2,1,0:T(8,128)(2,1)S(1)} async-done(((bf16[8,8,1536]{2,1,0:T(8,128)(2,1)}), bf16[8,8,1536]{2,1,0:T(8,128)(2,1)S(1)}, u32[]{:S(2)}, u32[]{:S(2)}) %all-to-all-start) | async-done | bytes 196640 | tf_op jit(solution)/shard_map/all_to_all | solution.py:381
  18.5 1.4 %shard_map.72 = (bf16[4,16,64,128]{3,2,1,0:T(8,128)(2,1)S(1)}, f32[256,1024]{1,0:T(8,128)S(1)}, f32[256,1024]{1,0:T(8,128)S(1)}, bf16[96,1024]{1,0:T(8,128)(2,1)S(1)}) custom-call(bf16[256,256]{1,0:T(8,128)(2,1)S(1)} %collective-permute-done.a_ref, bf16[256,256]{1,0:T(8,128)(2,1)S(1)} %get-tuple-element.28.b_ref, ...), custom_call_target="tpu_custom_call" | custom-call | flops 6000000000 | tf_op jit(solution)/shard_map/pallas_call | solution.py:20
  20.0 1.6 %shard_map.73 = bf16[32,40,128]{2,1,0:T(8,128)(2,1)S(1)} custom-call(bf16[16,1024]{1,0:T(8,128)(2,1)S(1)} %collective-permute-done.2.near_ref, bf16[16,1024]{1,0:T(8,128)(2,1)S(1)} %collective-permute-done.3.far_ref, bf16[4,16,64,128]{3,2,1,0:T(8,128)(2,1)S(1)} %get-tuple-element.35.wide_ref, f32[256,1024]{1,0:T(8,128)S(1)} %get-tuple-element.36.part_ref, ...), custom_call_target="tpu_custom_call" | custom-call | tf_op jit(solution)/shard_map/pallas_call | solution.py:20
  21.6 17.1 %all_to_all.15.got_ref = bf16[32,40,128]{2,1,0:T(8,128)(2,1)S(1)} all-to-all(bf16[32,40,128]{2,1,0:T(8,128)(2,1)S(1)} %shard_map.73), channel_id=1, replica_groups=mesh['slab'=4,'brick'=8] {'slab','brick'}, dimensions={0} | all-to-all | bytes 655360 | tf_op jit(solution)/shard_map/all_to_all | solution.py:438
  38.7 0.7 %shard_map.74 = (bf16[32,16,128]{2,1,0:T(8,128)(2,1)}, bf16[8,24,128]{2,1,0:T(8,128)(2,1)S(1)}, bf16[8,24,128]{2,1,0:T(8,128)(2,1)S(1)}, bf16[8,24,128]{2,1,0:T(8,128)(2,1)S(1)}, bf16[8,24,128]{2,1,0:T(8,128)(2,1)S(1)}) custom-call(bf16[32,40,128]{2,1,0:T(8,128)(2,1)S(1)} %all_to_all.15.got_ref), custom_call_target="tpu_custom_call" | custom-call | tf_op jit(solution)/shard_map/pallas_call | solution.py:20
  39.4 2.6 %all-to-all-start.2 = ((bf16[32,16,128]{2,1,0:T(8,128)(2,1)}), bf16[32,16,128]{2,1,0:T(8,128)(2,1)S(1)}, u32[]{:S(2)}, u32[]{:S(2)}) async-start(bf16[32,16,128]{2,1,0:T(8,128)(2,1)} %get-tuple-element.41), calls=%async_computation.2 | async-start | bytes 262144 | tf_op jit(solution)/shard_map/all_to_all | solution.py:445
  42.0 0.2 collective-permute-start.4
  42.2 1.7 %collective-permute-start.5 = (bf16[8,24,128]{2,1,0:T(8,128)(2,1)S(1)}, bf16[8,24,128]{2,1,0:T(8,128)(2,1)S(1)}, u32[]{:S(2)}, u32[]{:S(2)}) collective-permute-start(bf16[8,24,128]{2,1,0:T(8,128)(2,1)S(1)} %get-tuple-element.44), channel_id=1, source_target_pairs={{0,16},{8,24},{16,0},{24,8},{1,17},{9,25},{17,1},{25,9},{2,18},{10... | collective-permute-start | bytes 147464 | tf_op jit(solution)/shard_map/ppermute | solution.py:448
  43.9 0.1 collective-permute-start.6
  44.0 2.8 %collective-permute-done.5.refs_2_ = bf16[8,24,128]{2,1,0:T(8,128)(2,1)S(1)} collective-permute-done((bf16[8,24,128]{2,1,0:T(8,128)(2,1)S(1)}, bf16[8,24,128]{2,1,0:T(8,128)(2,1)S(1)}, u32[]{:S(2)}, u32[]{:S(2)}) %collective-permute-start.5) | collective-permute-done | bytes 49184 | tf_op jit(solution)/shard_map/ppermute | solution.py:448
  46.8 1.2 %collective-permute-done.6.refs_3_ = bf16[8,24,128]{2,1,0:T(8,128)(2,1)S(1)} collective-permute-done((bf16[8,24,128]{2,1,0:T(8,128)(2,1)S(1)}, bf16[8,24,128]{2,1,0:T(8,128)(2,1)S(1)}, u32[]{:S(2)}, u32[]{:S(2)}) %collective-permute-start.6) | collective-permute-done | bytes 49184 | tf_op jit(solution)/shard_map/ppermute | solution.py:448
  48.0 1.7 %all-to-all-done.2.whole_ref = bf16[32,16,128]{2,1,0:T(8,128)(2,1)S(1)} async-done(((bf16[32,16,128]{2,1,0:T(8,128)(2,1)}), bf16[32,16,128]{2,1,0:T(8,128)(2,1)S(1)}, u32[]{:S(2)}, u32[]{:S(2)}) %all-to-all-start.2) | async-done | bytes 131104 | tf_op jit(solution)/shard_map/all_to_all | solution.py:445
  49.8 0.9 %shard_map.75 = (bf16[12,8192]{1,0:T(8,128)(2,1)}, f32[3,3,3,16,32]{4,3,2,1,0:T(8,128)}, f32[256,96]{1,0:T(8,128)}) custom-call(bf16[32,16,128]{2,1,0:T(8,128)(2,1)S(1)} %all-to-all-done.2.whole_ref, bf16[8,24,128]{2,1,0:T(8,128)(2,1)S(1)} %get-tuple-element.42.refs_0_, bf16[8,24,128]{2,1,0:T(8,128)(2,1)S(1)} %collective-permute-done.4.refs_1_, ...), custom_call_target="tpu_custom_call" | custom-call | tf_op jit(solution)/shard_map/pallas_call | solution.py:20
  (12 shorter events, 0.1 us)
Async XLA Ops:
  0.6 2.4 %copy-start = (bf16[12,1,8192]{2,0,1:T(8,128)(2,1)S(1)}, bf16[12,1,8192]{2,0,1:T(8,128)(2,1)}, u32[]{:S(2)}) copy-start(bf16[12,1,8192]{2,0,1:T(8,128)(2,1)} %param.7) | copy-start | bytes 589828
  0.6 1.0 %copy-start.1 = (bf16[16,2,16,256]{3,2,1,0:T(8,128)(2,1)S(1)}, bf16[16,2,16,256]{3,2,1,0:T(8,128)(2,1)}, u32[]{:S(2)}) copy-start(bf16[16,2,16,256]{3,2,1,0:T(8,128)(2,1)} %v_ref.1) | copy-start | bytes 786436
  1.9 8.8 %collective-permute-start = (bf16[256,256]{1,0:T(8,128)(2,1)S(1)}, bf16[256,256]{1,0:T(8,128)(2,1)S(1)}, u32[]{:S(2)}, u32[]{:S(2)}) collective-permute-start(bf16[256,256]{1,0:T(8,128)(2,1)S(1)} %get-tuple-element.28.b_ref), channel_id=1, source_target_pairs={{0,8},{16,24},{8,0},{24,16},{1,9},{17,25},{9,1},{25,17},{2,10},{18... | collective-permute-start | bytes 393224 | tf_op jit(solution)/shard_map/ppermute | solution.py:374
  2.4 8.2 %collective-permute-start.1 = (bf16[256,256]{1,0:T(8,128)(2,1)S(1)}, bf16[256,256]{1,0:T(8,128)(2,1)S(1)}, u32[]{:S(2)}, u32[]{:S(2)}) collective-permute-start(bf16[256,256]{1,0:T(8,128)(2,1)S(1)} %get-tuple-element.29.c_ref), channel_id=1, source_target_pairs={{8,16},{16,8},{9,17},{17,9},{10,18},{18,10},{11,19},{19,11},{12,20... | collective-permute-start | bytes 393224 | tf_op jit(solution)/shard_map/ppermute | solution.py:373
  3.8 14.8 %all-to-all-start = ((bf16[8,8,1536]{2,1,0:T(8,128)(2,1)}), bf16[8,8,1536]{2,1,0:T(8,128)(2,1)S(1)}, u32[]{:S(2)}, u32[]{:S(2)}) async-start(bf16[8,8,1536]{2,1,0:T(8,128)(2,1)} %shard_map.70), calls=%async_computation | async-start | bytes 393216 | tf_op jit(solution)/shard_map/all_to_all | solution.py:381
  10.7 5.6 %copy-start.2 = (bf16[32,16,3,3,3]{0,1,4,3,2:T(8,128)(2,1)S(1)}, bf16[32,16,3,3,3]{0,1,4,3,2:T(8,128)(2,1)}, u32[]{:S(2)}) copy-start(bf16[32,16,3,3,3]{0,1,4,3,2:T(8,128)(2,1)} %param.5) | copy-start | bytes 82948
  10.7 5.6 %copy-start.3 = (bf16[96,32,2,2,2]{0,4,3,2,1:T(2,128)(2,1)S(1)}, bf16[96,32,2,2,2]{0,4,3,2,1:T(2,128)(2,1)}, u32[]{:S(2)}) copy-start(bf16[96,32,2,2,2]{0,4,3,2,1:T(2,128)(2,1)} %param.6) | copy-start | bytes 147460
  10.7 9.3 %collective-permute-start.3 = (bf16[16,1024]{1,0:T(8,128)(2,1)S(1)}, bf16[16,1024]{1,0:T(8,128)(2,1)S(1)}, u32[]{:S(2)}, u32[]{:S(2)}) collective-permute-start(bf16[16,1024]{1,0:T(8,128)(2,1)S(1)} %shard_map.68.refs_0_), channel_id=1, source_target_pairs={{1,2},{3,4},{5,6},{2,1},{4,3},{6,5},{9,10},{11,12},{13,14},{10,9},... | collective-permute-start | bytes 98312 | tf_op jit(solution)/shard_map/ppermute | solution.py:388
  11.5 8.4 %collective-permute-start.2 = (bf16[16,1024]{1,0:T(8,128)(2,1)S(1)}, bf16[16,1024]{1,0:T(8,128)(2,1)S(1)}, u32[]{:S(2)}, u32[]{:S(2)}) collective-permute-start(bf16[16,1024]{1,0:T(8,128)(2,1)S(1)} %shard_map.69), channel_id=1, source_target_pairs={{0,1},{2,3},{4,5},{6,7},{1,0},{3,2},{5,4},{7,6},{8,9},{10,11},{12,... | collective-permute-start | bytes 98312 | tf_op jit(solution)/shard_map/ppermute | solution.py:389
  39.4 10.3 %all-to-all-start.2 = ((bf16[32,16,128]{2,1,0:T(8,128)(2,1)}), bf16[32,16,128]{2,1,0:T(8,128)(2,1)S(1)}, u32[]{:S(2)}, u32[]{:S(2)}) async-start(bf16[32,16,128]{2,1,0:T(8,128)(2,1)} %get-tuple-element.41), calls=%async_computation.2 | async-start | bytes 262144 | tf_op jit(solution)/shard_map/all_to_all | solution.py:445
  42.0 2.0 %collective-permute-start.4 = (bf16[8,24,128]{2,1,0:T(8,128)(2,1)S(1)}, bf16[8,24,128]{2,1,0:T(8,128)(2,1)S(1)}, u32[]{:S(2)}, u32[]{:S(2)}) collective-permute-start(bf16[8,24,128]{2,1,0:T(8,128)(2,1)S(1)} %get-tuple-element.43), channel_id=1, source_target_pairs={{0,8},{8,0},{16,24},{24,16},{1,9},{9,1},{17,25},{25,17},{2,10},{10... | collective-permute-start | bytes 147464 | tf_op jit(solution)/shard_map/ppermute | solution.py:448
  42.2 4.6 %collective-permute-start.5 = (bf16[8,24,128]{2,1,0:T(8,128)(2,1)S(1)}, bf16[8,24,128]{2,1,0:T(8,128)(2,1)S(1)}, u32[]{:S(2)}, u32[]{:S(2)}) collective-permute-start(bf16[8,24,128]{2,1,0:T(8,128)(2,1)S(1)} %get-tuple-element.44), channel_id=1, source_target_pairs={{0,16},{8,24},{16,0},{24,8},{1,17},{9,25},{17,1},{25,9},{2,18},{10... | collective-permute-start | bytes 147464 | tf_op jit(solution)/shard_map/ppermute | solution.py:448
  43.9 4.2 %collective-permute-start.6 = (bf16[8,24,128]{2,1,0:T(8,128)(2,1)S(1)}, bf16[8,24,128]{2,1,0:T(8,128)(2,1)S(1)}, u32[]{:S(2)}, u32[]{:S(2)}) collective-permute-start(bf16[8,24,128]{2,1,0:T(8,128)(2,1)S(1)} %get-tuple-element.45), channel_id=1, source_target_pairs={{0,24},{8,16},{16,8},{24,0},{1,25},{9,17},{17,9},{25,1},{2,26},{10... | collective-permute-start | bytes 147464 | tf_op jit(solution)/shard_map/ppermute | solution.py:448

commit v8 on v7

--- a/solution.py
+++ b/solution.py
@@ -308,15 +308,19 @@
     send_ref[25:, :16] = jnp.zeros((slots - 25, 16, 128), bf16)
 
 
-def sum_kernel(got_ref, share_ref, *piece_refs):
+def sum_kernel(got_ref, share_ref, mark_ref):
     devices = got_ref.shape[0]
-    bricks = piece_refs[0].shape[0]
     total = got_ref[0, :16].astype(f32)
     for d in range(1, devices):
         total = total + got_ref[d, :16].astype(f32)
     total = total.astype(bf16)
+    mark_ref[...] = total
     for d in range(devices):
         share_ref[d] = total
+
+
+def sort_kernel(got_ref, _, *piece_refs):
+    bricks = piece_refs[0].shape[0]
     me = lax.axis_index("slab")
     for k, piece_ref in enumerate(piece_refs):
         start = jnp.bitwise_xor(me, k) * bricks
@@ -437,11 +441,15 @@
     )
     got = lax.all_to_all(send, ALL, 0, 0, tiled=True)
     piece = jax.ShapeDtypeStruct((bricks, chunk_rows, 128), bf16)
-    share, *pieces = call(
+    share, mark = call(
         sum_kernel,
-        (jax.ShapeDtypeStruct((devices, 16, 128), bf16),) + (piece,) * slabs,
+        (
+            jax.ShapeDtypeStruct((devices, 16, 128), bf16),
+            jax.ShapeDtypeStruct((16, 128), bf16),
+        ),
         got,
     )
+    pieces = list(call(sort_kernel, (piece,) * slabs, got, mark))
     whole = lax.all_to_all(share, ALL, 0, 0, tiled=True)
     for k in range(1, slabs):
         pairs = [(i, i ^ k) for i in range(slabs)]

time: 51 us -> 51 us (level)
    pallas_call x9 -> x10, Pallas kernels: 6.36 us -> 6.39 us  [call(): pl.pallas_call(body, out_shape=outs, in_specs=[vmem] * len(args), out_spe...]
where the time goes in v8:
time: 51 us; the launch traced here: 50.7 us
  starting transfers between devices  18.1 us (35%)
  blocking collectives  17.1 us (34%)
  waiting for transfers between devices  7.21 us (14%)
  Pallas kernels  6.39 us (13%)
  local copies, waits for them, and re-layouts  1 us (2%)
  between operations  0.78 us (2%)
    all_to_all x1, blocking collectives, per_device(): got = lax.all_to_all(send, ALL, 0, 0, tiled=True)  17.1 us
    all_to_all x1, starting transfers between devices, per_device(): cotangent = lax.all_to_all(cotangent, 'brick', 0, 0, tiled=True)  6.85 us
    pallas_call x10, Pallas kernels, call(): pl.pallas_call(body, out_shape=outs, in_specs=[vmem] * len(args), out_spe...  6.39 us
    ppermute x1, starting transfers between devices, per_device(): got_near = lax.ppermute(near, 'brick', near_pairs)  4.79 us
    ppermute x3, waiting for transfers between devices, per_device(): pieces[k] = lax.ppermute(pieces[k], 'slab', pairs)  4.01 us
    all_to_all x1, starting transfers between devices, per_device(): whole = lax.all_to_all(share, ALL, 0, 0, tiled=True)  2.58 us
    ppermute x3, starting transfers between devices, per_device(): pieces[k] = lax.ppermute(pieces[k], 'slab', pairs)  1.96 us
    all_to_all x1, waiting for transfers between devices, per_device(): whole = lax.all_to_all(share, ALL, 0, 0, tiled=True)  1.73 us
  transfers between devices with their start and end apart: 9, of which 4 were waited for; matrix products, arithmetic and copies ran while one was open for 0% of the time, Pallas kernels for 6%

profile of v8, /device:TPU:0, one launch (start us, length us, event | category | flops | bytes accessed | tf_op | source)
XLA Modules:
  0.0 50.7 jit_solution(333350457434405454)
XLA Ops:
  0.6 1.0 %copy-done.1 = bf16[16,2,16,256]{3,2,1,0:T(8,128)(2,1)S(1)} copy-done((bf16[16,2,16,256]{3,2,1,0:T(8,128)(2,1)S(1)}, bf16[16,2,16,256]{3,2,1,0:T(8,128)(2,1)}, u32[]{:S(2)}) %copy-start.1) | copy-done | bytes 262168
  1.6 0.2 shard_map.67
  1.9 0.5 %collective-permute-start = (bf16[256,256]{1,0:T(8,128)(2,1)S(1)}, bf16[256,256]{1,0:T(8,128)(2,1)S(1)}, u32[]{:S(2)}, u32[]{:S(2)}) collective-permute-start(bf16[256,256]{1,0:T(8,128)(2,1)S(1)} %get-tuple-element.29.b_ref), channel_id=1, source_target_pairs={{0,8},{16,24},{8,0},{24,16},{1,9},{17,25},{9,1},{25,17},{2,10},{18... | collective-permute-start | bytes 393224 | tf_op jit(solution)/shard_map/ppermute | solution.py:378
  2.4 0.7 %collective-permute-start.1 = (bf16[256,256]{1,0:T(8,128)(2,1)S(1)}, bf16[256,256]{1,0:T(8,128)(2,1)S(1)}, u32[]{:S(2)}, u32[]{:S(2)}) collective-permute-start(bf16[256,256]{1,0:T(8,128)(2,1)S(1)} %get-tuple-element.30.c_ref), channel_id=1, source_target_pairs={{8,16},{16,8},{9,17},{17,9},{10,18},{18,10},{11,19},{19,11},{12,20... | collective-permute-start | bytes 393224 | tf_op jit(solution)/shard_map/ppermute | solution.py:377
  3.1 0.7 %shard_map.70 = bf16[8,8,1536]{2,1,0:T(8,128)(2,1)} custom-call(bf16[12,8192]{1,0:T(8,128)(2,1)S(1)} %bitcast.12), custom_call_target="tpu_custom_call" | custom-call | tf_op jit(solution)/shard_map/pallas_call | solution.py:20
  3.8 6.9 %all-to-all-start = ((bf16[8,8,1536]{2,1,0:T(8,128)(2,1)}), bf16[8,8,1536]{2,1,0:T(8,128)(2,1)S(1)}, u32[]{:S(2)}, u32[]{:S(2)}) async-start(bf16[8,8,1536]{2,1,0:T(8,128)(2,1)} %shard_map.70), calls=%async_computation | async-start | bytes 393216 | tf_op jit(solution)/shard_map/all_to_all | solution.py:385
  10.7 0.0 copy-start.2
  10.7 0.0 copy-start.3
  10.7 0.8 %collective-permute-start.3 = (bf16[16,1024]{1,0:T(8,128)(2,1)S(1)}, bf16[16,1024]{1,0:T(8,128)(2,1)S(1)}, u32[]{:S(2)}, u32[]{:S(2)}) collective-permute-start(bf16[16,1024]{1,0:T(8,128)(2,1)S(1)} %shard_map.68.refs_0_), channel_id=1, source_target_pairs={{1,2},{3,4},{5,6},{2,1},{4,3},{6,5},{9,10},{11,12},{13,14},{10,9},... | collective-permute-start | bytes 98312 | tf_op jit(solution)/shard_map/ppermute | solution.py:392
  11.5 4.8 %collective-permute-start.2 = (bf16[16,1024]{1,0:T(8,128)(2,1)S(1)}, bf16[16,1024]{1,0:T(8,128)(2,1)S(1)}, u32[]{:S(2)}, u32[]{:S(2)}) collective-permute-start(bf16[16,1024]{1,0:T(8,128)(2,1)S(1)} %shard_map.69), channel_id=1, source_target_pairs={{0,1},{2,3},{4,5},{6,7},{1,0},{3,2},{5,4},{7,6},{8,9},{10,11},{12,... | collective-permute-start | bytes 98312 | tf_op jit(solution)/shard_map/ppermute | solution.py:393
  16.3 0.8 %shard_map.71 = (bf16[256,1024]{1,0:T(8,128)(2,1)S(1)}, bf16[2,256,256]{2,1,0:T(8,128)(2,1)S(1)}, bf16[128,256]{1,0:T(8,128)(2,1)S(1)}, bf16[256,96]{1,0:T(8,128)(2,1)S(1)}) custom-call(bf16[432,32]{1,0:T(8,128)(2,1)S(1)} %bitcast.13, bf16[256,96]{1,0:T(8,128)(2,1)S(1)} %bitcast.14), custom_call_target="tpu_custom_call" | custom-call | flops 6000000000 | tf_op jit(solution)/shard_map/pallas_call | solution.py:20
  17.1 1.5 %all-to-all-done.g_ref = bf16[8,8,1536]{2,1,0:T(8,128)(2,1)S(1)} async-done(((bf16[8,8,1536]{2,1,0:T(8,128)(2,1)}), bf16[8,8,1536]{2,1,0:T(8,128)(2,1)S(1)}, u32[]{:S(2)}, u32[]{:S(2)}) %all-to-all-start) | async-done | bytes 196640 | tf_op jit(solution)/shard_map/all_to_all | solution.py:385
  18.5 1.4 %shard_map.72 = (bf16[4,16,64,128]{3,2,1,0:T(8,128)(2,1)S(1)}, f32[256,1024]{1,0:T(8,128)S(1)}, f32[256,1024]{1,0:T(8,128)S(1)}, bf16[96,1024]{1,0:T(8,128)(2,1)S(1)}) custom-call(bf16[256,256]{1,0:T(8,128)(2,1)S(1)} %collective-permute-done.a_ref, bf16[256,256]{1,0:T(8,128)(2,1)S(1)} %get-tuple-element.29.b_ref, ...), custom_call_target="tpu_custom_call" | custom-call | flops 6000000000 | tf_op jit(solution)/shard_map/pallas_call | solution.py:20
  20.0 1.6 %shard_map.73 = bf16[32,40,128]{2,1,0:T(8,128)(2,1)S(1)} custom-call(bf16[16,1024]{1,0:T(8,128)(2,1)S(1)} %collective-permute-done.2.near_ref, bf16[16,1024]{1,0:T(8,128)(2,1)S(1)} %collective-permute-done.3.far_ref, bf16[4,16,64,128]{3,2,1,0:T(8,128)(2,1)S(1)} %get-tuple-element.36.wide_ref, f32[256,1024]{1,0:T(8,128)S(1)} %get-tuple-element.37.part_ref, ...), custom_call_target="tpu_custom_call" | custom-call | tf_op jit(solution)/shard_map/pallas_call | solution.py:20
  21.6 17.1 %all_to_all.15.got_ref = bf16[32,40,128]{2,1,0:T(8,128)(2,1)S(1)} all-to-all(bf16[32,40,128]{2,1,0:T(8,128)(2,1)S(1)} %shard_map.73), channel_id=1, replica_groups=mesh['slab'=4,'brick'=8] {'slab','brick'}, dimensions={0} | all-to-all | bytes 655360 | tf_op jit(solution)/shard_map/all_to_all | solution.py:442
  38.7 0.7 %shard_map.74 = (bf16[32,16,128]{2,1,0:T(8,128)(2,1)}, bf16[16,128]{1,0:T(8,128)(2,1)S(1)}) custom-call(bf16[32,40,128]{2,1,0:T(8,128)(2,1)S(1)} %all_to_all.15.got_ref), custom_call_target="tpu_custom_call" | custom-call | tf_op jit(solution)/shard_map/pallas_call | solution.py:20
  39.4 2.6 %all-to-all-start.2 = ((bf16[32,16,128]{2,1,0:T(8,128)(2,1)}), bf16[32,16,128]{2,1,0:T(8,128)(2,1)S(1)}, u32[]{:S(2)}, u32[]{:S(2)}) async-start(bf16[32,16,128]{2,1,0:T(8,128)(2,1)} %get-tuple-element.42), calls=%async_computation.2 | async-start | bytes 262144 | tf_op jit(solution)/shard_map/all_to_all | solution.py:453
  42.1 0.2 collective-permute-start.4
  42.2 1.7 %collective-permute-start.5 = (bf16[8,24,128]{2,1,0:T(8,128)(2,1)S(1)}, bf16[8,24,128]{2,1,0:T(8,128)(2,1)S(1)}, u32[]{:S(2)}, u32[]{:S(2)}) collective-permute-start(bf16[8,24,128]{2,1,0:T(8,128)(2,1)S(1)} %get-tuple-element.46), channel_id=1, source_target_pairs={{0,16},{8,24},{16,0},{24,8},{1,17},{9,25},{17,1},{25,9},{2,18},{10... | collective-permute-start | bytes 147464 | tf_op jit(solution)/shard_map/ppermute | solution.py:456
  43.9 0.1 collective-permute-start.6
  44.0 2.8 %collective-permute-done.5.refs_2_ = bf16[8,24,128]{2,1,0:T(8,128)(2,1)S(1)} collective-permute-done((bf16[8,24,128]{2,1,0:T(8,128)(2,1)S(1)}, bf16[8,24,128]{2,1,0:T(8,128)(2,1)S(1)}, u32[]{:S(2)}, u32[]{:S(2)}) %collective-permute-start.5) | collective-permute-done | bytes 49184 | tf_op jit(solution)/shard_map/ppermute | solution.py:456
  46.8 1.2 %collective-permute-done.6.refs_3_ = bf16[8,24,128]{2,1,0:T(8,128)(2,1)S(1)} collective-permute-done((bf16[8,24,128]{2,1,0:T(8,128)(2,1)S(1)}, bf16[8,24,128]{2,1,0:T(8,128)(2,1)S(1)}, u32[]{:S(2)}, u32[]{:S(2)}) %collective-permute-start.6) | collective-permute-done | bytes 49184 | tf_op jit(solution)/shard_map/ppermute | solution.py:456
  48.0 1.7 %all-to-all-done.2.whole_ref = bf16[32,16,128]{2,1,0:T(8,128)(2,1)S(1)} async-done(((bf16[32,16,128]{2,1,0:T(8,128)(2,1)}), bf16[32,16,128]{2,1,0:T(8,128)(2,1)S(1)}, u32[]{:S(2)}, u32[]{:S(2)}) %all-to-all-start.2) | async-done | bytes 131104 | tf_op jit(solution)/shard_map/all_to_all | solution.py:453
  49.8 0.9 %shard_map.76 = (bf16[12,8192]{1,0:T(8,128)(2,1)}, f32[3,3,3,16,32]{4,3,2,1,0:T(8,128)}, f32[256,96]{1,0:T(8,128)}) custom-call(bf16[32,16,128]{2,1,0:T(8,128)(2,1)S(1)} %all-to-all-done.2.whole_ref, bf16[8,24,128]{2,1,0:T(8,128)(2,1)S(1)} %get-tuple-element.44.refs_0_, bf16[8,24,128]{2,1,0:T(8,128)(2,1)S(1)} %collective-permute-done.4.refs_1_, ...), custom_call_target="tpu_custom_call" | custom-call | tf_op jit(solution)/shard_map/pallas_call | solution.py:20
  (13 shorter events, 0.1 us)
Async XLA Ops:
  0.6 2.4 %copy-start = (bf16[12,1,8192]{2,0,1:T(8,128)(2,1)S(1)}, bf16[12,1,8192]{2,0,1:T(8,128)(2,1)}, u32[]{:S(2)}) copy-start(bf16[12,1,8192]{2,0,1:T(8,128)(2,1)} %param.7) | copy-start | bytes 589828
  0.6 1.0 %copy-start.1 = (bf16[16,2,16,256]{3,2,1,0:T(8,128)(2,1)S(1)}, bf16[16,2,16,256]{3,2,1,0:T(8,128)(2,1)}, u32[]{:S(2)}) copy-start(bf16[16,2,16,256]{3,2,1,0:T(8,128)(2,1)} %v_ref.1) | copy-start | bytes 786436
  1.9 8.8 %collective-permute-start = (bf16[256,256]{1,0:T(8,128)(2,1)S(1)}, bf16[256,256]{1,0:T(8,128)(2,1)S(1)}, u32[]{:S(2)}, u32[]{:S(2)}) collective-permute-start(bf16[256,256]{1,0:T(8,128)(2,1)S(1)} %get-tuple-element.29.b_ref), channel_id=1, source_target_pairs={{0,8},{16,24},{8,0},{24,16},{1,9},{17,25},{9,1},{25,17},{2,10},{18... | collective-permute-start | bytes 393224 | tf_op jit(solution)/shard_map/ppermute | solution.py:378
  2.4 8.2 %collective-permute-start.1 = (bf16[256,256]{1,0:T(8,128)(2,1)S(1)}, bf16[256,256]{1,0:T(8,128)(2,1)S(1)}, u32[]{:S(2)}, u32[]{:S(2)}) collective-permute-start(bf16[256,256]{1,0:T(8,128)(2,1)S(1)} %get-tuple-element.30.c_ref), channel_id=1, source_target_pairs={{8,16},{16,8},{9,17},{17,9},{10,18},{18,10},{11,19},{19,11},{12,20... | collective-permute-start | bytes 393224 | tf_op jit(solution)/shard_map/ppermute | solution.py:377
  3.8 14.8 %all-to-all-start = ((bf16[8,8,1536]{2,1,0:T(8,128)(2,1)}), bf16[8,8,1536]{2,1,0:T(8,128)(2,1)S(1)}, u32[]{:S(2)}, u32[]{:S(2)}) async-start(bf16[8,8,1536]{2,1,0:T(8,128)(2,1)} %shard_map.70), calls=%async_computation | async-start | bytes 393216 | tf_op jit(solution)/shard_map/all_to_all | solution.py:385
  10.7 5.6 %copy-start.2 = (bf16[32,16,3,3,3]{0,1,4,3,2:T(8,128)(2,1)S(1)}, bf16[32,16,3,3,3]{0,1,4,3,2:T(8,128)(2,1)}, u32[]{:S(2)}) copy-start(bf16[32,16,3,3,3]{0,1,4,3,2:T(8,128)(2,1)} %param.5) | copy-start | bytes 82948
  10.7 5.6 %copy-start.3 = (bf16[96,32,2,2,2]{0,4,3,2,1:T(2,128)(2,1)S(1)}, bf16[96,32,2,2,2]{0,4,3,2,1:T(2,128)(2,1)}, u32[]{:S(2)}) copy-start(bf16[96,32,2,2,2]{0,4,3,2,1:T(2,128)(2,1)} %param.6) | copy-start | bytes 147460
  10.7 9.3 %collective-permute-start.3 = (bf16[16,1024]{1,0:T(8,128)(2,1)S(1)}, bf16[16,1024]{1,0:T(8,128)(2,1)S(1)}, u32[]{:S(2)}, u32[]{:S(2)}) collective-permute-start(bf16[16,1024]{1,0:T(8,128)(2,1)S(1)} %shard_map.68.refs_0_), channel_id=1, source_target_pairs={{1,2},{3,4},{5,6},{2,1},{4,3},{6,5},{9,10},{11,12},{13,14},{10,9},... | collective-permute-start | bytes 98312 | tf_op jit(solution)/shard_map/ppermute | solution.py:392
  11.5 8.4 %collective-permute-start.2 = (bf16[16,1024]{1,0:T(8,128)(2,1)S(1)}, bf16[16,1024]{1,0:T(8,128)(2,1)S(1)}, u32[]{:S(2)}, u32[]{:S(2)}) collective-permute-start(bf16[16,1024]{1,0:T(8,128)(2,1)S(1)} %shard_map.69), channel_id=1, source_target_pairs={{0,1},{2,3},{4,5},{6,7},{1,0},{3,2},{5,4},{7,6},{8,9},{10,11},{12,... | collective-permute-start | bytes 98312 | tf_op jit(solution)/shard_map/ppermute | solution.py:393
  39.4 10.3 %all-to-all-start.2 = ((bf16[32,16,128]{2,1,0:T(8,128)(2,1)}), bf16[32,16,128]{2,1,0:T(8,128)(2,1)S(1)}, u32[]{:S(2)}, u32[]{:S(2)}) async-start(bf16[32,16,128]{2,1,0:T(8,128)(2,1)} %get-tuple-element.42), calls=%async_computation.2 | async-start | bytes 262144 | tf_op jit(solution)/shard_map/all_to_all | solution.py:453
  42.1 2.0 %collective-permute-start.4 = (bf16[8,24,128]{2,1,0:T(8,128)(2,1)S(1)}, bf16[8,24,128]{2,1,0:T(8,128)(2,1)S(1)}, u32[]{:S(2)}, u32[]{:S(2)}) collective-permute-start(bf16[8,24,128]{2,1,0:T(8,128)(2,1)S(1)} %get-tuple-element.45), channel_id=1, source_target_pairs={{0,8},{8,0},{16,24},{24,16},{1,9},{9,1},{17,25},{25,17},{2,10},{10... | collective-permute-start | bytes 147464 | tf_op jit(solution)/shard_map/ppermute | solution.py:456
  42.2 4.6 %collective-permute-start.5 = (bf16[8,24,128]{2,1,0:T(8,128)(2,1)S(1)}, bf16[8,24,128]{2,1,0:T(8,128)(2,1)S(1)}, u32[]{:S(2)}, u32[]{:S(2)}) collective-permute-start(bf16[8,24,128]{2,1,0:T(8,128)(2,1)S(1)} %get-tuple-element.46), channel_id=1, source_target_pairs={{0,16},{8,24},{16,0},{24,8},{1,17},{9,25},{17,1},{25,9},{2,18},{10... | collective-permute-start | bytes 147464 | tf_op jit(solution)/shard_map/ppermute | solution.py:456
  43.9 4.1 %collective-permute-start.6 = (bf16[8,24,128]{2,1,0:T(8,128)(2,1)S(1)}, bf16[8,24,128]{2,1,0:T(8,128)(2,1)S(1)}, u32[]{:S(2)}, u32[]{:S(2)}) collective-permute-start(bf16[8,24,128]{2,1,0:T(8,128)(2,1)S(1)} %get-tuple-element.47), channel_id=1, source_target_pairs={{0,24},{8,16},{16,8},{24,0},{1,25},{9,17},{17,9},{25,1},{2,26},{10... | collective-permute-start | bytes 147464 | tf_op jit(solution)/shard_map/ppermute | solution.py:456

commit v9 on v7

--- a/solution.py
+++ b/solution.py
@@ -282,8 +282,7 @@
         (8 * mid, 8 * mid),
         lambda s: (s % 2) * (4 * mid) + ((s // 2) % 4) * mid + s // 8,
     )
-    ordered = dot(natural, hidden).astype(bf16)
-    grad_two = dot_nt(ordered, grad_ref[...])
+    grad_two = dot(natural, dot_nt(hidden, grad_ref[...]).astype(bf16))
     moments = dot_nt(x_ref[...], delta).reshape(4, 4, 4, channels, 8 * mid)
     by_r = moments[:, :, 0:3, :, : 4 * mid] + moments[:, :, 1:4, :, 4 * mid :]
     for i in range(4):

time: 51 us -> 51.3 us (level)
  no operation moved by 1% of the time
where the time goes in v9:
time: 51.3 us; the launch traced here: 51 us
  starting transfers between devices  18.1 us (35%)
  blocking collectives  17.1 us (33%)
  waiting for transfers between devices  7.25 us (14%)
  Pallas kernels  6.66 us (13%)
  local copies, waits for them, and re-layouts  1 us (2%)
  between operations  0.77 us (2%)
    all_to_all x1, blocking collectives, per_device(): got = lax.all_to_all(send, ALL, 0, 0, tiled=True)  17.1 us
    all_to_all x1, starting transfers between devices, per_device(): cotangent = lax.all_to_all(cotangent, 'brick', 0, 0, tiled=True)  6.85 us
    pallas_call x9, Pallas kernels, call(): pl.pallas_call(body, out_shape=outs, in_specs=[vmem] * len(args), out_spe...  6.66 us
    ppermute x1, starting transfers between devices, per_device(): got_near = lax.ppermute(near, 'brick', near_pairs)  4.79 us
    ppermute x3, waiting for transfers between devices, per_device(): pieces[k] = lax.ppermute(pieces[k], 'slab', pairs)  4.06 us
    all_to_all x1, starting transfers between devices, per_device(): whole = lax.all_to_all(share, ALL, 0, 0, tiled=True)  2.58 us
    ppermute x3, starting transfers between devices, per_device(): pieces[k] = lax.ppermute(pieces[k], 'slab', pairs)  1.96 us
    all_to_all x1, waiting for transfers between devices, per_device(): whole = lax.all_to_all(share, ALL, 0, 0, tiled=True)  1.72 us
  transfers between devices with their start and end apart: 9, of which 4 were waited for; matrix products, arithmetic and copies ran while one was open for 0% of the time, Pallas kernels for 6%

profile of v9, /device:TPU:0, one launch (start us, length us, event | category | flops | bytes accessed | tf_op | source)
XLA Modules:
  0.0 51.0 jit_solution(9556867836432534039)
XLA Ops:
  0.6 1.0 %copy-done.1 = bf16[16,2,16,256]{3,2,1,0:T(8,128)(2,1)S(1)} copy-done((bf16[16,2,16,256]{3,2,1,0:T(8,128)(2,1)S(1)}, bf16[16,2,16,256]{3,2,1,0:T(8,128)(2,1)}, u32[]{:S(2)}) %copy-start.1) | copy-done | bytes 262168
  1.6 0.2 shard_map.67
  1.9 0.5 %collective-permute-start = (bf16[256,256]{1,0:T(8,128)(2,1)S(1)}, bf16[256,256]{1,0:T(8,128)(2,1)S(1)}, u32[]{:S(2)}, u32[]{:S(2)}) collective-permute-start(bf16[256,256]{1,0:T(8,128)(2,1)S(1)} %get-tuple-element.28.b_ref), channel_id=1, source_target_pairs={{0,8},{16,24},{8,0},{24,16},{1,9},{17,25},{9,1},{25,17},{2,10},{18... | collective-permute-start | bytes 393224 | tf_op jit(solution)/shard_map/ppermute | solution.py:373
  2.4 0.7 %collective-permute-start.1 = (bf16[256,256]{1,0:T(8,128)(2,1)S(1)}, bf16[256,256]{1,0:T(8,128)(2,1)S(1)}, u32[]{:S(2)}, u32[]{:S(2)}) collective-permute-start(bf16[256,256]{1,0:T(8,128)(2,1)S(1)} %get-tuple-element.29.c_ref), channel_id=1, source_target_pairs={{8,16},{16,8},{9,17},{17,9},{10,18},{18,10},{11,19},{19,11},{12,20... | collective-permute-start | bytes 393224 | tf_op jit(solution)/shard_map/ppermute | solution.py:372
  3.1 0.7 %shard_map.70 = bf16[8,8,1536]{2,1,0:T(8,128)(2,1)} custom-call(bf16[12,8192]{1,0:T(8,128)(2,1)S(1)} %bitcast.12), custom_call_target="tpu_custom_call" | custom-call | tf_op jit(solution)/shard_map/pallas_call | solution.py:20
  3.8 6.9 %all-to-all-start = ((bf16[8,8,1536]{2,1,0:T(8,128)(2,1)}), bf16[8,8,1536]{2,1,0:T(8,128)(2,1)S(1)}, u32[]{:S(2)}, u32[]{:S(2)}) async-start(bf16[8,8,1536]{2,1,0:T(8,128)(2,1)} %shard_map.70), calls=%async_computation | async-start | bytes 393216 | tf_op jit(solution)/shard_map/all_to_all | solution.py:380
  10.7 0.0 copy-start.2
  10.7 0.0 copy-start.3
  10.7 0.8 %collective-permute-start.3 = (bf16[16,1024]{1,0:T(8,128)(2,1)S(1)}, bf16[16,1024]{1,0:T(8,128)(2,1)S(1)}, u32[]{:S(2)}, u32[]{:S(2)}) collective-permute-start(bf16[16,1024]{1,0:T(8,128)(2,1)S(1)} %shard_map.68.refs_0_), channel_id=1, source_target_pairs={{1,2},{3,4},{5,6},{2,1},{4,3},{6,5},{9,10},{11,12},{13,14},{10,9},... | collective-permute-start | bytes 98312 | tf_op jit(solution)/shard_map/ppermute | solution.py:387
  11.5 4.8 %collective-permute-start.2 = (bf16[16,1024]{1,0:T(8,128)(2,1)S(1)}, bf16[16,1024]{1,0:T(8,128)(2,1)S(1)}, u32[]{:S(2)}, u32[]{:S(2)}) collective-permute-start(bf16[16,1024]{1,0:T(8,128)(2,1)S(1)} %shard_map.69), channel_id=1, source_target_pairs={{0,1},{2,3},{4,5},{6,7},{1,0},{3,2},{5,4},{7,6},{8,9},{10,11},{12,... | collective-permute-start | bytes 98312 | tf_op jit(solution)/shard_map/ppermute | solution.py:388
  16.3 0.8 %shard_map.71 = (bf16[256,1024]{1,0:T(8,128)(2,1)S(1)}, bf16[2,256,256]{2,1,0:T(8,128)(2,1)S(1)}, bf16[128,256]{1,0:T(8,128)(2,1)S(1)}, bf16[256,96]{1,0:T(8,128)(2,1)S(1)}) custom-call(bf16[432,32]{1,0:T(8,128)(2,1)S(1)} %bitcast.13, bf16[256,96]{1,0:T(8,128)(2,1)S(1)} %bitcast.14), custom_call_target="tpu_custom_call" | custom-call | flops 6000000000 | tf_op jit(solution)/shard_map/pallas_call | solution.py:20
  17.1 1.5 %all-to-all-done.g_ref = bf16[8,8,1536]{2,1,0:T(8,128)(2,1)S(1)} async-done(((bf16[8,8,1536]{2,1,0:T(8,128)(2,1)}), bf16[8,8,1536]{2,1,0:T(8,128)(2,1)S(1)}, u32[]{:S(2)}, u32[]{:S(2)}) %all-to-all-start) | async-done | bytes 196640 | tf_op jit(solution)/shard_map/all_to_all | solution.py:380
  18.5 1.4 %shard_map.72 = (bf16[4,16,64,128]{3,2,1,0:T(8,128)(2,1)S(1)}, f32[256,1024]{1,0:T(8,128)S(1)}, f32[256,1024]{1,0:T(8,128)S(1)}, bf16[96,1024]{1,0:T(8,128)(2,1)S(1)}) custom-call(bf16[256,256]{1,0:T(8,128)(2,1)S(1)} %collective-permute-done.a_ref, bf16[256,256]{1,0:T(8,128)(2,1)S(1)} %get-tuple-element.28.b_ref, ...), custom_call_target="tpu_custom_call" | custom-call | flops 6000000000 | tf_op jit(solution)/shard_map/pallas_call | solution.py:20
  20.0 1.9 %shard_map.73 = bf16[32,40,128]{2,1,0:T(8,128)(2,1)S(1)} custom-call(bf16[16,1024]{1,0:T(8,128)(2,1)S(1)} %collective-permute-done.2.near_ref, bf16[16,1024]{1,0:T(8,128)(2,1)S(1)} %collective-permute-done.3.far_ref, bf16[4,16,64,128]{3,2,1,0:T(8,128)(2,1)S(1)} %get-tuple-element.35.wide_ref, f32[256,1024]{1,0:T(8,128)S(1)} %get-tuple-element.36.part_ref, ...), custom_call_target="tpu_custom_call" | custom-call | tf_op jit(solution)/shard_map/pallas_call | solution.py:20
  21.9 17.1 %all_to_all.15.got_ref = bf16[32,40,128]{2,1,0:T(8,128)(2,1)S(1)} all-to-all(bf16[32,40,128]{2,1,0:T(8,128)(2,1)S(1)} %shard_map.73), channel_id=1, replica_groups=mesh['slab'=4,'brick'=8] {'slab','brick'}, dimensions={0} | all-to-all | bytes 655360 | tf_op jit(solution)/shard_map/all_to_all | solution.py:437
  39.0 0.7 %shard_map.74 = (bf16[32,16,128]{2,1,0:T(8,128)(2,1)}, bf16[8,24,128]{2,1,0:T(8,128)(2,1)S(1)}, bf16[8,24,128]{2,1,0:T(8,128)(2,1)S(1)}, bf16[8,24,128]{2,1,0:T(8,128)(2,1)S(1)}, bf16[8,24,128]{2,1,0:T(8,128)(2,1)S(1)}) custom-call(bf16[32,40,128]{2,1,0:T(8,128)(2,1)S(1)} %all_to_all.15.got_ref), custom_call_target="tpu_custom_call" | custom-call | tf_op jit(solution)/shard_map/pallas_call | solution.py:20
  39.7 2.6 %all-to-all-start.2 = ((bf16[32,16,128]{2,1,0:T(8,128)(2,1)}), bf16[32,16,128]{2,1,0:T(8,128)(2,1)S(1)}, u32[]{:S(2)}, u32[]{:S(2)}) async-start(bf16[32,16,128]{2,1,0:T(8,128)(2,1)} %get-tuple-element.41), calls=%async_computation.2 | async-start | bytes 262144 | tf_op jit(solution)/shard_map/all_to_all | solution.py:444
  42.3 0.2 collective-permute-start.4
  42.5 1.7 %collective-permute-start.5 = (bf16[8,24,128]{2,1,0:T(8,128)(2,1)S(1)}, bf16[8,24,128]{2,1,0:T(8,128)(2,1)S(1)}, u32[]{:S(2)}, u32[]{:S(2)}) collective-permute-start(bf16[8,24,128]{2,1,0:T(8,128)(2,1)S(1)} %get-tuple-element.44), channel_id=1, source_target_pairs={{0,16},{8,24},{16,0},{24,8},{1,17},{9,25},{17,1},{25,9},{2,18},{10... | collective-permute-start | bytes 147464 | tf_op jit(solution)/shard_map/ppermute | solution.py:447
  44.2 0.1 collective-permute-start.6
  44.3 2.8 %collective-permute-done.5.refs_2_ = bf16[8,24,128]{2,1,0:T(8,128)(2,1)S(1)} collective-permute-done((bf16[8,24,128]{2,1,0:T(8,128)(2,1)S(1)}, bf16[8,24,128]{2,1,0:T(8,128)(2,1)S(1)}, u32[]{:S(2)}, u32[]{:S(2)}) %collective-permute-start.5) | collective-permute-done | bytes 49184 | tf_op jit(solution)/shard_map/ppermute | solution.py:447
  47.1 1.2 %collective-permute-done.6.refs_3_ = bf16[8,24,128]{2,1,0:T(8,128)(2,1)S(1)} collective-permute-done((bf16[8,24,128]{2,1,0:T(8,128)(2,1)S(1)}, bf16[8,24,128]{2,1,0:T(8,128)(2,1)S(1)}, u32[]{:S(2)}, u32[]{:S(2)}) %collective-permute-start.6) | collective-permute-done | bytes 49184 | tf_op jit(solution)/shard_map/ppermute | solution.py:447
  48.3 1.7 %all-to-all-done.2.whole_ref = bf16[32,16,128]{2,1,0:T(8,128)(2,1)S(1)} async-done(((bf16[32,16,128]{2,1,0:T(8,128)(2,1)}), bf16[32,16,128]{2,1,0:T(8,128)(2,1)S(1)}, u32[]{:S(2)}, u32[]{:S(2)}) %all-to-all-start.2) | async-done | bytes 131104 | tf_op jit(solution)/shard_map/all_to_all | solution.py:444
  50.1 0.9 %shard_map.75 = (bf16[12,8192]{1,0:T(8,128)(2,1)}, f32[3,3,3,16,32]{4,3,2,1,0:T(8,128)}, f32[256,96]{1,0:T(8,128)}) custom-call(bf16[32,16,128]{2,1,0:T(8,128)(2,1)S(1)} %all-to-all-done.2.whole_ref, bf16[8,24,128]{2,1,0:T(8,128)(2,1)S(1)} %get-tuple-element.42.refs_0_, bf16[8,24,128]{2,1,0:T(8,128)(2,1)S(1)} %collective-permute-done.4.refs_1_, ...), custom_call_target="tpu_custom_call" | custom-call | tf_op jit(solution)/shard_map/pallas_call | solution.py:20
  (12 shorter events, 0.1 us)
Async XLA Ops:
  0.6 2.4 %copy-start = (bf16[12,1,8192]{2,0,1:T(8,128)(2,1)S(1)}, bf16[12,1,8192]{2,0,1:T(8,128)(2,1)}, u32[]{:S(2)}) copy-start(bf16[12,1,8192]{2,0,1:T(8,128)(2,1)} %param.7) | copy-start | bytes 589828
  0.6 1.0 %copy-start.1 = (bf16[16,2,16,256]{3,2,1,0:T(8,128)(2,1)S(1)}, bf16[16,2,16,256]{3,2,1,0:T(8,128)(2,1)}, u32[]{:S(2)}) copy-start(bf16[16,2,16,256]{3,2,1,0:T(8,128)(2,1)} %v_ref.1) | copy-start | bytes 786436
  1.9 8.8 %collective-permute-start = (bf16[256,256]{1,0:T(8,128)(2,1)S(1)}, bf16[256,256]{1,0:T(8,128)(2,1)S(1)}, u32[]{:S(2)}, u32[]{:S(2)}) collective-permute-start(bf16[256,256]{1,0:T(8,128)(2,1)S(1)} %get-tuple-element.28.b_ref), channel_id=1, source_target_pairs={{0,8},{16,24},{8,0},{24,16},{1,9},{17,25},{9,1},{25,17},{2,10},{18... | collective-permute-start | bytes 393224 | tf_op jit(solution)/shard_map/ppermute | solution.py:373
  2.4 8.2 %collective-permute-start.1 = (bf16[256,256]{1,0:T(8,128)(2,1)S(1)}, bf16[256,256]{1,0:T(8,128)(2,1)S(1)}, u32[]{:S(2)}, u32[]{:S(2)}) collective-permute-start(bf16[256,256]{1,0:T(8,128)(2,1)S(1)} %get-tuple-element.29.c_ref), channel_id=1, source_target_pairs={{8,16},{16,8},{9,17},{17,9},{10,18},{18,10},{11,19},{19,11},{12,20... | collective-permute-start | bytes 393224 | tf_op jit(solution)/shard_map/ppermute | solution.py:372
  3.8 14.8 %all-to-all-start = ((bf16[8,8,1536]{2,1,0:T(8,128)(2,1)}), bf16[8,8,1536]{2,1,0:T(8,128)(2,1)S(1)}, u32[]{:S(2)}, u32[]{:S(2)}) async-start(bf16[8,8,1536]{2,1,0:T(8,128)(2,1)} %shard_map.70), calls=%async_computation | async-start | bytes 393216 | tf_op jit(solution)/shard_map/all_to_all | solution.py:380
  10.7 5.6 %copy-start.2 = (bf16[32,16,3,3,3]{0,1,4,3,2:T(8,128)(2,1)S(1)}, bf16[32,16,3,3,3]{0,1,4,3,2:T(8,128)(2,1)}, u32[]{:S(2)}) copy-start(bf16[32,16,3,3,3]{0,1,4,3,2:T(8,128)(2,1)} %param.5) | copy-start | bytes 82948
  10.7 5.6 %copy-start.3 = (bf16[96,32,2,2,2]{0,4,3,2,1:T(2,128)(2,1)S(1)}, bf16[96,32,2,2,2]{0,4,3,2,1:T(2,128)(2,1)}, u32[]{:S(2)}) copy-start(bf16[96,32,2,2,2]{0,4,3,2,1:T(2,128)(2,1)} %param.6) | copy-start | bytes 147460
  10.7 9.3 %collective-permute-start.3 = (bf16[16,1024]{1,0:T(8,128)(2,1)S(1)}, bf16[16,1024]{1,0:T(8,128)(2,1)S(1)}, u32[]{:S(2)}, u32[]{:S(2)}) collective-permute-start(bf16[16,1024]{1,0:T(8,128)(2,1)S(1)} %shard_map.68.refs_0_), channel_id=1, source_target_pairs={{1,2},{3,4},{5,6},{2,1},{4,3},{6,5},{9,10},{11,12},{13,14},{10,9},... | collective-permute-start | bytes 98312 | tf_op jit(solution)/shard_map/ppermute | solution.py:387
  11.5 8.4 %collective-permute-start.2 = (bf16[16,1024]{1,0:T(8,128)(2,1)S(1)}, bf16[16,1024]{1,0:T(8,128)(2,1)S(1)}, u32[]{:S(2)}, u32[]{:S(2)}) collective-permute-start(bf16[16,1024]{1,0:T(8,128)(2,1)S(1)} %shard_map.69), channel_id=1, source_target_pairs={{0,1},{2,3},{4,5},{6,7},{1,0},{3,2},{5,4},{7,6},{8,9},{10,11},{12,... | collective-permute-start | bytes 98312 | tf_op jit(solution)/shard_map/ppermute | solution.py:388
  39.7 10.3 %all-to-all-start.2 = ((bf16[32,16,128]{2,1,0:T(8,128)(2,1)}), bf16[32,16,128]{2,1,0:T(8,128)(2,1)S(1)}, u32[]{:S(2)}, u32[]{:S(2)}) async-start(bf16[32,16,128]{2,1,0:T(8,128)(2,1)} %get-tuple-element.41), calls=%async_computation.2 | async-start | bytes 262144 | tf_op jit(solution)/shard_map/all_to_all | solution.py:444
  42.3 2.0 %collective-permute-start.4 = (bf16[8,24,128]{2,1,0:T(8,128)(2,1)S(1)}, bf16[8,24,128]{2,1,0:T(8,128)(2,1)S(1)}, u32[]{:S(2)}, u32[]{:S(2)}) collective-permute-start(bf16[8,24,128]{2,1,0:T(8,128)(2,1)S(1)} %get-tuple-element.43), channel_id=1, source_target_pairs={{0,8},{8,0},{16,24},{24,16},{1,9},{9,1},{17,25},{25,17},{2,10},{10... | collective-permute-start | bytes 147464 | tf_op jit(solution)/shard_map/ppermute | solution.py:447
  42.5 4.6 %collective-permute-start.5 = (bf16[8,24,128]{2,1,0:T(8,128)(2,1)S(1)}, bf16[8,24,128]{2,1,0:T(8,128)(2,1)S(1)}, u32[]{:S(2)}, u32[]{:S(2)}) collective-permute-start(bf16[8,24,128]{2,1,0:T(8,128)(2,1)S(1)} %get-tuple-element.44), channel_id=1, source_target_pairs={{0,16},{8,24},{16,0},{24,8},{1,17},{9,25},{17,1},{25,9},{2,18},{10... | collective-permute-start | bytes 147464 | tf_op jit(solution)/shard_map/ppermute | solution.py:447
  44.2 4.2 %collective-permute-start.6 = (bf16[8,24,128]{2,1,0:T(8,128)(2,1)S(1)}, bf16[8,24,128]{2,1,0:T(8,128)(2,1)S(1)}, u32[]{:S(2)}, u32[]{:S(2)}) collective-permute-start(bf16[8,24,128]{2,1,0:T(8,128)(2,1)S(1)} %get-tuple-element.45), channel_id=1, source_target_pairs={{0,24},{8,16},{16,8},{24,0},{1,25},{9,17},{17,9},{25,1},{2,26},{10... | collective-permute-start | bytes 147464 | tf_op jit(solution)/shard_map/ppermute | solution.py:447
